TPU v7x, 32 devices: a whole 2x2x4 slice. The times are simulated.
32 devices in a mesh: dp: 4 (over y, x), mp: 8 (over z, core).
Axes of the slice: x: 2, y: 2, z: 4, core: 2. Of those that a mesh axis runs over, the one named last changes fastest.
Arguments:
- tokens: bfloat16 [1536, 12288], P(('dp', 'mp')), may hold values from -6 to 6
- up_blocks: int32 [192, 3], replicated, may hold values from 0 to 47, as said below
- down_blocks: int32 [192, 3], replicated, may hold values from 0 to 47, as said below
- down_live: int32 [192], replicated, may hold values from 1 to 3, as said below
- up_weight: bfloat16 [192, 3, 256, 256], P('mp'), may hold values from -0.21875 to 0.21875
- low_in: bfloat16 [12288, 256], P('mp'), may hold values from -0.0546875 to 0.0546875
- low_out: bfloat16 [256, 49152], P(None, 'mp'), may hold values from -0.375 to 0.375
- down_weight: bfloat16 [192, 3, 256, 256], P('mp'), may hold values from -0.109375 to 0.109375
- cotangent: bfloat16 [1536, 12288], P(('dp', 'mp')), may hold values from -6 to 6
Outputs:
- mixed: bfloat16 [1536, 12288], P(('dp', 'mp'))
- input_grad: bfloat16 [1536, 12288], P(('dp', 'mp'))
- up_grad: float32 [192, 3, 256, 256], P('mp', None, 'dp')
- down_grad: float32 [192, 3, 256, 256], P('mp', None, 'dp')
- low_out_grad: float32 [256, 49152], P('dp', 'mp')
- low_in_grad: float32 [12288, 256], P('mp', 'dp')
Inputs may be any that keep to these rules, and one draw needn't show every extreme that they name: `up_blocks`: row i lists 3 different blocks: first i // 4, then blocks whose index differs from that one in exactly one bit. `down_blocks`: row i lists 3 different blocks: first i // 4, then blocks whose index differs from that one in exactly one bit. `down_live`: some hidden block uses all 3 slots.
All inputs are finite; a program needn't handle non-finite values.
Results may differ from a plain program's by a relative error of at most 0.0075.
Values may be sent and summed in bfloat16 or wider, within the bound.
No kernel may reach another device: no remote copies, remote signals or barrier semaphores. Data moves between devices by JAX's collectives and lax.ppermute only.
A program may use at most 256 MiB of HBM per device.

v0:
```python
import jax
import jax.numpy as jnp
from jax import lax
from jax.sharding import PartitionSpec as P


def activation(inputs):
    return jax.nn.gelu(inputs, approximate=True)


def local(
    tokens, up_blocks, down_blocks, down_live, up_weight, low_in, low_out, down_weight, cotangent
):
    local_blocks = up_weight.shape[0]
    up_slots = up_weight.shape[1]
    block_size = up_weight.shape[2]
    down_slots = down_weight.shape[1]
    device_rank = lax.axis_index("mp")
    row_local, width_size = tokens.shape
    width_blocks = width_size // block_size
    hidden_count = up_blocks.shape[0]
    col_width = low_in.shape[0]
    first_block = device_rank * local_blocks
    local_up = lax.dynamic_slice_in_dim(up_blocks, first_block, local_blocks, 0)
    local_down = lax.dynamic_slice_in_dim(down_blocks, first_block, local_blocks, 0)
    local_live = lax.dynamic_slice_in_dim(down_live, first_block, local_blocks, 0)
    keep_mask = (jnp.arange(down_slots, dtype=jnp.int32)[None, :] < local_live[:, None]).astype(
        jnp.bfloat16
    )
    up_width = local_blocks * up_slots * block_size
    down_width = local_blocks * down_slots * block_size
    whole_rows = lax.all_gather(tokens, "mp", axis=0, tiled=True)
    tok_total = whole_rows.shape[0]
    picked = jnp.take(
        whole_rows.reshape(tok_total, width_blocks, block_size), local_up.reshape(-1), axis=1
    )
    columns = lax.dynamic_slice_in_dim(whole_rows, device_rank * col_width, col_width, 1)
    picked = picked.reshape(tok_total, local_blocks, up_slots, block_size)
    low_partial = jnp.dot(columns, low_in, preferred_element_type=jnp.float32)
    low_half = lax.psum(low_partial, "mp").astype(jnp.bfloat16)
    sparse = jnp.einsum("tikb,ikbc->tic", picked, up_weight, preferred_element_type=jnp.float32)
    lifted = jnp.dot(low_half, low_out, preferred_element_type=jnp.float32).reshape(
        tok_total, local_blocks, block_size
    )
    before = sparse + lifted
    hidden = activation(before).astype(jnp.bfloat16)
    masked_down = down_weight * keep_mask[:, :, None, None]
    pieces = jnp.einsum(
        "tib,ikbc->tikc", hidden, masked_down, preferred_element_type=jnp.float32
    ).astype(jnp.bfloat16)
    arrived = lax.all_to_all(
        pieces.reshape(tok_total, 1, down_width), "mp", split_axis=0, concat_axis=1, tiled=True
    )
    arrived = arrived.reshape(row_local, hidden_count * down_slots, block_size)
    block_range = jnp.arange(width_blocks, dtype=jnp.int32)
    down_table = (down_blocks.reshape(-1)[:, None] == block_range[None, :]).astype(jnp.bfloat16)
    mixed = jnp.einsum("tsb,sj->tjb", arrived, down_table, preferred_element_type=jnp.float32)
    mixed = mixed.reshape(row_local, width_size).astype(jnp.bfloat16)
    dy_whole = lax.all_gather(cotangent, "mp", axis=0, tiled=True)
    wanted = jnp.take(
        dy_whole.reshape(tok_total, width_blocks, block_size), local_down.reshape(-1), axis=1
    )
    wanted = wanted.reshape(tok_total, local_blocks, down_slots, block_size)
    back_hidden = jnp.einsum(
        "tikc,ikbc->tib", wanted, masked_down, preferred_element_type=jnp.float32
    )
    _, pullback = jax.vjp(activation, before)
    back_half = pullback(back_hidden)[0].astype(jnp.bfloat16)
    down_grad = jnp.einsum("tib,tikc->ikbc", hidden, wanted, preferred_element_type=jnp.float32)
    down_grad = down_grad * keep_mask[:, :, None, None].astype(jnp.float32)
    up_grad = jnp.einsum("tikb,tic->ikbc", picked, back_half, preferred_element_type=jnp.float32)
    flat_back = back_half.reshape(tok_total, local_blocks * block_size)
    low_out_grad = lax.dot_general(
        low_half, flat_back, (((0,), (0,)), ((), ())), preferred_element_type=jnp.float32
    )
    low_back_part = lax.dot_general(
        flat_back, low_out, (((1,), (1,)), ((), ())), preferred_element_type=jnp.float32
    )
    back_low = lax.psum(low_back_part, "mp").astype(jnp.bfloat16)
    low_in_grad = lax.dot_general(
        columns, back_low, (((0,), (0,)), ((), ())), preferred_element_type=jnp.float32
    )
    low_side = lax.dot_general(
        back_low, low_in, (((1,), (1,)), ((), ())), preferred_element_type=jnp.float32
    ).astype(jnp.bfloat16)
    spread = jnp.einsum(
        "tic,ikbc->tikb", back_half, up_weight, preferred_element_type=jnp.float32
    ).astype(jnp.bfloat16)
    got_blocks, got_side = (
        lax.all_to_all(
            spread.reshape(tok_total, 1, up_width), "mp", split_axis=0, concat_axis=1, tiled=True
        ),
        lax.all_to_all(
            low_side.reshape(tok_total, 1, col_width), "mp", split_axis=0, concat_axis=1, tiled=True
        ),
    )
    got_blocks = got_blocks.reshape(row_local, hidden_count * up_slots, block_size)
    up_table = (up_blocks.reshape(-1)[:, None] == block_range[None, :]).astype(jnp.bfloat16)
    input_sum = jnp.einsum(
        "tsb,sj->tjb", got_blocks, up_table, preferred_element_type=jnp.float32
    ).reshape(row_local, width_size)
    input_grad = (input_sum + got_side.reshape(row_local, width_size).astype(jnp.float32)).astype(
        jnp.bfloat16
    )
    up_out, down_out, low_out_out, low_in_out = (
        lax.psum_scatter(up_grad, "dp", scatter_dimension=2, tiled=True),
        lax.psum_scatter(down_grad, "dp", scatter_dimension=2, tiled=True),
        lax.psum_scatter(low_out_grad, "dp", scatter_dimension=0, tiled=True),
        lax.psum_scatter(low_in_grad, "dp", scatter_dimension=1, tiled=True),
    )
    return (mixed, input_grad, up_out, down_out, low_out_out, low_in_out)


def solution(mesh):
    return jax.shard_map(
        local,
        mesh=mesh,
        in_specs=(
            P(("dp", "mp"), None),
            P(),
            P(),
            P(),
            P("mp", None, None, None),
            P("mp", None),
            P(None, "mp"),
            P("mp", None, None, None),
            P(("dp", "mp"), None),
        ),
        out_specs=(
            P(("dp", "mp"), None),
            P(("dp", "mp"), None),
            P("mp", None, "dp", None),
            P("mp", None, "dp", None),
            P("dp", "mp"),
            P("mp", "dp"),
        ),
        check_vma=False,
    )
```

profile of v0, /device:TPU:0, one launch (start us, length us, event | category | flops | bytes accessed | tf_op | source)
XLA Modules:
  0.0 1228.3 jit_solution(14743072241980587597)
XLA Ops:
  7.2 0.7 all-gather.5.cloned.1.call-update
  8.0 0.7 all-gather.3.cloned.1.call-update
  8.7 0.8 dynamic_slice.12
  9.5 0.8 constant_dynamic-slice_fusion
  10.4 0.8 constant_dynamic-slice_fusion.1
  11.5 91.6 %all-gather.5.cloned.1.call-done = bf16[384,12288]{1,0:T(8,128)(2,1)} async-done(((bf16[48,12288]{1,0:T(8,128)(2,1)}), bf16[384,12288]{1,0:T(8,128)(2,1)}) %all-gather.5.cloned.1.call-update) | async-done | bytes 9437200 | tf_op jit(solution)/shard_map/all_gather | solution.py:59
  103.1 12.8 %copy.86 = bf16[384,12288]{0,1:T(8,128)(2,1)} copy(bf16[384,12288]{1,0:T(8,128)(2,1)} %all-gather.5.cloned.1.call-done) | data formatting | bytes 18874368 | tf_op jit(solution)/shard_map/all_gather | solution.py:59
  115.9 12.6 %copy.87 = bf16[384,48,256]{2,0,1:T(8,128)(2,1)} copy(bf16[384,48,256]{0,2,1:T(8,128)(2,1)} %bitcast.123) | data formatting | bytes 18874368 | tf_op jit(solution)/shard_map/reshape | solution.py:61
  128.5 65.4 %all-gather.3.cloned.1.call-done = bf16[384,12288]{1,0:T(8,128)(2,1)} async-done(((bf16[48,12288]{1,0:T(8,128)(2,1)}), bf16[384,12288]{1,0:T(8,128)(2,1)}) %all-gather.3.cloned.1.call-update) | async-done | bytes 9437200 | tf_op jit(solution)/shard_map/all_gather | solution.py:32
  194.0 2.7 fusion.25
  196.7 31.3 %all-reduce.2 = bf16[384,256]{1,0:T(8,128)(2,1)S(1)} all-reduce(f32[384,256]{1,0:T(8,128)} %fusion.25), channel_id=1, replica_groups=mesh['dp'=4,'mp'=8] {'mp'}, use_global_device_ids=true, to_apply=%region_0.0 | all-reduce | flops 98304 | bytes 589824 | tf_op jit(solution)/shard_map/psum | solution.py:40
  228.0 12.7 %copy.76 = bf16[384,12288]{0,1:T(8,128)(2,1)} copy(bf16[384,12288]{1,0:T(8,128)(2,1)} %all-gather.3.cloned.1.call-done) | data formatting | bytes 18874368 | tf_op jit(solution)/shard_map/all_gather | solution.py:32
  240.7 12.7 %copy.77 = bf16[384,48,256]{2,0,1:T(8,128)(2,1)} copy(bf16[384,48,256]{0,2,1:T(8,128)(2,1)} %bitcast.124) | data formatting | bytes 18874368 | tf_op jit(solution)/shard_map/reshape | solution.py:35
  253.4 11.4 gather_fusion.1
  264.8 13.1 %broadcast_select_fusion = bf16[72,384,256]{2,1,0:T(8,128)(2,1)} fusion(bf16[72,384,256]{2,1,0:T(8,128)(2,1)} %gather_fusion.1, pred[72]{0:T(512)(128)(4,1)S(1)} %get-tuple-element.35), kind=kLoop, calls=%fused_computation.3 | loop fusion | flops 7077888 | bytes 28311624 | tf_op jit(solution)/shard_map/jit(_take)/select_n | solution.py:60
  278.0 5.4 fusion.46
  283.3 11.5 gather_fusion
  294.8 13.1 %broadcast_select_fusion.1 = bf16[72,384,256]{2,1,0:T(8,128)(2,1)} fusion(bf16[72,384,256]{2,1,0:T(8,128)(2,1)} %gather_fusion, pred[72]{0:T(512)(128)(4,1)S(1)} %get-tuple-element.36), kind=kLoop, calls=%fused_computation.4 | loop fusion | flops 7077888 | bytes 28311624 | tf_op jit(solution)/shard_map/jit(_take)/select_n | solution.py:34
  308.0 21.7 %multiply_convert_fusion = (bf16[384,24,256]{0,2,1:T(8,128)(2,1)}, f32[24,384,256,1]{1,2,3,0:T(8,128)}) fusion(f32[384,24,256]{0,2,1:T(8,128)} %bitcast.126, bf16[384,24,3,256]{3,0,2,1:T(8,128)(2,1)} %bitcast.114, bf16[24,3,256,256]{3,2,1,0:T(8,128)(2,1)} %param.15), kind=kOutput, calls=%fused_computation.22 | convolution fusion | flops 3647471616 | bytes 47185920 | tf_op jit(solution)/shard_map/tikb,ikbc->tic/dot_general | solution.py:41
  329.7 14.3 %multiply_bitcast_fusion = f32[24,3,256,256]{2,3,1,0:T(8,128)} fusion(f32[24,3]{1,0:T(8,128)S(1)} %get-tuple-element.31, bf16[384,24,3,256]{3,0,2,1:T(8,128)(2,1)} %bitcast.117, bf16[384,24,256]{0,2,1:T(8,128)(2,1)} %get-tuple-element.33), kind=kOutput, calls=%fused_computation.2 | convolution fusion | flops 3628597248 | bytes 37749024 | tf_op jit(solution)/shard_map/tib,tikc->ikbc/dot_general | solution.py:69
  344.0 18.9 %copy.97 = f32[24,3,256,256]{3,0,1,2:T(8,128)} copy(f32[24,3,256,256]{2,3,1,0:T(8,128)} %multiply_bitcast_fusion) | data formatting | bytes 37748736 | tf_op jit(solution)/shard_map/mul | solution.py:70
  363.0 17.8 %fusion.6 = bf16[384,24,256]{0,2,1:T(8,128)(2,1)S(1)} fusion(f32[384,24,256]{0,2,1:T(8,128)} %bitcast.127, f32[24,384,256,1]{1,2,3,0:T(8,128)} %get-tuple-element.34, bf16[384,24,3,256]{3,0,2,1:T(8,128)(2,1)} %bitcast.118, bf16[24,3,256,256]{3,2,1,0:T(8,128)(2,1)} %param.18, bf16[24,3]{1,0:T(8,128)(2,1)S(1)} %get-tuple-element.32), kind=kOutput, calls=%fused_computation.15 | convolution fusion | flops 3678142464 | bytes 47186064 | tf_op jit(solution)/shard_map/tikc,ikbc->tib/dot_general | solution.py:64
  380.7 2.2 copy-done.2
  382.9 2.3 fusion.44
  385.2 31.3 %all-reduce.3 = bf16[384,256]{1,0:T(8,128)(2,1)S(1)} all-reduce(f32[384,256]{1,0:T(8,128)} %fusion.44), channel_id=1, replica_groups=mesh['dp'=4,'mp'=8] {'mp'}, use_global_device_ids=true, to_apply=%region_1.3 | all-reduce | flops 98304 | bytes 589824 | tf_op jit(solution)/shard_map/psum | solution.py:79
  416.5 1.6 fusion.22
  418.1 0.5 broadcast.78
  418.7 1.5 reduce.2
  420.2 1.7 reshape.162
  421.9 3.6 all-to-all-start.2
  425.5 3.1 fusion.23
  428.6 15.0 %convolution_convert_fusion.1 = bf16[24,3,256,384]{3,2,1,0:T(8,128)(2,1)} fusion(bf16[24,3,256,256]{3,2,1,0:T(8,128)(2,1)} %param.18, bf16[384,24,256]{0,2,1:T(8,128)(2,1)} %get-tuple-element.33, bf16[24,3]{1,0:T(8,128)(2,1)S(1)} %get-tuple-element.32), kind=kOutput, calls=%fused_computation.8 | convolution fusion | flops 3635675136 | bytes 28311696 | tf_op jit(solution)/shard_map/tib,ikbc->tikc/dot_general | solution.py:48
  443.6 23.6 %reduce = bf16[384,18432]{0,1:T(8,128)(2,1)} reduce(bf16[384,1,18432]{0,2,1:T(8,128)(2,1)} %bitcast.116, bf16[]{:T(256)} %broadcast.78), dimensions={1}, to_apply=%copy.82.reduce_sub_computation | reduce | bytes 28311554 | tf_op jit(solution)/shard_map/reshape | solution.py:52
  467.1 18.3 %copy.123 = bf16[384,18432]{1,0:T(8,128)(2,1)} copy(bf16[384,18432]{0,1:T(8,128)(2,1)} %reduce) | data formatting | bytes 28311552
  485.4 16.5 %reshape.158 = bf16[8,2,442368]{2,1,0:T(2,128)(2,1)} reshape(bf16[384,18432]{1,0:T(8,128)(2,1)} %copy.123) | data formatting | bytes 28311552
  501.9 1.0 copy-done.4
  502.9 5.5 all-to-all-start
  508.5 7.0 fusion.45
  515.6 14.4 %fusion.15 = f32[24,3,256,256]{3,2,1,0:T(8,128)} fusion(bf16[384,24,3,256]{3,0,2,1:T(8,128)(2,1)} %bitcast.115, bf16[384,24,256]{0,2,1:T(8,128)(2,1)} %copy-done.2), kind=kOutput, calls=%fused_computation.28 | convolution fusion | flops 3623878656 | bytes 37748736 | tf_op jit(solution)/shard_map/tikb,tic->ikbc/dot_general | solution.py:71
  530.1 11.3 convolution_convert_fusion
  541.4 23.6 %reduce.1 = bf16[384,18432]{0,1:T(8,128)(2,1)} reduce(bf16[384,1,18432]{0,2,1:T(8,128)(2,1)} %bitcast.113, bf16[]{:T(256)} %broadcast.78), dimensions={1}, to_apply=%copy.89.reduce_sub_computation | reduce | bytes 28311554 | tf_op jit(solution)/shard_map/reshape | solution.py:91
  565.0 18.5 %copy.124 = bf16[384,18432]{1,0:T(8,128)(2,1)} copy(bf16[384,18432]{0,1:T(8,128)(2,1)} %reduce.1) | data formatting | bytes 28311552
  583.5 16.5 %reshape.160 = bf16[8,2,442368]{2,1,0:T(2,128)(2,1)} reshape(bf16[384,18432]{1,0:T(8,128)(2,1)} %copy.124) | data formatting | bytes 28311552
  600.0 215.9 %all-to-all-done = bf16[8,2,442368]{2,1,0:T(2,128)(2,1)} async-done(((bf16[8,2,442368]{2,1,0:T(2,128)(2,1)}), bf16[8,2,442368]{2,1,0:T(2,128)(2,1)}, u32[]{:S(2)}, u32[]{:S(2)}) %all-to-all-start) | async-done | bytes 14155808 | tf_op jit(solution)/shard_map/all_to_all | solution.py:51
  816.0 5.5 all-to-all-start.1
  822.1 4.4 reshape.163
  826.5 2.4 convert_bitcast_fusion
  829.0 1.4 copy.92
  830.4 2.8 copy.122
  833.1 19.8 %reshape.159 = bf16[384,1,18432]{2,1,0:T(2,128)(2,1)} reshape(bf16[8,2,442368]{2,1,0:T(2,128)(2,1)} %all-to-all-done) | data formatting | bytes 28311552
  852.9 17.2 %copy.118 = bf16[384,1,18432]{2,0,1:T(8,128)(2,1)S(1)} copy(bf16[384,1,18432]{2,1,0:T(2,128)(2,1)} %reshape.159) | data formatting | bytes 28311552
  870.1 19.2 %copy.83 = bf16[48,8,1,18432]{3,1,0,2:T(8,128)(2,1)} copy(bf16[48,8,1,18432]{3,0,1,2:T(8,128)(2,1)S(1)} %bitcast.121) | data formatting | bytes 28311552 | tf_op jit(solution)/shard_map/all_to_all | solution.py:51
  889.3 20.5 %reshape.117 = bf16[48,576,256]{2,1,0:T(8,128)(2,1)} reshape(bf16[48,8,1,18432]{3,1,0,2:T(8,128)(2,1)} %copy.83) | data formatting | bytes 28311552 | tf_op jit(solution)/shard_map/reshape | solution.py:54
  909.8 7.6 convolution_convert_fusion.3
  917.4 1.4 copy.120
  918.9 210.1 %all-to-all-done.1 = bf16[8,2,442368]{2,1,0:T(2,128)(2,1)} async-done(((bf16[8,2,442368]{2,1,0:T(2,128)(2,1)}), bf16[8,2,442368]{2,1,0:T(2,128)(2,1)}, u32[]{:S(2)}, u32[]{:S(2)}) %all-to-all-start.1) | async-done | bytes 14155808 | tf_op jit(solution)/shard_map/all_to_all | solution.py:90
  1128.9 19.8 %reshape.161 = bf16[384,1,18432]{2,1,0:T(2,128)(2,1)} reshape(bf16[8,2,442368]{2,1,0:T(2,128)(2,1)} %all-to-all-done.1) | data formatting | bytes 28311552
  1148.7 17.2 %copy.119 = bf16[384,1,18432]{2,0,1:T(8,128)(2,1)S(1)} copy(bf16[384,1,18432]{2,1,0:T(2,128)(2,1)} %reshape.161) | data formatting | bytes 28311552
  1165.9 19.0 %copy.90 = bf16[48,8,1,18432]{3,1,0,2:T(8,128)(2,1)} copy(bf16[48,8,1,18432]{3,0,1,2:T(8,128)(2,1)S(1)} %bitcast.122) | data formatting | bytes 28311552 | tf_op jit(solution)/shard_map/all_to_all | solution.py:90
  1184.9 20.8 %reshape.122 = bf16[48,576,256]{2,1,0:T(8,128)(2,1)} reshape(bf16[48,8,1,18432]{3,1,0,2:T(8,128)(2,1)} %copy.90) | data formatting | bytes 28311552 | tf_op jit(solution)/shard_map/reshape | solution.py:97
  1205.7 6.5 fusion.30
  1212.2 1.4 copy.121
  1213.6 1.4 add_convert_fusion
  1215.0 6.0 copy.98
  (41 shorter events, 1.4 us)
Async XLA Ops:
  7.2 270.8 %copy-start = (bf16[256,6144]{1,0:T(8,128)(2,1)S(1)}, bf16[256,6144]{1,0:T(8,128)(2,1)}, u32[]{:S(2)}) copy-start(bf16[256,6144]{1,0:T(8,128)(2,1)} %param.17) | copy-start | bytes 9437188
  7.2 95.9 %all-gather.5.cloned.1.call-start = ((), (), s32[]{:S(2)}) async-start(), calls=%async_computation.8 | async-start | bytes 10616832 | tf_op jit(solution)/shard_map/all_gather | solution.py:59
  7.9 186.1 %all-gather.3.cloned.1.call-start = ((), (), s32[]{:S(2)}) async-start(), calls=%async_computation.7 | async-start | bytes 10616832 | tf_op jit(solution)/shard_map/all_gather | solution.py:32
  8.7 1206.3 %reduce-scatter.7.cloned.1.call-start = ((), (), s32[]{:S(2)}) async-start(), calls=%async_computation.10 | async-start | bytes 23592960 | tf_op jit(solution)/shard_map/reduce_scatter | solution.py:107
  380.7 2.2 copy-start.2
  421.9 80.0 %all-to-all-start.2 = ((bf16[8,2,36864]{2,1,0:T(2,128)(2,1)}), bf16[8,2,36864]{2,1,0:T(2,128)(2,1)S(1)}, u32[]{:S(2)}, u32[]{:S(2)}) async-start(bf16[8,2,36864]{2,1,0:T(2,128)(2,1)} %reshape.162), calls=%async_computation.2 | async-start | bytes 2359296 | tf_op jit(solution)/shard_map/all_to_all | solution.py:93
  425.5 795.5 %reduce-scatter.11.cloned.1.call-start = ((), (), s32[]{:S(2)}) async-start(), calls=%async_computation.12 | async-start | bytes 1966080 | tf_op jit(solution)/shard_map/reduce_scatter | solution.py:109
  501.9 1.0 copy-start.4
  502.9 313.0 %all-to-all-start = ((bf16[8,2,442368]{2,1,0:T(2,128)(2,1)}), bf16[8,2,442368]{2,1,0:T(2,128)(2,1)}, u32[]{:S(2)}, u32[]{:S(2)}) async-start(bf16[8,2,442368]{2,1,0:T(2,128)(2,1)} %reshape.158), calls=%async_computation | async-start | bytes 28311552 | tf_op jit(solution)/shard_map/all_to_all | solution.py:51
  508.4 712.6 %reduce-scatter.9.cloned.1.call-start = ((), (), s32[]{:S(2)}) async-start(), calls=%async_computation.11 | async-start | bytes 7864320 | tf_op jit(solution)/shard_map/reduce_scatter | solution.py:108
  515.6 705.5 %reduce-scatter.5.cloned.1.call-start = ((), (), s32[]{:S(2)}) async-start(), calls=%async_computation.9 | async-start | bytes 23592960 | tf_op jit(solution)/shard_map/reduce_scatter | solution.py:106
  600.0 221.4 %copy-start.5 = (s32[192,3]{0,1:T(4,128)S(1)}, s32[192,3]{0,1:T(4,128)}, u32[]{:S(2)}) copy-start(s32[192,3]{0,1:T(4,128)} %param.12) | copy-start | bytes 6916
  600.0 221.6 %copy-start.6 = (s32[192,3]{0,1:T(4,128)S(1)}, s32[192,3]{0,1:T(4,128)}, u32[]{:S(2)}) copy-start(s32[192,3]{0,1:T(4,128)} %param.13) | copy-start | bytes 6916
  816.0 313.0 %all-to-all-start.1 = ((bf16[8,2,442368]{2,1,0:T(2,128)(2,1)}), bf16[8,2,442368]{2,1,0:T(2,128)(2,1)}, u32[]{:S(2)}, u32[]{:S(2)}) async-start(bf16[8,2,442368]{2,1,0:T(2,128)(2,1)} %reshape.160), calls=%async_computation.1 | async-start | bytes 28311552 | tf_op jit(solution)/shard_map/all_to_all | solution.py:90
  1205.7 7.9 copy-start.3
  1212.2 8.8 copy-start.1
Sparse Core Ops, SparseCore 0:
  9.7 93.4 all-gather.4
  104.8 89.1 all-gather.2
  363.1 169.1 reduce-scatter.6
  536.0 30.9 reduce-scatter.10
  570.6 70.1 reduce-scatter.8
  644.7 170.8 reduce-scatter.4
where the time goes:
time: 1240 us; the launch traced here: 1230 us
  waiting for transfers between devices  585 us (47%)
  local copies, waits for them, and re-layouts  342 us (28%)
  matrix products  131 us (11%)
  other arithmetic  78.9 us (6%)
  blocking collectives  62.6 us (5%)
  starting transfers between devices  14.8 us (1%)
  between operations  14.8 us (1%)
    all_to_all x1, waiting for transfers between devices, local(): lax.all_to_all(pieces.reshape(tok_total, 1, down_width), 'mp', split_axis...  216 us
    all_to_all x1, waiting for transfers between devices, local(): lax.all_to_all(spread.reshape(tok_total, 1, up_width), 'mp', split_axis=0...  210 us
    unnamed x30, local copies, waits for them, and re-layouts  165 us
    all_gather x1, waiting for transfers between devices, local(): dy_whole = lax.all_gather(cotangent, 'mp', axis=0, tiled=True)  91.6 us
    all_gather x1, waiting for transfers between devices, local(): whole_rows = lax.all_gather(tokens, 'mp', axis=0, tiled=True)  65.4 us
    psum x1, blocking collectives, local(): back_low = lax.psum(low_back_part, 'mp').astype(jnp.bfloat16)  31.3 us
    psum x1, blocking collectives, local(): low_half = lax.psum(low_partial, 'mp').astype(jnp.bfloat16)  31.3 us
  transfers between devices with their start and end apart: 9, of which 4 were waited for; matrix products, arithmetic and copies ran while one was open for 33% of the time, Pallas kernels for 0%

commit v1 on v0

v1 whole, which is shorter than its diff:
```python
import functools

import jax
import jax.numpy as jnp
from jax import lax
from jax.experimental import pallas as pl
from jax.experimental.pallas import tpu as pltpu
from jax.sharding import PartitionSpec as P

F32 = jnp.float32
BF16 = jnp.bfloat16
GELU_SCALE = 0.7978845608028654
GELU_CUBE = 0.044715
VMEM_LIMIT = 60 * 1024 * 1024


def dot_nn(a, b):
    return lax.dot_general(a, b, (((1,), (0,)), ((), ())), preferred_element_type=F32)


def dot_nt(a, b):
    return lax.dot_general(a, b, (((1,), (1,)), ((), ())), preferred_element_type=F32)


def dot_tn(a, b):
    return lax.dot_general(a, b, (((0,), (0,)), ((), ())), preferred_element_type=F32)


def column_block(index, size):
    return pl.ds(pl.multiple_of(index * size, size), size)


def copies_in(chunks, positions, held, sems):
    rows = chunks[0].shape[0]
    copies = []
    for number, chunk in enumerate(chunks):
        first = pl.multiple_of(positions[number] * rows, 16)
        copies.append(
            pltpu.make_async_copy(chunk, held.at[pl.ds(first, rows), :], sems.at[number])
        )
    return copies


def fill_zero(total, size):
    @pl.loop(0, total.shape[1] // size)
    def _(block):
        total[:, column_block(block, size)] = jnp.zeros((total.shape[0], size), total.dtype)


def write_out(total, held, outs, out_rows, sems, size):
    @pl.loop(0, total.shape[1] // size)
    def _(block):
        columns = column_block(block, size)
        held[:, columns] = total[:, columns].astype(held.dtype)

    copies = []
    for out in outs:
        for part in range(out.shape[0]):
            number = len(copies)
            first = pl.multiple_of(out_rows[number] * out.shape[1], 16)
            copies.append(
                pltpu.make_async_copy(
                    held.at[pl.ds(first, out.shape[1]), :], out.at[part], sems.at[number]
                )
            )
    for copy in copies:
        copy.start()
    for copy in copies:
        copy.wait()


def forward_kernel(chunk_count, out_count, size, up_ref, down_ref, live_ref, pos_ref, out_ref, *refs):
    chunks = refs[:chunk_count]
    low_half, up_weight, low_out, down_weight, hidden, slope = refs[chunk_count : chunk_count + 6]
    outs = refs[chunk_count + 6 : chunk_count + 6 + out_count]
    held, total, in_sems, out_sems = refs[chunk_count + 6 + out_count :]
    step = pl.program_id(0)
    up_slots = up_weight.shape[1]
    down_slots = down_weight.shape[1]

    @pl.when(step == 0)
    def _():
        copies = copies_in(chunks, pos_ref, held, in_sems)
        for copy in copies:
            copy.start()
        fill_zero(total, size)
        for copy in copies:
            copy.wait()

    before = dot_nn(low_half[...], low_out[...])
    for slot in range(up_slots):
        columns = column_block(up_ref[step * up_slots + slot], size)
        before = before + dot_nn(held[:, columns], up_weight[0, slot])
    square = before * before
    bent = jnp.tanh(GELU_SCALE * before * (1.0 + GELU_CUBE * square))
    half = 0.5 * (1.0 + bent)
    active = (before * half).astype(BF16)
    hidden[0] = active
    slope[0] = half + 0.5 * before * (1.0 - bent * bent) * (
        GELU_SCALE * (1.0 + 3.0 * GELU_CUBE * square)
    )
    for slot in range(down_slots):
        columns = column_block(down_ref[step * down_slots + slot], size)
        weight = jnp.where(slot < live_ref[step], down_weight[0, slot], jnp.zeros((), BF16))
        total[:, columns] += dot_nn(active, weight)

    @pl.when(step == pl.num_programs(0) - 1)
    def _():
        write_out(total, held, outs, out_ref, out_sems, size)


def gradient_kernel(chunk_count, first_step, size, up_ref, down_ref, live_ref, pos_ref, quarter_ref, *refs):
    x_chunks = refs[:chunk_count]
    y_chunks = refs[chunk_count : 2 * chunk_count]
    low_half, hidden, slope, down_weight, low_out = refs[2 * chunk_count : 2 * chunk_count + 5]
    back_half, back_low, up_own, up_send, up_pass, down_own, down_send, down_pass = refs[
        2 * chunk_count + 5 : 2 * chunk_count + 13
    ]
    x_held, y_held, block_grad, x_sems, y_sems = refs[2 * chunk_count + 13 :]
    here = pl.program_id(0)
    step = here + first_step
    up_slots = up_own.shape[1] - 1
    down_slots = down_own.shape[1]
    quarter_rows = up_own.shape[2]

    @pl.when(here == 0)
    def _():
        copies = copies_in(x_chunks, pos_ref, x_held, x_sems)
        copies += copies_in(y_chunks, pos_ref, y_held, y_sems)
        for copy in copies:
            copy.start()
        back_low[...] = jnp.zeros(back_low.shape, F32)
        for copy in copies:
            copy.wait()

    wanted = []
    back_hidden = None
    for slot in range(down_slots):
        columns = column_block(down_ref[step * down_slots + slot], size)
        weight = jnp.where(slot < live_ref[step], down_weight[0, slot], jnp.zeros((), BF16))
        part = dot_nt(y_held[:, columns], weight)
        back_hidden = part if back_hidden is None else back_hidden + part
    back = (back_hidden * slope[0]).astype(BF16)
    back_half[0] = back
    back_low[...] += dot_nt(back, low_out[...])

    def spread_rows(number, own, send, passed, slot, pass_first):
        own[0, slot] = block_grad[number, quarter(0), :]
        passed[0, slot] = block_grad[number, quarter(3 - pass_first), :].astype(BF16)
        send[0, 0, slot] = block_grad[number, quarter(pass_first), :].astype(BF16)
        send[1, 0, slot] = block_grad[number, quarter(3), :].astype(BF16)

    def quarter(which):
        return pl.ds(pl.multiple_of(quarter_ref[which] * quarter_rows, quarter_rows), quarter_rows)

    active = hidden[0]
    for slot in range(down_slots):
        columns = column_block(down_ref[step * down_slots + slot], size)
        keep = (slot < live_ref[step]).astype(F32)
        block_grad[slot] = dot_tn(active, y_held[:, columns]) * keep
    for slot in range(down_slots):
        spread_rows(slot, down_own, down_send, down_pass, slot, 2)
    for slot in range(up_slots):
        columns = column_block(up_ref[step * up_slots + slot], size)
        block_grad[down_slots + slot] = dot_tn(x_held[:, columns], back)
    block_grad[down_slots + up_slots] = dot_tn(low_half[...], back)
    for slot in range(up_slots + 1):
        spread_rows(down_slots + slot, up_own, up_send, up_pass, slot, 1)


def spread_kernel(out_count, size, up_ref, rank_ref, out_ref, *refs):
    back_half, up_weight, back_low, low_in = refs[:4]
    outs = refs[4 : 4 + out_count]
    held, total, out_sems = refs[4 + out_count :]
    step = pl.program_id(0)
    up_slots = up_weight.shape[1]

    @pl.when(step == 0)
    def _():
        fill_zero(total, size)
        first = rank_ref[0] * (low_in.shape[0] // size)

        @pl.loop(0, low_in.shape[0] // size)
        def _(block):
            rows = pl.ds(pl.multiple_of(block * size, size), size)
            side = dot_nt(back_low[...], low_in[rows, :])
            total[:, column_block(first + block, size)] = side

    for slot in range(up_slots):
        columns = column_block(up_ref[step * up_slots + slot], size)
        total[:, columns] += dot_nt(back_half[0], up_weight[0, slot])

    @pl.when(step == pl.num_programs(0) - 1)
    def _():
        write_out(total, held, outs, out_ref, out_sems, size)


def whole_spec(array):
    zeros = (0,) * array.ndim
    return pl.BlockSpec(array.shape, lambda i, *_: zeros)


def any_spec():
    return pl.BlockSpec(memory_space=pl.ANY)


def block_spec(array, first=0):
    rest = (0,) * (array.ndim - 1)
    return pl.BlockSpec((1,) + array.shape[1:], lambda i, *_: (i + first,) + rest)


def params():
    return pltpu.CompilerParams(
        dimension_semantics=("arbitrary",), vmem_limit_bytes=VMEM_LIMIT
    )


def shape(dims, dtype):
    return jax.ShapeDtypeStruct(dims, dtype)


def run_forward(scalars, chunks, low_half, up_weight, low_out, down_weight, out_shapes, size):
    count, tok_total, width = up_weight.shape[0], low_half.shape[0], chunks[0].shape[1]
    out_total = sum(dims[0] for dims in out_shapes)
    hidden = shape((count, tok_total, size), BF16)
    slope = shape((count, tok_total, size), F32)
    products = 2 * up_weight.shape[1] + 1
    return pl.pallas_call(
        functools.partial(forward_kernel, len(chunks), len(out_shapes), size),
        out_shape=[hidden, slope] + [shape(dims, BF16) for dims in out_shapes],
        grid_spec=pltpu.PrefetchScalarGridSpec(
            num_scalar_prefetch=len(scalars),
            grid=(count,),
            in_specs=[any_spec()] * len(chunks)
            + [
                whole_spec(low_half),
                block_spec(up_weight),
                pl.BlockSpec((low_out.shape[0], size), lambda i, *_: (0, i)),
                block_spec(down_weight),
            ],
            out_specs=[block_spec(hidden), block_spec(slope)] + [any_spec()] * len(out_shapes),
            scratch_shapes=[
                pltpu.VMEM((tok_total, width), BF16),
                pltpu.VMEM((tok_total, width), F32),
                pltpu.SemaphoreType.DMA((len(chunks),)),
                pltpu.SemaphoreType.DMA((out_total,)),
            ],
        ),
        compiler_params=params(),
        cost_estimate=pl.CostEstimate(
            flops=2 * products * count * tok_total * size * size,
            bytes_accessed=60_000_000,
            transcendentals=count * tok_total * size,
        ),
        name="forward",
    )(*scalars, *chunks, low_half, up_weight, low_out, down_weight)


def run_gradients(
    scalars, x_chunks, y_chunks, low_half, hidden, slope, down_weight, low_out, first, count, parts, size
):
    tok_total, width = low_half.shape[0], x_chunks[0].shape[1]
    down_slots = down_weight.shape[1]
    up_slots = down_slots
    rows = size // parts
    back_half = shape((count, tok_total, size), BF16)
    back_low = shape(low_half.shape, F32)
    outs = [back_half, back_low]
    specs = [block_spec(back_half), whole_spec(back_low)]
    for slots in (up_slots + 1, down_slots):
        own = shape((count, slots, rows, size), F32)
        send = shape((2, count, slots, rows, size), BF16)
        passed = shape((count, slots, rows, size), BF16)
        outs += [own, send, passed]
        specs += [
            block_spec(own),
            pl.BlockSpec((2, 1, slots, rows, size), lambda i, *_: (0, i, 0, 0, 0)),
            block_spec(passed),
        ]
    return pl.pallas_call(
        functools.partial(gradient_kernel, len(x_chunks), first, size),
        out_shape=outs,
        grid_spec=pltpu.PrefetchScalarGridSpec(
            num_scalar_prefetch=len(scalars),
            grid=(count,),
            in_specs=[any_spec()] * (len(x_chunks) + len(y_chunks))
            + [
                whole_spec(low_half),
                block_spec(hidden, first),
                block_spec(slope, first),
                block_spec(down_weight, first),
                pl.BlockSpec((low_out.shape[0], size), lambda i, *_: (0, i + first)),
            ],
            out_specs=specs,
            scratch_shapes=[
                pltpu.VMEM((tok_total, width), BF16),
                pltpu.VMEM((tok_total, width), BF16),
                pltpu.VMEM((down_slots + up_slots + 1, size, size), F32),
                pltpu.SemaphoreType.DMA((len(x_chunks),)),
                pltpu.SemaphoreType.DMA((len(y_chunks),)),
            ],
        ),
        compiler_params=params(),
        cost_estimate=pl.CostEstimate(
            flops=2 * 11 * count * tok_total * size * size,
            bytes_accessed=50_000_000,
            transcendentals=0,
        ),
        name="gradients",
    )(*scalars, *x_chunks, *y_chunks, low_half, hidden, slope, down_weight, low_out)


def run_spread(scalars, back_half, up_weight, back_low, low_in, out_shapes, width, size):
    count, tok_total = back_half.shape[:2]
    out_total = sum(dims[0] for dims in out_shapes)
    return pl.pallas_call(
        functools.partial(spread_kernel, len(out_shapes), size),
        out_shape=[shape(dims, BF16) for dims in out_shapes],
        grid_spec=pltpu.PrefetchScalarGridSpec(
            num_scalar_prefetch=len(scalars),
            grid=(count,),
            in_specs=[
                block_spec(back_half),
                block_spec(up_weight),
                whole_spec(back_low),
                whole_spec(low_in),
            ],
            out_specs=[any_spec()] * len(out_shapes),
            scratch_shapes=[
                pltpu.VMEM((tok_total, width), BF16),
                pltpu.VMEM((tok_total, width), F32),
                pltpu.SemaphoreType.DMA((out_total,)),
            ],
        ),
        compiler_params=params(),
        cost_estimate=pl.CostEstimate(
            flops=2 * 3 * count * tok_total * size * size,
            bytes_accessed=30_000_000,
            transcendentals=0,
        ),
        name="spread",
    )(*scalars, back_half, up_weight, back_low, low_in)


def local(mp_size, dp_size, tokens, up_blocks, down_blocks, down_live, up_weight, low_in, low_out, down_weight, cotangent):
    count, up_slots, size = up_weight.shape[:3]
    down_slots = down_weight.shape[1]
    rows, width = tokens.shape
    tok_total = rows * mp_size
    col_width = low_in.shape[0]
    rank = lax.axis_index("mp")
    part = lax.axis_index("dp")
    chip, core = rank // 2, rank % 2
    chips = mp_size // 2
    by_ring = rows % 16 == 0
    ring = [(i, (i + 2) % mp_size) for i in range(mp_size)]
    swap = [(i, i ^ 1) for i in range(mp_size)]

    up_index = lax.dynamic_slice_in_dim(up_blocks, rank * count, count, 0).reshape(-1)
    down_index = lax.dynamic_slice_in_dim(down_blocks, rank * count, count, 0).reshape(-1)
    live = lax.dynamic_slice_in_dim(down_live, rank * count, count, 0)
    quarters = part ^ jnp.arange(dp_size, dtype=jnp.int32)

    chip_order = (chip - jnp.arange(chips, dtype=jnp.int32)) % chips
    if by_ring:
        positions = jnp.concatenate([chip_order * 2 + core, chip_order * 2 + (1 - core)])
        out_shapes = [(chips, rows, width), (chips, rows, width)]
    else:
        positions = jnp.zeros((1,), jnp.int32)
        out_shapes = [(1, tok_total, width)]

    def gather(block):
        if not by_ring:
            return [lax.all_gather(block, "mp", axis=0, tiled=True)]
        same = [block]
        for _ in range(chips - 1):
            same.append(lax.ppermute(same[-1], "mp", ring))
        return same + [lax.ppermute(piece, "mp", swap) for piece in same]

    def scatter_sum(parts):
        if not by_ring:
            whole = parts[0].reshape(mp_size, rows, width)
            return lax.psum_scatter(whole, "mp", scatter_dimension=0).reshape(rows, width)
        keep, give = parts
        got = lax.ppermute(give, "mp", swap)

        def mine(place):
            return keep[place].astype(F32) + got[place].astype(F32)

        moving = mine(1 % chips).astype(BF16)
        for place in range(2, chips + 1):
            moving = lax.ppermute(moving, "mp", ring)
            moving = (mine(place % chips) + moving.astype(F32)).astype(BF16)
        return moving

    def sum_all(partial):
        low = lax.psum_scatter(partial, "mp", scatter_dimension=0, tiled=True)
        return lax.all_gather(low.astype(BF16), "mp", axis=0, tiled=True)

    x_chunks = gather(tokens)
    y_chunks = gather(cotangent)

    columns = jnp.concatenate(
        [lax.dynamic_slice_in_dim(piece, rank * col_width, col_width, 1) for piece in x_chunks], 0
    )
    if by_ring:
        back_order = jnp.argsort(positions)
        columns = jnp.take(
            columns.reshape(mp_size, rows, col_width), back_order, axis=0, mode="clip"
        ).reshape(tok_total, col_width)
    low_half = sum_all(jnp.dot(columns, low_in, preferred_element_type=F32))

    hidden, slope, *mixed_parts = run_forward(
        (up_index, down_index, live, positions, positions),
        x_chunks, low_half, up_weight, low_out, down_weight, out_shapes, size,
    )
    mixed = scatter_sum(mixed_parts)

    cuts = 2 if count % 2 == 0 else 1
    step_x = [(i, i ^ 1) for i in range(dp_size)]
    step_y = [(i, i ^ 2) for i in range(dp_size)]

    def exchange(own, send, passed, first, second):
        got = lax.ppermute(send, "dp", first)
        onward = (passed.astype(F32) + got[1].astype(F32)).astype(BF16)
        last = lax.ppermute(onward, "dp", second)
        return own + got[0].astype(F32) + last.astype(F32)

    back_parts, low_parts, up_sums, down_sums = [], [], [], []
    for cut in range(cuts):
        back_half, back_low, up_own, up_send, up_pass, down_own, down_send, down_pass = run_gradients(
            (up_index, down_index, live, positions, quarters),
            x_chunks, y_chunks, low_half, hidden, slope, down_weight, low_out,
            cut * (count // cuts), count // cuts, dp_size, size,
        )
        back_parts.append(back_half)
        low_parts.append(back_low)
        up_sums.append(exchange(up_own, up_send, up_pass, step_x, step_y))
        down_sums.append(exchange(down_own, down_send, down_pass, step_y, step_x))
    back_low = sum_all(sum(low_parts))
    low_in_part = lax.dot_general(
        columns, back_low, (((0,), (0,)), ((), ())), preferred_element_type=F32
    )
    low_in_grad = lax.psum_scatter(low_in_part, "dp", scatter_dimension=1, tiled=True)
    input_parts = run_spread(
        (up_index, rank.reshape(1), positions),
        jnp.concatenate(back_parts, 0), up_weight, back_low, low_in, out_shapes, width, size,
    )
    input_grad = scatter_sum(input_parts)
    up_sum = jnp.concatenate(up_sums, 0)
    down_grad = jnp.concatenate(down_sums, 0)
    up_grad = up_sum[:, :up_slots]
    low_out_grad = jnp.transpose(up_sum[:, up_slots], (1, 0, 2)).reshape(size // dp_size, count * size)
    return (mixed, input_grad, up_grad, down_grad, low_out_grad, low_in_grad)


def solution(mesh):
    return jax.shard_map(
        functools.partial(local, mesh.shape["mp"], mesh.shape["dp"]),
        mesh=mesh,
        in_specs=(
            P(("dp", "mp"), None),
            P(),
            P(),
            P(),
            P("mp", None, None, None),
            P("mp", None),
            P(None, "mp"),
            P("mp", None, None, None),
            P(("dp", "mp"), None),
        ),
        out_specs=(
            P(("dp", "mp"), None),
            P(("dp", "mp"), None),
            P("mp", None, "dp", None),
            P("mp", None, "dp", None),
            P("dp", "mp"),
            P("mp", "dp"),
        ),
        check_vma=False,
    )
```

time: 1240 us -> 646 us (0.52)
  local copies, waits for them, and re-layouts: 342 us -> 15.7 us
  waiting for transfers between devices: 585 us -> 398 us
  matrix products: 131 us -> 4.57 us
  Pallas kernels: 0 us -> 123 us
  other arithmetic: 78.9 us -> 44.9 us
  blocking collectives: 62.6 us -> 29.4 us
    all_to_all x3 -> x0, waiting for transfers between devices: 426 us -> none  [the longest x1 216 us: local(): lax.all_to_all(pieces.reshape(tok_total, 1, down_width), 'mp', split_axis...]
    ppermute x0 -> x30, waiting for transfers between devices: none -> 366 us  [the longest x6 149 us: gather(): same.append(lax.ppermute(same[-1], 'mp', ring))]
    unnamed x30 -> x61, local copies, waits for them, and re-layouts: 165 us -> 7.4 us
    all_gather x2 -> x0, waiting for transfers between devices: 157 us -> none  [the longest x1 91.6 us: local(): dy_whole = lax.all_gather(cotangent, 'mp', axis=0, tiled=True)]
    dot_general x13 -> x1, matrix products: 128 us -> 2.8 us  [local(): low_half = sum_all(jnp.dot(columns, low_in, preferred_element_type=F32))]
    pallas_call x0 -> x4, Pallas kernels: none -> 123 us  [the longest x2 54.1 us: run_gradients(): pl.pallas_call(functools.partial(gradient_kernel, len(x_chunks), first, s...]
    reshape x7 -> x3, local copies, waits for them, and re-layouts: 67.3 us -> 2.47 us  [the longest x1 1.28 us: local(): jnp.transpose(up_sum[:, up_slots], (1, 0, 2))]
    psum x2 -> x0, blocking collectives: 62.6 us -> none  [the longest x1 31.3 us: local(): back_low = lax.psum(low_back_part, 'mp').astype(jnp.bfloat16)]
  transfers between devices with their start and end apart: 9 -> 33, of which waited for: 4 -> 19; matrix products, arithmetic and copies ran while one was open for 33% -> 9% of each run, Pallas kernels for 0% -> 15%
where the time goes in v1:
time: 646 us; the launch traced here: 644 us
  waiting for transfers between devices  398 us (62%)
  Pallas kernels  123 us (19%)
  other arithmetic  44.9 us (7%)
  blocking collectives  29.4 us (5%)
  local copies, waits for them, and re-layouts  15.7 us (2%)
  starting transfers between devices  14.3 us (2%)
  between operations  14.2 us (2%)
    ppermute x6, waiting for transfers between devices, gather(): same.append(lax.ppermute(same[-1], 'mp', ring))  149 us
    ppermute x6, waiting for transfers between devices, scatter_sum(): moving = lax.ppermute(moving, 'mp', ring)  129 us
    pallas_call x2, Pallas kernels, run_gradients(): pl.pallas_call(functools.partial(gradient_kernel, len(x_chunks), first, s...  54.1 us
    ppermute x4, waiting for transfers between devices, exchange(): last = lax.ppermute(onward, 'dp', second)  53.7 us
    pallas_call x1, Pallas kernels, run_forward(): pl.pallas_call(functools.partial(forward_kernel, len(chunks), len(out_sha...  40.9 us
    ppermute x4, waiting for transfers between devices, exchange(): got = lax.ppermute(send, 'dp', first)  34.4 us
    reduce_scatter x2, waiting for transfers between devices, sum_all(): low = lax.psum_scatter(partial, 'mp', scatter_dimension=0, tiled=True)  31.6 us
    all_gather x2, blocking collectives, sum_all(): return lax.all_gather(low.astype(BF16), 'mp', axis=0, tiled=True)  29.4 us
  transfers between devices with their start and end apart: 33, of which 19 were waited for; matrix products, arithmetic and copies ran while one was open for 9% of the time, Pallas kernels for 15%

profile of v1, /device:TPU:0, one launch (start us, length us, event | category | flops | bytes accessed | tf_op | source)
XLA Modules:
  0.0 643.7 jit_solution(3723852263672209706)
XLA Ops:
  7.2 3.1 collective-permute-start
  10.3 28.2 %collective-permute-done.refs_1_ = bf16[48,12288]{1,0:T(8,128)(2,1)S(1)} collective-permute-done((bf16[48,12288]{1,0:T(8,128)(2,1)}, bf16[48,12288]{1,0:T(8,128)(2,1)S(1)}, u32[]{:S(2)}, u32[]{:S(2)}) %collective-permute-start) | collective-permute-done | bytes 1179680 | tf_op jit(solution)/shard_map/ppermute | solution.py:377
  38.5 1.3 collective-permute-start.11
  39.8 29.4 %collective-permute-done.1.refs_2_ = bf16[48,12288]{1,0:T(8,128)(2,1)S(1)} collective-permute-done((bf16[48,12288]{1,0:T(8,128)(2,1)S(1)}, bf16[48,12288]{1,0:T(8,128)(2,1)S(1)}, u32[]{:S(2)}, u32[]{:S(2)}) %collective-permute-start.1) | collective-permute-done | bytes 1179680 | tf_op jit(solution)/shard_map/ppermute | solution.py:377
  69.2 25.4 %collective-permute-done.11.refs_9_ = bf16[48,12288]{1,0:T(8,128)(2,1)} collective-permute-done((bf16[48,12288]{1,0:T(8,128)(2,1)}, bf16[48,12288]{1,0:T(8,128)(2,1)}, u32[]{:S(2)}, u32[]{:S(2)}) %collective-permute-start.11) | collective-permute-done | bytes 1179680 | tf_op jit(solution)/shard_map/ppermute | solution.py:377
  94.7 1.0 sort.17
  96.2 0.9 dynamic-slice_dynamic-update-slice_fusion.7
  97.2 22.6 %collective-permute-done.2.refs_3_ = bf16[48,12288]{1,0:T(8,128)(2,1)S(1)} collective-permute-done((bf16[48,12288]{1,0:T(8,128)(2,1)S(1)}, bf16[48,12288]{1,0:T(8,128)(2,1)S(1)}, u32[]{:S(2)}, u32[]{:S(2)}) %collective-permute-start.2) | collective-permute-done | bytes 1179680 | tf_op jit(solution)/shard_map/ppermute | solution.py:377
  119.8 23.6 %collective-permute-done.12.refs_10_ = bf16[48,12288]{1,0:T(8,128)(2,1)} collective-permute-done((bf16[48,12288]{1,0:T(8,128)(2,1)}, bf16[48,12288]{1,0:T(8,128)(2,1)}, u32[]{:S(2)}, u32[]{:S(2)}) %collective-permute-start.12) | collective-permute-done | bytes 1179680 | tf_op jit(solution)/shard_map/ppermute | solution.py:377
  143.4 0.9 dynamic-slice_dynamic-update-slice_fusion.3
  144.5 0.9 copy-done.3
  146.4 1.0 copy-done.16
  147.4 3.0 gather_fusion
  150.4 2.8 fusion.20
  153.9 19.8 %collective-permute-done.13.refs_11_ = bf16[48,12288]{1,0:T(8,128)(2,1)} collective-permute-done((bf16[48,12288]{1,0:T(8,128)(2,1)}, bf16[48,12288]{1,0:T(8,128)(2,1)}, u32[]{:S(2)}, u32[]{:S(2)}) %collective-permute-start.13) | collective-permute-done | bytes 1179680 | tf_op jit(solution)/shard_map/ppermute | solution.py:377
  174.4 0.7 constant_dynamic-slice_fusion
  175.0 0.8 copy.18
  176.4 0.8 copy.17
  178.3 7.7 %reduce-scatter.4.cloned.1.call-done = f32[48,256]{1,0:T(8,128)} async-done(((f32[384,256]{1,0:T(8,128)}), f32[48,256]{1,0:T(8,128)}) %reduce-scatter.4.cloned.1.call-update) | async-done | bytes 49168 | tf_op jit(solution)/shard_map/reduce_scatter | solution.py:397
  186.0 0.8 convert_element_type.202
  186.8 15.1 %all_gather.6.refs_8_.refs_16_ = bf16[384,256]{1,0:T(8,128)(2,1)} all-gather(bf16[48,256]{1,0:T(8,128)(2,1)S(1)} %convert_element_type.202), channel_id=1, replica_groups=mesh['dp'=4,'mp'=8] {'mp'}, dimensions={0}, use_global_device_ids=true | all-gather | bytes 221184 | tf_op jit(solution)/shard_map/all_gather | solution.py:398
  202.0 40.9 %forward.1 = (bf16[24,384,256]{2,1,0:T(8,128)(2,1)}, f32[24,384,256]{2,1,0:T(8,128)}, bf16[4,48,12288]{2,1,0:T(8,128)(2,1)}, bf16[4,48,12288]{2,1,0:T(8,128)(2,1)}) custom-call(s32[72]{0:T(128)} %reshape.72.up_ref, s32[72]{0:T(128)} %reshape.73.down_ref, s32[24]{0:T(128)} %dynamic_slice.35.live_ref, s32[8]{0:T(128)} %copy-done.19, s32[8]{0:T(128)} %copy-done.19, ...), custom_call_target="tpu_custom_call" | custom-call | flops 8455716864 | bytes 60000000 | tf_op jit(solution)/shard_map/forward/pallas_call | solution.py:228
  242.9 1.0 copy-done.8
  244.3 27.0 %gradients.3 = (bf16[12,384,256]{2,1,0:T(8,128)(2,1)}, f32[384,256]{1,0:T(8,128)}, f32[12,4,64,256]{3,2,1,0:T(8,128)}, bf16[2,12,4,64,256]{4,3,2,1,0:T(8,128)(2,...) custom-call(s32[72]{0:T(128)} %reshape.72.up_ref, ...), custom_call_target="tpu_custom_call" | custom-call | flops 6643777536 | bytes 50000000 | tf_op jit(solution)/shard_map/gradients/pallas_call | solution.py:280
  271.3 1.5 collective-permute-start.28
  272.8 1.5 collective-permute-start.24
  274.3 27.1 %gradients.2 = (bf16[12,384,256]{2,1,0:T(8,128)(2,1)}, f32[384,256]{1,0:T(8,128)}, f32[12,4,64,256]{3,2,1,0:T(8,128)}, bf16[2,12,4,64,256]{4,3,2,1,0:T(8,128)(2,...) custom-call(s32[72]{0:T(128)} %reshape.72.up_ref, ...), custom_call_target="tpu_custom_call" | custom-call | flops 6643777536 | bytes 50000000 | tf_op jit(solution)/shard_map/gradients/pallas_call | solution.py:280
  302.6 1.8 add.163
  304.5 5.1 pad_maximum_fusion.refs_0_
  309.5 23.9 %reduce-scatter.6.cloned.1.call-done = f32[48,256]{1,0:T(8,128)} async-done(((f32[384,256]{1,0:T(8,128)}), f32[48,256]{1,0:T(8,128)}) %reduce-scatter.6.cloned.1.call-update) | async-done | bytes 49168 | tf_op jit(solution)/shard_map/reduce_scatter | solution.py:397
  333.4 0.8 convert_element_type.219
  334.2 14.3 %all_gather.7.refs_2_ = bf16[384,256]{1,0:T(8,128)(2,1)S(1)} all-gather(bf16[48,256]{1,0:T(8,128)(2,1)S(1)} %convert_element_type.219), channel_id=1, replica_groups=mesh['dp'=4,'mp'=8] {'mp'}, dimensions={0}, use_global_device_ids=true | all-gather | bytes 221184 | tf_op jit(solution)/shard_map/all_gather | solution.py:398
  348.5 0.7 copy-done.14
  349.2 1.8 fusion.21
  351.0 2.8 fusion.5
  353.8 1.5 collective-permute-start.29
  355.3 30.3 %collective-permute-done.26 = bf16[2,12,3,64,256]{4,3,2,1,0:T(8,128)(2,1)} collective-permute-done((bf16[2,12,3,64,256]{4,3,2,1,0:T(8,128)(2,1)}, bf16[2,12,3,64,256]{4,3,2,1,0:T(8,128)(2,1)}, u32[]{:S(2)}, u32[]{:S(2)}) %collective-permute-start.26) | collective-permute-done | bytes 2359328 | tf_op jit(solution)/shard_map/ppermute | solution.py:424
  385.6 2.7 fusion.7
  388.3 1.3 collective-permute-start.27
  389.6 27.6 %spread.1 = (bf16[4,48,12288]{2,1,0:T(8,128)(2,1)}, bf16[4,48,12288]{2,1,0:T(8,128)(2,1)}) custom-call(s32[72]{0:T(128)} %reshape.72.up_ref, s32[1]{0:T(128)} %bitcast.6.rank_ref, s32[8]{0:T(128)} %copy-done.19, bf16[24,384,256]{2,1,0:T(8,128)(2,1)} %pad_maximum_fusion.refs_0_, bf16[24,3,256,256]{3,2,1,0:T(8,128)(2,1)} %refs_1_.1, ...), custom_call_target="tpu_custom_call" | custom-call | flops 3623878656 | bytes 30000000 | tf_op jit(solution)/shard_map/spread/pallas_call | solution.py:316
  417.4 2.6 fusion.1
  420.0 4.2 collective-permute-done.22
  424.7 2.2 fusion.3
  426.9 22.5 %collective-permute-done.29 = bf16[12,3,64,256]{3,2,1,0:T(8,128)(2,1)} collective-permute-done((bf16[12,3,64,256]{3,2,1,0:T(8,128)(2,1)}, bf16[12,3,64,256]{3,2,1,0:T(8,128)(2,1)}, u32[]{:S(2)}, u32[]{:S(2)}) %collective-permute-start.29) | collective-permute-done | bytes 1179680 | tf_op jit(solution)/shard_map/ppermute | solution.py:426
  450.0 2.1 fusion.6
  452.1 21.7 %collective-permute-done.27 = bf16[12,3,64,256]{3,2,1,0:T(8,128)(2,1)S(1)} collective-permute-done((bf16[12,3,64,256]{3,2,1,0:T(8,128)(2,1)}, bf16[12,3,64,256]{3,2,1,0:T(8,128)(2,1)S(1)}, u32[]{:S(2)}, u32[]{:S(2)}) %collective-permute-start.27) | collective-permute-done | bytes 1179680 | tf_op jit(solution)/shard_map/ppermute | solution.py:426
  473.8 2.0 fusion.8
  475.8 2.7 pad_maximum_fusion.1
  478.6 1.7 fusion.16
  480.8 2.4 fusion.2
  483.2 9.5 %collective-permute-done.23 = bf16[12,4,64,256]{3,2,1,0:T(8,128)(2,1)S(1)} collective-permute-done((bf16[12,4,64,256]{3,2,1,0:T(8,128)(2,1)S(1)}, bf16[12,4,64,256]{3,2,1,0:T(8,128)(2,1)S(1)}, u32[]{:S(2)}, u32[]{:S(2)}) %collective-permute-start.23) | collective-permute-done | bytes 1572896 | tf_op jit(solution)/shard_map/ppermute | solution.py:426
  492.7 2.2 fusion.4
  495.0 1.3 copy.20
  496.3 2.7 fusion
  499.4 11.7 %collective-permute-done.8 = bf16[48,12288]{1,0:T(8,128)(2,1)S(1)} collective-permute-done((bf16[48,12288]{1,0:T(8,128)(2,1)S(1)}, bf16[48,12288]{1,0:T(8,128)(2,1)S(1)}, u32[]{:S(2)}, u32[]{:S(2)}) %collective-permute-start.8) | collective-permute-done | bytes 1179680 | tf_op jit(solution)/shard_map/ppermute | solution.py:392
  511.0 1.7 fusion.12
  512.8 23.5 %collective-permute-done.19 = bf16[48,12288]{1,0:T(8,128)(2,1)S(1)} collective-permute-done((bf16[48,12288]{1,0:T(8,128)(2,1)S(1)}, bf16[48,12288]{1,0:T(8,128)(2,1)S(1)}, u32[]{:S(2)}, u32[]{:S(2)}) %collective-permute-start.19) | collective-permute-done | bytes 1179680 | tf_op jit(solution)/shard_map/ppermute | solution.py:392
  536.8 24.8 %collective-permute-done.9 = bf16[48,12288]{1,0:T(8,128)(2,1)S(1)} collective-permute-done((bf16[48,12288]{1,0:T(8,128)(2,1)S(1)}, bf16[48,12288]{1,0:T(8,128)(2,1)S(1)}, u32[]{:S(2)}, u32[]{:S(2)}) %collective-permute-start.9) | collective-permute-done | bytes 1179680 | tf_op jit(solution)/shard_map/ppermute | solution.py:392
  561.6 1.7 fusion.13
  563.3 23.5 %collective-permute-done.20 = bf16[48,12288]{1,0:T(8,128)(2,1)S(1)} collective-permute-done((bf16[48,12288]{1,0:T(8,128)(2,1)S(1)}, bf16[48,12288]{1,0:T(8,128)(2,1)S(1)}, u32[]{:S(2)}, u32[]{:S(2)}) %collective-permute-start.20) | collective-permute-done | bytes 1179680 | tf_op jit(solution)/shard_map/ppermute | solution.py:392
  587.4 24.8 %collective-permute-done.10 = bf16[48,12288]{1,0:T(8,128)(2,1)S(1)} collective-permute-done((bf16[48,12288]{1,0:T(8,128)(2,1)S(1)}, bf16[48,12288]{1,0:T(8,128)(2,1)S(1)}, u32[]{:S(2)}, u32[]{:S(2)}) %collective-permute-start.10) | collective-permute-done | bytes 1179680 | tf_op jit(solution)/shard_map/ppermute | solution.py:392
  612.1 2.7 fusion.14
  614.8 20.9 %collective-permute-done.21 = bf16[48,12288]{1,0:T(8,128)(2,1)S(1)} collective-permute-done((bf16[48,12288]{1,0:T(8,128)(2,1)S(1)}, bf16[48,12288]{1,0:T(8,128)(2,1)S(1)}, u32[]{:S(2)}, u32[]{:S(2)}) %collective-permute-start.21) | collective-permute-done | bytes 1179680 | tf_op jit(solution)/shard_map/ppermute | solution.py:392
  635.7 1.4 fusion.11
  (114 shorter events, 9.8 us)
Async XLA Ops:
  7.2 178.8 %reduce-scatter.4.cloned.1.call-start = ((), (), s32[]{:S(2)}) async-start(), calls=%async_computation.3 | async-start | bytes 442368 | tf_op jit(solution)/shard_map/reduce_scatter | solution.py:397
  7.2 31.3 %collective-permute-start = (bf16[48,12288]{1,0:T(8,128)(2,1)}, bf16[48,12288]{1,0:T(8,128)(2,1)S(1)}, u32[]{:S(2)}, u32[]{:S(2)}) collective-permute-start(bf16[48,12288]{1,0:T(8,128)(2,1)} %refs_0_.5), channel_id=1, source_target_pairs={{0,2},{1,3},{2,4},{3,5},{4,6},{5,7},{6,0},{7,1},{8,10},{9,11},{10,... | collective-permute-start | bytes 3538952 | tf_op jit(solution)/shard_map/ppermute | solution.py:377
  38.5 111.9 %copy-start = (bf16[48,12288]{1,0:T(8,128)(2,1)}, bf16[48,12288]{1,0:T(8,128)(2,1)S(1)}, u32[]{:S(2)}) copy-start(bf16[48,12288]{1,0:T(8,128)(2,1)S(1)} %collective-permute-done.refs_1_) | copy-start | bytes 3538948
  38.5 30.7 %collective-permute-start.1 = (bf16[48,12288]{1,0:T(8,128)(2,1)S(1)}, bf16[48,12288]{1,0:T(8,128)(2,1)S(1)}, u32[]{:S(2)}, u32[]{:S(2)}) collective-permute-start(bf16[48,12288]{1,0:T(8,128)(2,1)S(1)} %collective-permute-done.refs_1_), channel_id=1, source_target_pairs={{0,2},{1,3},{2,4},{3,5},{4,6},{5,7},{6,0},{7,1},{8,10},{9,11},{10,... | collective-permute-start | bytes 3538952 | tf_op jit(solution)/shard_map/ppermute | solution.py:377
  38.5 56.1 %collective-permute-start.11 = (bf16[48,12288]{1,0:T(8,128)(2,1)}, bf16[48,12288]{1,0:T(8,128)(2,1)}, u32[]{:S(2)}, u32[]{:S(2)}) collective-permute-start(bf16[48,12288]{1,0:T(8,128)(2,1)} %refs_8_.3), channel_id=1, source_target_pairs={{0,2},{1,3},{2,4},{3,5},{4,6},{5,7},{6,0},{7,1},{8,10},{9,11},{10,... | collective-permute-start | bytes 3538952 | tf_op jit(solution)/shard_map/ppermute | solution.py:377
  69.2 81.2 %copy-start.1 = (bf16[48,12288]{1,0:T(8,128)(2,1)}, bf16[48,12288]{1,0:T(8,128)(2,1)S(1)}, u32[]{:S(2)}) copy-start(bf16[48,12288]{1,0:T(8,128)(2,1)S(1)} %collective-permute-done.1.refs_2_) | copy-start | bytes 3538948
  69.2 50.6 %collective-permute-start.2 = (bf16[48,12288]{1,0:T(8,128)(2,1)S(1)}, bf16[48,12288]{1,0:T(8,128)(2,1)S(1)}, u32[]{:S(2)}, u32[]{:S(2)}) collective-permute-start(bf16[48,12288]{1,0:T(8,128)(2,1)S(1)} %collective-permute-done.1.refs_2_), channel_id=1, source_target_pairs={{0,2},{1,3},{2,4},{3,5},{4,6},{5,7},{6,0},{7,1},{8,10},{9,11},{10,... | collective-permute-start | bytes 3538952 | tf_op jit(solution)/shard_map/ppermute | solution.py:377
  94.6 48.8 %collective-permute-start.12 = (bf16[48,12288]{1,0:T(8,128)(2,1)}, bf16[48,12288]{1,0:T(8,128)(2,1)}, u32[]{:S(2)}, u32[]{:S(2)}) collective-permute-start(bf16[48,12288]{1,0:T(8,128)(2,1)} %collective-permute-done.11.refs_9_), channel_id=1, source_target_pairs={{0,2},{1,3},{2,4},{3,5},{4,6},{5,7},{6,0},{7,1},{8,10},{9,11},{10,... | collective-permute-start | bytes 3538952 | tf_op jit(solution)/shard_map/ppermute | solution.py:377
  94.6 48.9 %collective-permute-start.3 = (bf16[48,12288]{1,0:T(8,128)(2,1)}, bf16[48,12288]{1,0:T(8,128)(2,1)}, u32[]{:S(2)}, u32[]{:S(2)}) collective-permute-start(bf16[48,12288]{1,0:T(8,128)(2,1)} %refs_0_.5), channel_id=1, source_target_pairs={{0,1},{1,0},{2,3},{3,2},{4,5},{5,4},{6,7},{7,6},{8,9},{9,8},{10,11... | collective-permute-start | bytes 3538952 | tf_op jit(solution)/shard_map/ppermute | solution.py:378
  94.7 107.3 %copy-start.19 = (s32[8]{0:T(128)}, s32[8]{0:T(128)S(1)}, u32[]{:S(2)}) copy-start(s32[8]{0:T(128)S(1)} %pad_add_fusion.pos_ref.out_ref) | copy-start | bytes 100
  95.7 48.7 %collective-permute-start.4 = (bf16[48,12288]{1,0:T(8,128)(2,1)S(1)}, bf16[48,12288]{1,0:T(8,128)(2,1)S(1)}, u32[]{:S(2)}, u32[]{:S(2)}) collective-permute-start(bf16[48,12288]{1,0:T(8,128)(2,1)S(1)} %collective-permute-done.refs_1_), channel_id=1, source_target_pairs={{0,1},{1,0},{2,3},{3,2},{4,5},{5,4},{6,7},{7,6},{8,9},{9,8},{10,11... | collective-permute-start | bytes 3538952 | tf_op jit(solution)/shard_map/ppermute | solution.py:378
  97.1 47.3 %collective-permute-start.5 = (bf16[48,12288]{1,0:T(8,128)(2,1)S(1)}, bf16[48,12288]{1,0:T(8,128)(2,1)S(1)}, u32[]{:S(2)}, u32[]{:S(2)}) collective-permute-start(bf16[48,12288]{1,0:T(8,128)(2,1)S(1)} %collective-permute-done.1.refs_2_), channel_id=1, source_target_pairs={{0,1},{1,0},{2,3},{3,2},{4,5},{5,4},{6,7},{7,6},{8,9},{9,8},{10,11... | collective-permute-start | bytes 3538952 | tf_op jit(solution)/shard_map/ppermute | solution.py:378
  119.8 33.5 %copy-start.2 = (bf16[48,12288]{1,0:T(8,128)(2,1)}, bf16[48,12288]{1,0:T(8,128)(2,1)S(1)}, u32[]{:S(2)}) copy-start(bf16[48,12288]{1,0:T(8,128)(2,1)S(1)} %collective-permute-done.2.refs_3_) | copy-start | bytes 3538948
  119.8 24.7 %collective-permute-start.6 = (bf16[48,12288]{1,0:T(8,128)(2,1)S(1)}, bf16[48,12288]{1,0:T(8,128)(2,1)S(1)}, u32[]{:S(2)}, u32[]{:S(2)}) collective-permute-start(bf16[48,12288]{1,0:T(8,128)(2,1)S(1)} %collective-permute-done.2.refs_3_), channel_id=1, source_target_pairs={{0,1},{1,0},{2,3},{3,2},{4,5},{5,4},{6,7},{7,6},{8,9},{9,8},{10,11... | collective-permute-start | bytes 3538952 | tf_op jit(solution)/shard_map/ppermute | solution.py:378
  143.4 30.3 %collective-permute-start.13 = (bf16[48,12288]{1,0:T(8,128)(2,1)}, bf16[48,12288]{1,0:T(8,128)(2,1)}, u32[]{:S(2)}, u32[]{:S(2)}) collective-permute-start(bf16[48,12288]{1,0:T(8,128)(2,1)} %collective-permute-done.12.refs_10_), channel_id=1, source_target_pairs={{0,2},{1,3},{2,4},{3,5},{4,6},{5,7},{6,0},{7,1},{8,10},{9,11},{10,... | collective-permute-start | bytes 3538952 | tf_op jit(solution)/shard_map/ppermute | solution.py:377
  144.4 1.0 copy-start.3
  144.4 1.4 copy-start.4
  145.4 1.0 copy-start.5
  146.4 1.0 copy-start.16
  147.4 27.0 %copy-start.20 = (s32[192,3]{0,1:T(4,128)S(1)}, s32[192,3]{0,1:T(4,128)}, u32[]{:S(2)}) copy-start(s32[192,3]{0,1:T(4,128)} %param.11) | copy-start | bytes 6916
  147.4 27.0 %copy-start.21 = (s32[192,3]{0,1:T(4,128)S(1)}, s32[192,3]{0,1:T(4,128)}, u32[]{:S(2)}) copy-start(s32[192,3]{0,1:T(4,128)} %param.10) | copy-start | bytes 6916
  150.4 23.3 %copy-start.22 = (s32[192]{0:T(256)S(1)}, s32[192]{0:T(256)}, u32[]{:S(2)}) copy-start(s32[192]{0:T(256)} %param.12) | copy-start | bytes 2308
  150.4 2.9 copy-start.7
  153.2 180.2 %reduce-scatter.6.cloned.1.call-start = ((), (), s32[]{:S(2)}) async-start(), calls=%async_computation.4 | async-start | bytes 442368 | tf_op jit(solution)/shard_map/reduce_scatter | solution.py:397
  153.3 89.5 %collective-permute-start.14 = (bf16[48,12288]{1,0:T(8,128)(2,1)S(1)}, bf16[48,12288]{1,0:T(8,128)(2,1)S(1)}, u32[]{:S(2)}, u32[]{:S(2)}) collective-permute-start(bf16[48,12288]{1,0:T(8,128)(2,1)S(1)} %copy-done.7), channel_id=1, source_target_pairs={{0,1},{1,0},{2,3},{3,2},{4,5},{5,4},{6,7},{7,6},{8,9},{9,8},{10,11... | collective-permute-start | bytes 3538952 | tf_op jit(solution)/shard_map/ppermute | solution.py:378
  153.4 89.5 %collective-permute-start.15 = (bf16[48,12288]{1,0:T(8,128)(2,1)}, bf16[48,12288]{1,0:T(8,128)(2,1)S(1)}, u32[]{:S(2)}, u32[]{:S(2)}) collective-permute-start(bf16[48,12288]{1,0:T(8,128)(2,1)} %collective-permute-done.11.refs_9_), channel_id=1, source_target_pairs={{0,1},{1,0},{2,3},{3,2},{4,5},{5,4},{6,7},{7,6},{8,9},{9,8},{10,11... | collective-permute-start | bytes 3538952 | tf_op jit(solution)/shard_map/ppermute | solution.py:378
  153.9 89.0 %collective-permute-start.16 = (bf16[48,12288]{1,0:T(8,128)(2,1)}, bf16[48,12288]{1,0:T(8,128)(2,1)}, u32[]{:S(2)}, u32[]{:S(2)}) collective-permute-start(bf16[48,12288]{1,0:T(8,128)(2,1)} %collective-permute-done.12.refs_10_), channel_id=1, source_target_pairs={{0,1},{1,0},{2,3},{3,2},{4,5},{5,4},{6,7},{7,6},{8,9},{9,8},{10,11... | collective-permute-start | bytes 3538952 | tf_op jit(solution)/shard_map/ppermute | solution.py:378
  173.7 69.2 %collective-permute-start.17 = (bf16[48,12288]{1,0:T(8,128)(2,1)}, bf16[48,12288]{1,0:T(8,128)(2,1)}, u32[]{:S(2)}, u32[]{:S(2)}) collective-permute-start(bf16[48,12288]{1,0:T(8,128)(2,1)} %collective-permute-done.13.refs_11_), channel_id=1, source_target_pairs={{0,1},{1,0},{2,3},{3,2},{4,5},{5,4},{6,7},{7,6},{8,9},{9,8},{10,11... | collective-permute-start | bytes 3538952 | tf_op jit(solution)/shard_map/ppermute | solution.py:378
  242.8 1.1 copy-start.8
  242.9 1.4 copy-start.9
  271.3 79.7 %collective-permute-start.28 = (bf16[2,12,3,64,256]{4,3,2,1,0:T(8,128)(2,1)}, bf16[2,12,3,64,256]{4,3,2,1,0:T(8,128)(2,1)S(1)}, u32[]{:S(2)}, u32[]{:S(2)}) collective-permute-start(bf16[2,12,3,64,256]{4,3,2,1,0:T(8,128)(2,1)} %get-tuple-element.50), channel_id=1, source_target_pairs={{0,16},{8,24},{16,0},{24,8},{1,17},{9,25},{17,1},{25,9},{2,18},{10... | collective-permute-start | bytes 7077896 | tf_op jit(solution)/shard_map/ppermute | solution.py:424
  272.8 29.8 %copy-start.18 = (f32[384,256]{1,0:T(8,128)S(1)}, f32[384,256]{1,0:T(8,128)}, u32[]{:S(2)}) copy-start(f32[384,256]{1,0:T(8,128)} %get-tuple-element.37) | copy-start | bytes 1179652
  272.8 144.4 %collective-permute-start.24 = (bf16[2,12,4,64,256]{4,3,2,1,0:T(8,128)(2,1)}, bf16[2,12,4,64,256]{4,3,2,1,0:T(8,128)(2,1)}, u32[]{:S(2)}, u32[]{:S(2)}) collective-permute-start(bf16[2,12,4,64,256]{4,3,2,1,0:T(8,128)(2,1)} %get-tuple-element.44), channel_id=1, source_target_pairs={{0,8},{8,0},{16,24},{24,16},{1,9},{9,1},{17,25},{25,17},{2,10},{10... | collective-permute-start | bytes 9437192 | tf_op jit(solution)/shard_map/ppermute | solution.py:424
  301.4 84.2 %collective-permute-start.26 = (bf16[2,12,3,64,256]{4,3,2,1,0:T(8,128)(2,1)}, bf16[2,12,3,64,256]{4,3,2,1,0:T(8,128)(2,1)}, u32[]{:S(2)}, u32[]{:S(2)}) collective-permute-start(bf16[2,12,3,64,256]{4,3,2,1,0:T(8,128)(2,1)} %get-tuple-element.47), channel_id=1, source_target_pairs={{0,16},{8,24},{16,0},{24,8},{1,17},{9,25},{17,1},{25,9},{2,18},{10... | collective-permute-start | bytes 7077896 | tf_op jit(solution)/shard_map/ppermute | solution.py:424
  302.0 176.5 %collective-permute-start.7 = (bf16[4,48,12288]{2,1,0:T(8,128)(2,1)}, bf16[4,48,12288]{2,1,0:T(8,128)(2,1)}, u32[]{:S(2)}, u32[]{:S(2)}) collective-permute-start(bf16[4,48,12288]{2,1,0:T(8,128)(2,1)} %get-tuple-element.31), channel_id=1, source_target_pairs={{0,1},{1,0},{2,3},{3,2},{4,5},{5,4},{6,7},{7,6},{8,9},{9,8},{10,11... | collective-permute-start | bytes 14155784 | tf_op jit(solution)/shard_map/ppermute | solution.py:385
  302.0 122.1 %collective-permute-start.22 = (bf16[2,12,4,64,256]{4,3,2,1,0:T(8,128)(2,1)}, bf16[2,12,4,64,256]{4,3,2,1,0:T(8,128)(2,1)}, u32[]{:S(2)}, u32[]{:S(2)}) collective-permute-start(bf16[2,12,4,64,256]{4,3,2,1,0:T(8,128)(2,1)} %get-tuple-element.41), channel_id=1, source_target_pairs={{0,8},{8,0},{16,24},{24,16},{1,9},{9,1},{17,25},{25,17},{2,10},{10... | collective-permute-start | bytes 9437192 | tf_op jit(solution)/shard_map/ppermute | solution.py:424
  304.4 332.7 %reduce-scatter.8.cloned.1.call-start = ((), (), s32[]{:S(2)}) async-start(), calls=%async_computation.5 | async-start | bytes 1966080 | tf_op jit(solution)/shard_map/reduce_scatter | solution.py:444
  304.5 44.8 %copy-start.6 = (bf16[8,48,1536]{2,1,0:T(8,128)(2,1)S(1)}, bf16[8,48,1536]{2,1,0:T(8,128)(2,1)}, u32[]{:S(2)}) copy-start(bf16[8,48,1536]{2,1,0:T(8,128)(2,1)} %gather_fusion) | copy-start | bytes 3538948
  348.5 0.7 copy-start.14
  351.0 34.6 %copy-start.17 = (bf16[12,3,64,256]{3,2,1,0:T(8,128)(2,1)S(1)}, bf16[12,3,64,256]{3,2,1,0:T(8,128)(2,1)}, u32[]{:S(2)}) copy-start(bf16[12,3,64,256]{3,2,1,0:T(8,128)(2,1)} %get-tuple-element.48) | copy-start | bytes 3538948
  353.8 95.6 %collective-permute-start.29 = (bf16[12,3,64,256]{3,2,1,0:T(8,128)(2,1)}, bf16[12,3,64,256]{3,2,1,0:T(8,128)(2,1)}, u32[]{:S(2)}, u32[]{:S(2)}) collective-permute-start(bf16[12,3,64,256]{3,2,1,0:T(8,128)(2,1)} %fusion.5), channel_id=1, source_target_pairs={{0,8},{8,0},{16,24},{24,16},{1,9},{9,1},{17,25},{25,17},{2,10},{10... | collective-permute-start | bytes 3538952 | tf_op jit(solution)/shard_map/ppermute | solution.py:426
  388.3 85.5 %collective-permute-start.27 = (bf16[12,3,64,256]{3,2,1,0:T(8,128)(2,1)}, bf16[12,3,64,256]{3,2,1,0:T(8,128)(2,1)S(1)}, u32[]{:S(2)}, u32[]{:S(2)}) collective-permute-start(bf16[12,3,64,256]{3,2,1,0:T(8,128)(2,1)} %fusion.7), channel_id=1, source_target_pairs={{0,8},{8,0},{16,24},{24,16},{1,9},{9,1},{17,25},{25,17},{2,10},{10... | collective-permute-start | bytes 3538952 | tf_op jit(solution)/shard_map/ppermute | solution.py:426
  417.3 81.7 %collective-permute-start.18 = (bf16[4,48,12288]{2,1,0:T(8,128)(2,1)}, bf16[4,48,12288]{2,1,0:T(8,128)(2,1)S(1)}, u32[]{:S(2)}, u32[]{:S(2)}) collective-permute-start(bf16[4,48,12288]{2,1,0:T(8,128)(2,1)} %get-tuple-element.39), channel_id=1, source_target_pairs={{0,1},{1,0},{2,3},{3,2},{4,5},{5,4},{6,7},{7,6},{8,9},{9,8},{10,11... | collective-permute-start | bytes 14155784 | tf_op jit(solution)/shard_map/ppermute | solution.py:385
  417.4 7.4 %copy-start.15 = (bf16[12,4,64,256]{3,2,1,0:T(8,128)(2,1)S(1)}, bf16[12,4,64,256]{3,2,1,0:T(8,128)(2,1)}, u32[]{:S(2)}) copy-start(bf16[12,4,64,256]{3,2,1,0:T(8,128)(2,1)} %get-tuple-element.42) | copy-start | bytes 4718596
  424.1 56.2 %collective-permute-start.25 = (bf16[12,4,64,256]{3,2,1,0:T(8,128)(2,1)S(1)}, bf16[12,4,64,256]{3,2,1,0:T(8,128)(2,1)S(1)}, u32[]{:S(2)}, u32[]{:S(2)}) collective-permute-start(bf16[12,4,64,256]{3,2,1,0:T(8,128)(2,1)S(1)} %fusion.1), channel_id=1, source_target_pairs={{0,16},{8,24},{16,0},{24,8},{1,17},{9,25},{17,1},{25,9},{2,18},{10... | collective-permute-start | bytes 4718600 | tf_op jit(solution)/shard_map/ppermute | solution.py:426
  424.7 25.3 %copy-start.12 = (f32[12,3,64,256]{3,2,1,0:T(8,128)S(1)}, f32[12,3,64,256]{3,2,1,0:T(8,128)}, u32[]{:S(2)}) copy-start(f32[12,3,64,256]{3,2,1,0:T(8,128)} %get-tuple-element.49) | copy-start | bytes 7077892
  449.4 43.3 %collective-permute-start.23 = (bf16[12,4,64,256]{3,2,1,0:T(8,128)(2,1)S(1)}, bf16[12,4,64,256]{3,2,1,0:T(8,128)(2,1)S(1)}, u32[]{:S(2)}, u32[]{:S(2)}) collective-permute-start(bf16[12,4,64,256]{3,2,1,0:T(8,128)(2,1)S(1)} %fusion.3), channel_id=1, source_target_pairs={{0,16},{8,24},{16,0},{24,8},{1,17},{9,25},{17,1},{25,9},{2,18},{10... | collective-permute-start | bytes 4718600 | tf_op jit(solution)/shard_map/ppermute | solution.py:426
  450.0 23.8 %copy-start.13 = (f32[12,3,64,256]{3,2,1,0:T(8,128)S(1)}, f32[12,3,64,256]{3,2,1,0:T(8,128)}, u32[]{:S(2)}) copy-start(f32[12,3,64,256]{3,2,1,0:T(8,128)} %get-tuple-element.46) | copy-start | bytes 7077892
  473.8 4.7 slice-start
  475.8 2.7 slice-start.1
  478.6 2.2 copy-start.10
  480.3 30.8 %collective-permute-start.8 = (bf16[48,12288]{1,0:T(8,128)(2,1)S(1)}, bf16[48,12288]{1,0:T(8,128)(2,1)S(1)}, u32[]{:S(2)}, u32[]{:S(2)}) collective-permute-start(bf16[48,12288]{1,0:T(8,128)(2,1)S(1)} %fusion.16), channel_id=1, source_target_pairs={{0,2},{1,3},{2,4},{3,5},{4,6},{5,7},{6,0},{7,1},{8,10},{9,11},{10,... | collective-permute-start | bytes 3538952 | tf_op jit(solution)/shard_map/ppermute | solution.py:392
  480.8 11.9 %copy-start.11 = (f32[12,4,64,256]{3,2,1,0:T(8,128)S(1)}, f32[12,4,64,256]{3,2,1,0:T(8,128)}, u32[]{:S(2)}) copy-start(f32[12,4,64,256]{3,2,1,0:T(8,128)} %get-tuple-element.40) | copy-start | bytes 9437188
  495.0 4.0 slice-start.2
  496.3 2.7 slice-start.3
  499.3 37.0 %collective-permute-start.19 = (bf16[48,12288]{1,0:T(8,128)(2,1)S(1)}, bf16[48,12288]{1,0:T(8,128)(2,1)S(1)}, u32[]{:S(2)}, u32[]{:S(2)}) collective-permute-start(bf16[48,12288]{1,0:T(8,128)(2,1)S(1)} %fusion.17), channel_id=1, source_target_pairs={{0,2},{1,3},{2,4},{3,5},{4,6},{5,7},{6,0},{7,1},{8,10},{9,11},{10,... | collective-permute-start | bytes 3538952 | tf_op jit(solution)/shard_map/ppermute | solution.py:392
  512.7 48.9 %collective-permute-start.9 = (bf16[48,12288]{1,0:T(8,128)(2,1)S(1)}, bf16[48,12288]{1,0:T(8,128)(2,1)S(1)}, u32[]{:S(2)}, u32[]{:S(2)}) collective-permute-start(bf16[48,12288]{1,0:T(8,128)(2,1)S(1)} %fusion.12), channel_id=1, source_target_pairs={{0,2},{1,3},{2,4},{3,5},{4,6},{5,7},{6,0},{7,1},{8,10},{9,11},{10,... | collective-permute-start | bytes 3538952 | tf_op jit(solution)/shard_map/ppermute | solution.py:392
  536.7 50.1 %collective-permute-start.20 = (bf16[48,12288]{1,0:T(8,128)(2,1)S(1)}, bf16[48,12288]{1,0:T(8,128)(2,1)S(1)}, u32[]{:S(2)}, u32[]{:S(2)}) collective-permute-start(bf16[48,12288]{1,0:T(8,128)(2,1)S(1)} %fusion.9), channel_id=1, source_target_pairs={{0,2},{1,3},{2,4},{3,5},{4,6},{5,7},{6,0},{7,1},{8,10},{9,11},{10,... | collective-permute-start | bytes 3538952 | tf_op jit(solution)/shard_map/ppermute | solution.py:392
  563.3 48.9 %collective-permute-start.10 = (bf16[48,12288]{1,0:T(8,128)(2,1)S(1)}, bf16[48,12288]{1,0:T(8,128)(2,1)S(1)}, u32[]{:S(2)}, u32[]{:S(2)}) collective-permute-start(bf16[48,12288]{1,0:T(8,128)(2,1)S(1)} %fusion.13), channel_id=1, source_target_pairs={{0,2},{1,3},{2,4},{3,5},{4,6},{5,7},{6,0},{7,1},{8,10},{9,11},{10,... | collective-permute-start | bytes 3538952 | tf_op jit(solution)/shard_map/ppermute | solution.py:392
  587.3 48.4 %collective-permute-start.21 = (bf16[48,12288]{1,0:T(8,128)(2,1)S(1)}, bf16[48,12288]{1,0:T(8,128)(2,1)S(1)}, u32[]{:S(2)}, u32[]{:S(2)}) collective-permute-start(bf16[48,12288]{1,0:T(8,128)(2,1)S(1)} %fusion.10), channel_id=1, source_target_pairs={{0,2},{1,3},{2,4},{3,5},{4,6},{5,7},{6,0},{7,1},{8,10},{9,11},{10,... | collective-permute-start | bytes 3538952 | tf_op jit(solution)/shard_map/ppermute | solution.py:392
Sparse Core Ops, SparseCore 0:
  153.4 32.6 reduce-scatter.3
  304.5 28.8 reduce-scatter.5
  351.1 41.7 reduce-scatter.7

commit v2 on v0

v2 whole, which is shorter than its diff:
```python
import functools

import jax
import jax.numpy as jnp
from jax import lax
from jax.experimental import pallas as pl
from jax.experimental.pallas import tpu as pltpu
from jax.sharding import PartitionSpec as P

F32 = jnp.float32
BF16 = jnp.bfloat16
GELU_SCALE = 0.7978845608028654
GELU_CUBE = 0.044715
PER_HIDDEN, PER_PIECES, PER_BACK, PER_GRADIENTS, PER_SPREAD = 4, 6, 4, 3, 6
COST = pl.CostEstimate(flops=1, bytes_accessed=1, transcendentals=0)
VMEM_LIMIT = 60 * 1024 * 1024


def dot_nn(a, b):
    return lax.dot_general(a, b, (((1,), (0,)), ((), ())), preferred_element_type=F32)


def dot_nt(a, b):
    return lax.dot_general(a, b, (((1,), (1,)), ((), ())), preferred_element_type=F32)


def dot_tn(a, b):
    return lax.dot_general(a, b, (((0,), (0,)), ((), ())), preferred_element_type=F32)


def column_block(index, size):
    return pl.ds(pl.multiple_of(index * size, size), size)


def copies_in(chunks, held, sems):
    rows, columns = chunks[0].shape
    blocks = held.shape[0] // rows
    return [
        pltpu.make_async_copy(
            chunk,
            held.at[pl.ds(number % blocks * rows, rows), pl.ds(number // blocks * columns, columns)],
            sems.at[number],
        )
        for number, chunk in enumerate(chunks)
    ]


def fill_zero(total, size):
    @pl.loop(0, total.shape[1] // size)
    def _(block):
        total[:, column_block(block, size)] = jnp.zeros((total.shape[0], size), total.dtype)


def write_out(total, held, outs, sems, size):
    @pl.loop(0, total.shape[1] // size)
    def _(block):
        columns = column_block(block, size)
        held[:, columns] = total[:, columns].astype(held.dtype)

    copies = []
    for number, out in enumerate(outs):
        rows = out.shape[0]
        copies.append(
            pltpu.make_async_copy(held.at[pl.ds(number * rows, rows), :], out, sems.at[number])
        )
    for copy in copies:
        copy.start()
    for copy in copies:
        copy.wait()


def hidden_kernel(chunk_count, wait_count, per, size, up_ref, *refs):
    chunks = refs[:chunk_count]
    low_half, up_weight, low_out = refs[chunk_count : chunk_count + 3]
    hidden, slope, held, in_sems = refs[chunk_count + 3 + wait_count :]
    up_slots = up_weight.shape[1]

    @pl.when(pl.program_id(0) == 0)
    def _():
        copies = copies_in(chunks, held, in_sems)
        for copy in copies:
            copy.start()
        for copy in copies:
            copy.wait()

    for inner in range(per):
        first = (pl.program_id(0) * per + inner) * up_slots
        picked = [held[:, column_block(up_ref[first + slot], size)] for slot in range(up_slots)]
        weights = [up_weight[inner, slot] for slot in range(up_slots)]
        before = dot_nn(
            jnp.concatenate(picked + [low_half[...]], axis=1),
            jnp.concatenate(weights + [low_out[:, inner * size : (inner + 1) * size]], axis=0),
        )
        square = before * before
        bent = jnp.tanh(GELU_SCALE * before * (1.0 + GELU_CUBE * square))
        half = 0.5 * (1.0 + bent)
        hidden[inner] = (before * half).astype(BF16)
        slope[inner] = half + 0.5 * before * (1.0 - bent * bent) * (
            GELU_SCALE * (1.0 + 3.0 * GELU_CUBE * square)
        )


def pieces_kernel(out_count, wait_count, per, size, down_ref, live_ref, *refs):
    hidden, down_weight = refs[:2]
    first_out = 2 + wait_count
    outs = refs[first_out : first_out + out_count]
    held, total, out_sems = refs[first_out + out_count :]
    down_slots = down_weight.shape[1]

    @pl.when(pl.program_id(0) == 0)
    def _():
        fill_zero(total, size)

    for inner in range(per):
        step = pl.program_id(0) * per + inner
        weights = [
            jnp.where(slot < live_ref[step], down_weight[inner, slot], jnp.zeros((), BF16))
            for slot in range(down_slots)
        ]
        pieces = dot_nn(hidden[inner], jnp.concatenate(weights, axis=1))
        for slot in range(down_slots):
            columns = column_block(down_ref[step * down_slots + slot], size)
            total[:, columns] += pieces[:, slot * size : (slot + 1) * size]

    @pl.when(pl.program_id(0) == pl.num_programs(0) - 1)
    def _():
        write_out(total, held, outs, out_sems, size)


def back_kernel(chunk_count, wait_count, per, size, down_ref, live_ref, *refs):
    chunks = refs[:chunk_count]
    slope, down_weight, low_out = refs[chunk_count : chunk_count + 3]
    back_half, back_low, held, sems = refs[chunk_count + 3 + wait_count :]
    down_slots = down_weight.shape[1]

    @pl.when(pl.program_id(0) == 0)
    def _():
        copies = copies_in(chunks, held, sems)
        for copy in copies:
            copy.start()
        back_low[...] = jnp.zeros(back_low.shape, F32)
        for copy in copies:
            copy.wait()

    backs = []
    for inner in range(per):
        step = pl.program_id(0) * per + inner
        wanted = [
            held[:, column_block(down_ref[step * down_slots + slot], size)]
            for slot in range(down_slots)
        ]
        weights = [
            jnp.where(slot < live_ref[step], down_weight[inner, slot], jnp.zeros((), BF16))
            for slot in range(down_slots)
        ]
        back_hidden = dot_nt(jnp.concatenate(wanted, axis=1), jnp.concatenate(weights, axis=1))
        back = (back_hidden * slope[inner]).astype(BF16)
        back_half[inner] = back
        backs.append(back)
    back_low[...] += dot_nt(jnp.concatenate(backs, axis=1), low_out[...])


def load_all(chunks, held, sems):
    @pl.when(pl.program_id(0) == 0)
    def _():
        copies = copies_in(chunks, held, sems)
        for copy in copies:
            copy.start()
        for copy in copies:
            copy.wait()


def write_groups(groups, outs, per, make):
    first = 0
    for number, (length, way) in enumerate(groups):
        steps = length // per
        inside = (pl.program_id(0) >= first) & (pl.program_id(0) < first + steps)

        @pl.when(inside)
        def _(number=number, way=way):
            own, send, passed = outs[3 * number : 3 * number + 3]
            for inner in range(per):
                for slot in range(own.shape[1]):
                    own[inner, slot] = make(inner, slot, 0)
                    passed[inner, slot] = make(inner, slot, 3 - way).astype(BF16)
                    send[0, inner, slot] = make(inner, slot, way).astype(BF16)
                    send[1, inner, slot] = make(inner, slot, 3).astype(BF16)

        first += steps


def down_kernel(
    chunk_count, wait_count, first_step, per, groups, size, down_ref, live_ref, quarter_ref, *refs
):
    chunks = refs[:chunk_count]
    hidden = refs[chunk_count]
    outs = refs[chunk_count + 1 + wait_count : -3]
    held, part, sems = refs[-3:]
    slots, rows = outs[0].shape[1:3]
    load_all(chunks, held, sems)
    step = first_step + pl.program_id(0) * per
    for inner in range(per):
        wanted = [
            held[:, column_block(down_ref[(step + inner) * slots + slot], size)]
            for slot in range(slots)
        ]
        part[inner] = dot_tn(hidden[inner], jnp.concatenate(wanted, axis=1))

    def make(inner, slot, which):
        keep = (slot < live_ref[step + inner]).astype(F32)
        first = pl.multiple_of(quarter_ref[which] * rows, rows)
        return part[inner, pl.ds(first, rows), slot * size : (slot + 1) * size] * keep

    write_groups(groups, outs, per, make)


def up_kernel(chunk_count, wait_count, first_step, per, groups, size, up_ref, quarter_ref, *refs):
    chunks = refs[:chunk_count]
    low_half, back_half = refs[chunk_count : chunk_count + 2]
    outs = refs[chunk_count + 2 + wait_count : -3]
    held, part, sems = refs[-3:]
    slots, rows = outs[0].shape[1] - 1, outs[0].shape[2]
    load_all(chunks, held, sems)
    step = first_step + pl.program_id(0) * per
    for inner in range(per):
        picked = [
            held[:, column_block(up_ref[(step + inner) * slots + slot], size)]
            for slot in range(slots)
        ]
        part[inner] = dot_tn(jnp.concatenate(picked + [low_half[...]], axis=1), back_half[inner])

    def make(inner, slot, which):
        first = pl.multiple_of(quarter_ref[which] * rows + slot * size, rows)
        return part[inner, pl.ds(first, rows), :]

    write_groups(groups, outs, per, make)


def spread_kernel(out_count, wait_count, per, size, up_ref, rank_ref, *refs):
    back_half, up_weight, back_low, low_in = refs[:4]
    first_out = 4 + wait_count
    outs = refs[first_out : first_out + out_count]
    held, total, out_sems = refs[first_out + out_count :]
    up_slots = up_weight.shape[1]

    @pl.when(pl.program_id(0) == 0)
    def _():
        fill_zero(total, size)
        first = rank_ref[0] * (low_in.shape[0] // size)

        @pl.loop(0, low_in.shape[0] // size)
        def _(block):
            rows = pl.ds(pl.multiple_of(block * size, size), size)
            side = dot_nt(back_low[...], low_in[rows, :])
            total[:, column_block(first + block, size)] = side

    for inner in range(per):
        step = pl.program_id(0) * per + inner
        weights = jnp.concatenate([up_weight[inner, slot] for slot in range(up_slots)], axis=0)
        spread = dot_nt(back_half[inner], weights)
        for slot in range(up_slots):
            columns = column_block(up_ref[step * up_slots + slot], size)
            total[:, columns] += spread[:, slot * size : (slot + 1) * size]

    @pl.when(pl.program_id(0) == pl.num_programs(0) - 1)
    def _():
        write_out(total, held, outs, out_sems, size)


def whole_spec(array):
    zeros = (0,) * array.ndim
    return pl.BlockSpec(array.shape, lambda i, *_: zeros)


def any_spec():
    return pl.BlockSpec(memory_space=pl.ANY)


def block_spec(array, per, first=0):
    rest = (0,) * (array.ndim - 1)
    return pl.BlockSpec((per,) + array.shape[1:], lambda i, *_: (i + first // per,) + rest)


def blocks_per_step(count, most):
    return max(per for per in range(1, most + 1) if count % per == 0)


def params():
    return pltpu.CompilerParams(
        dimension_semantics=("arbitrary",), vmem_limit_bytes=VMEM_LIMIT
    )


def shape(dims, dtype):
    return jax.ShapeDtypeStruct(dims, dtype)


def run_hidden(scalars, chunks, low_half, up_weight, low_out, waits, size):
    count, tok_total, width = up_weight.shape[0], low_half.shape[0], chunks[0].shape[1]
    per = blocks_per_step(count, PER_HIDDEN)
    hidden = shape((count, tok_total, size), BF16)
    slope = shape((count, tok_total, size), F32)
    return pl.pallas_call(
        functools.partial(hidden_kernel, len(chunks), len(waits), per, size),
        out_shape=[hidden, slope],
        grid_spec=pltpu.PrefetchScalarGridSpec(
            num_scalar_prefetch=len(scalars),
            grid=(count // per,),
            in_specs=[any_spec()] * len(chunks)
            + [
                whole_spec(low_half),
                block_spec(up_weight, per),
                pl.BlockSpec((low_out.shape[0], per * size), lambda i, *_: (0, i)),
            ]
            + [any_spec()] * len(waits),
            out_specs=[block_spec(hidden, per), block_spec(slope, per)],
            scratch_shapes=[
                pltpu.VMEM((tok_total, width), BF16),
                pltpu.SemaphoreType.DMA((len(chunks),)),
            ],
        ),
        compiler_params=params(),
        cost_estimate=COST,
        name="hidden",
    )(*scalars, *chunks, low_half, up_weight, low_out, *waits)


def run_pieces(scalars, hidden, down_weight, waits, out_shapes, width, size):
    count, tok_total = hidden.shape[:2]
    per = blocks_per_step(count, PER_PIECES)
    return pl.pallas_call(
        functools.partial(pieces_kernel, len(out_shapes), len(waits), per, size),
        out_shape=[shape(dims, BF16) for dims in out_shapes],
        grid_spec=pltpu.PrefetchScalarGridSpec(
            num_scalar_prefetch=len(scalars),
            grid=(count // per,),
            in_specs=[block_spec(hidden, per), block_spec(down_weight, per)] + [any_spec()] * len(waits),
            out_specs=[any_spec()] * len(out_shapes),
            scratch_shapes=[
                pltpu.VMEM((tok_total, width), BF16),
                pltpu.VMEM((tok_total, width), F32),
                pltpu.SemaphoreType.DMA((len(out_shapes),)),
            ],
        ),
        compiler_params=params(),
        cost_estimate=COST,
        name="pieces",
    )(*scalars, hidden, down_weight, *waits)


def run_back(scalars, chunks, slope, down_weight, low_out, waits, width, size):
    count, tok_total = slope.shape[:2]
    per = blocks_per_step(count, PER_BACK)
    back_half = shape((count, tok_total, size), BF16)
    back_low = shape((tok_total, low_out.shape[0]), F32)
    return pl.pallas_call(
        functools.partial(back_kernel, len(chunks), len(waits), per, size),
        out_shape=[back_half, back_low],
        grid_spec=pltpu.PrefetchScalarGridSpec(
            num_scalar_prefetch=len(scalars),
            grid=(count // per,),
            in_specs=[any_spec()] * len(chunks)
            + [
                block_spec(slope, per),
                block_spec(down_weight, per),
                pl.BlockSpec((low_out.shape[0], per * size), lambda i, *_: (0, i)),
            ]
            + [any_spec()] * len(waits),
            out_specs=[block_spec(back_half, per), whole_spec(back_low)],
            scratch_shapes=[
                pltpu.VMEM((tok_total, width), BF16),
                pltpu.SemaphoreType.DMA((len(chunks),)),
            ],
        ),
        compiler_params=params(),
        cost_estimate=COST,
        name="back",
    )(*scalars, *chunks, slope, down_weight, low_out, *waits)


def run_gradients(
    kernel, scalars, chunks, whole, blocks, waits, first, groups, slots, part_shape, parts, width
):
    per = min(blocks_per_step(length, PER_GRADIENTS) for length, _ in groups)
    tok_total, size = blocks.shape[1:]
    rows = size // parts
    outs, specs, step = [], [], 0
    for length, _ in groups:
        last = length // per - 1

        def place(i, start=step, last=last):
            return jnp.clip(i - start, 0, last)

        outs += [
            shape((length, slots, rows, size), F32),
            shape((2, length, slots, rows, size), BF16),
            shape((length, slots, rows, size), BF16),
        ]
        one = pl.BlockSpec((per, slots, rows, size), lambda i, *_, at=place: (at(i), 0, 0, 0))
        two = pl.BlockSpec((2, per, slots, rows, size), lambda i, *_, at=place: (0, at(i), 0, 0, 0))
        specs += [one, two, one]
        step += length // per
    results = pl.pallas_call(
        functools.partial(kernel, len(chunks), len(waits), first, per, groups, size),
        out_shape=outs,
        grid_spec=pltpu.PrefetchScalarGridSpec(
            num_scalar_prefetch=len(scalars),
            grid=(step,),
            in_specs=[any_spec()] * len(chunks)
            + [whole_spec(array) for array in whole]
            + [block_spec(blocks, per, first)]
            + [any_spec()] * len(waits),
            out_specs=specs,
            scratch_shapes=[
                pltpu.VMEM((tok_total, width), BF16),
                pltpu.VMEM((per,) + part_shape, F32),
                pltpu.SemaphoreType.DMA((len(chunks),)),
            ],
        ),
        compiler_params=params(),
        cost_estimate=COST,
        name=kernel.__name__,
    )(*scalars, *chunks, *whole, blocks, *waits)
    return [results[3 * number : 3 * number + 3] for number in range(len(groups))]


def run_spread(scalars, back_half, up_weight, back_low, low_in, waits, out_shapes, width, size):
    count, tok_total = back_half.shape[:2]
    per = blocks_per_step(count, PER_SPREAD)
    return pl.pallas_call(
        functools.partial(spread_kernel, len(out_shapes), len(waits), per, size),
        out_shape=[shape(dims, BF16) for dims in out_shapes],
        grid_spec=pltpu.PrefetchScalarGridSpec(
            num_scalar_prefetch=len(scalars),
            grid=(count // per,),
            in_specs=[
                block_spec(back_half, per),
                block_spec(up_weight, per),
                whole_spec(back_low),
                whole_spec(low_in),
            ]
            + [any_spec()] * len(waits),
            out_specs=[any_spec()] * len(out_shapes),
            scratch_shapes=[
                pltpu.VMEM((tok_total, width), BF16),
                pltpu.VMEM((tok_total, width), F32),
                pltpu.SemaphoreType.DMA((len(out_shapes),)),
            ],
        ),
        compiler_params=params(),
        cost_estimate=COST,
        name="spread",
    )(*scalars, back_half, up_weight, back_low, low_in, *waits)


def pass_kernel(half_count, *refs):
    out, first = refs[-1], 0
    for half in range(half_count):
        passed, got = refs[2 * half : 2 * half + 2]
        length = passed.shape[0]
        out[first : first + length] = (passed[...].astype(F32) + got[0].astype(F32)).astype(BF16)
        first += length


def run_pass(halves):
    length = sum(passed.shape[0] for passed, _ in halves)
    out = shape((length,) + halves[0][0].shape[1:], BF16)
    specs = []
    for passed, got in halves:
        specs += [
            whole_spec(passed),
            pl.BlockSpec((1,) + got.shape[1:], lambda i: (1, 0, 0, 0, 0)),
        ]
    return pl.pallas_call(
        functools.partial(pass_kernel, len(halves)),
        out_shape=out,
        grid=(1,),
        in_specs=specs,
        out_specs=whole_spec(out),
        compiler_params=params(),
        cost_estimate=COST,
        name="pass_on",
    )(*[array for pair in halves for array in pair])


def add_kernel(*refs):
    total = refs[0][...].astype(F32)
    for part in refs[1:-1]:
        total = total + part[...].astype(F32)
    refs[-1][...] = total.astype(BF16)


def run_add(arrays):
    rows, width = arrays[0].shape
    steps = 4 if width % 512 == 0 else 1
    spec = pl.BlockSpec((rows, width // steps), lambda i: (0, i))
    return pl.pallas_call(
        add_kernel,
        out_shape=shape((rows, width), BF16),
        grid=(steps,),
        in_specs=[spec] * len(arrays),
        out_specs=spec,
        compiler_params=params(),
        cost_estimate=COST,
        name="add_rows",
    )(*arrays)


def side_kernel(columns, back_low, out):
    out[...] = dot_tn(columns[...], back_low[...]).astype(BF16)


def run_side(columns, back_low, size):
    return pl.pallas_call(
        side_kernel,
        out_shape=shape((columns.shape[1], back_low.shape[1]), BF16),
        grid=(1,),
        in_specs=[whole_spec(columns), whole_spec(back_low)],
        out_specs=pl.BlockSpec((columns.shape[1], back_low.shape[1]), lambda i: (0, 0)),
        compiler_params=params(),
        cost_estimate=COST,
        name="low_in_part",
    )(columns, back_low)


def fence(values, waits):
    values, waits = list(values), list(waits)
    return list(pl.pallas_call(
        lambda *refs: None,
        out_shape=[shape(value.shape, value.dtype) for value in values],
        in_specs=[any_spec()] * (len(values) + len(waits)),
        out_specs=[any_spec()] * len(values),
        input_output_aliases={number: number for number in range(len(values))},
        compiler_params=pltpu.CompilerParams(vmem_limit_bytes=VMEM_LIMIT),
        cost_estimate=COST,
        name="fence",
    )(*values, *waits))


def local(mp_size, dp_size, tokens, up_blocks, down_blocks, down_live, up_weight, low_in, low_out, down_weight, cotangent):
    count, up_slots, size = up_weight.shape[:3]
    rows, width = tokens.shape
    tok_total = rows * mp_size
    col_width = low_in.shape[0]
    rank = lax.axis_index("mp")
    part = lax.axis_index("dp")
    chips = mp_size // 2
    by_ring = rows % 16 == 0 and chips == 4
    swap = [(i, i ^ 1) for i in range(mp_size)]
    step_x = [(i, i ^ 1) for i in range(dp_size)]
    step_y = [(i, i ^ 2) for i in range(dp_size)]

    up_index = lax.dynamic_slice_in_dim(up_blocks, rank * count, count, 0).reshape(-1)
    down_index = lax.dynamic_slice_in_dim(down_blocks, rank * count, count, 0).reshape(-1)
    live = lax.dynamic_slice_in_dim(down_live, rank * count, count, 0)
    quarters = part ^ jnp.arange(dp_size, dtype=jnp.int32)
    out_shapes = [(rows, width)] * mp_size if by_ring else [(tok_total, width)]

    def swapped(piece):
        return lax.ppermute(piece, "mp", swap)

    def shifted(piece, by):
        return lax.ppermute(piece, "mp", [(i, (i + 2 * by) % mp_size) for i in range(mp_size)])

    def add_round(parts, given, place, *moved):
        return run_add([parts[place % chips], given[place % chips], *moved])

    def scatter_whole(parts):
        whole = parts[0].reshape(mp_size, rows, width)
        return lax.psum_scatter(whole, "mp", scatter_dimension=0)

    def over_dp(value, way):
        return lax.ppermute(value, "dp", step_y if way == 2 else step_x)

    def pass_on(parts, gots):
        return [
            run_pass([(part[n][2], got[n]) for part, got in zip(parts, gots)])
            for n in range(len(groups))
        ]

    def sum_rows(chip_sums):
        low = chip_sums[0]
        for back in range(1, chips):
            low = low + shifted(chip_sums[back], -back)
        low = low.astype(BF16)
        same = jnp.concatenate([low] + [shifted(low, back) for back in range(1, chips)], 0)
        return same, jnp.concatenate([same, swapped(same)], 0)

    def sum_whole(partial):
        low = lax.psum_scatter(partial, "mp", scatter_dimension=0, tiled=True).astype(BF16)
        return lax.all_gather(low, "mp", axis=0, tiled=True)

    def take_columns(piece, place):
        return lax.dynamic_slice_in_dim(piece, place * col_width, col_width, 1)

    if by_ring:
        both_low = jnp.concatenate([low_in, swapped(low_in)], 0)
        x_same, chip_sums = [tokens], []
        for step in range(chips):
            both = [take_columns(x_same[step], rank), take_columns(x_same[step], rank ^ 1)]
            chip_sums.append(
                jnp.dot(jnp.concatenate(both, 1), both_low, preferred_element_type=F32)
            )
            if step < chips - 1:
                x_same.append(shifted(x_same[step], 1))
        x_chunks = x_same + [swapped(piece) for piece in x_same]
        low_same, low_half = sum_rows(chip_sums)
        y_same, y_other = [cotangent], [swapped(cotangent)]
        arriving = shifted(fence([cotangent], [low_same])[0], 1)
    else:
        x_chunks = [lax.all_gather(tokens, "mp", axis=0, tiled=True)]
        y_chunks = [lax.all_gather(cotangent, "mp", axis=0, tiled=True)]
        low = jnp.dot(take_columns(x_chunks[0], rank), low_in, preferred_element_type=F32)
        low_half = sum_whole(low)
    columns = jnp.concatenate([take_columns(piece, rank) for piece in x_chunks], 0)
    hidden, slope = run_hidden((up_index,), x_chunks, low_half, up_weight, low_out, [], size)
    if by_ring:
        arrived, hidden = fence([arriving, hidden], y_other + [slope])
        y_same.append(arrived)
        y_other.append(swapped(arrived))
        arriving = shifted(arrived, 1)
    mixed_parts = list(
        run_pieces((down_index, live), hidden, down_weight, [], out_shapes, width, size)
    )
    if by_ring:
        arrived, *mixed_parts[chips:] = fence(
            [arriving] + mixed_parts[chips:], y_other + [columns]
        )
        y_same.append(arrived)
        y_other.append(swapped(arrived))
        arriving = shifted(arrived, 1)
        mixed_given = [None] + [swapped(piece) for piece in mixed_parts[chips + 1 :]]
        arrived = fence([arriving], mixed_given[1:] + y_other)[0]
        y_same.append(arrived)
        y_other.append(swapped(arrived))
        y_chunks = y_same + y_other

    down_slots = down_weight.shape[1]
    if count % 4 == 0:
        groups = ((count // 4, 2), (count // 4, 1))
        starts = (0, count // 2)
    else:
        groups, starts = ((count, 2),), (0,)

    def down_part(start, waits):
        return run_gradients(
            down_kernel, (down_index, live, quarters), y_chunks, [], hidden, waits, start, groups,
            down_slots, (size, down_slots * size), dp_size, width,
        )

    def up_part(start, waits):
        return run_gradients(
            up_kernel, (up_index, quarters), x_chunks, [low_half], back_half, waits, start, groups,
            up_slots + 1, ((up_slots + 1) * size, size), dp_size, width,
        )

    def send_round(parts, moving, waits, give=()):
        here = [part[1] for part in parts]
        sent = fence(here + moving + list(give), waits)
        got = [over_dp(value, way) for value, (_, way) in zip(sent, groups)]
        rest = sent[len(here) :]
        moved = [shifted(value, 1) for value in rest[: len(moving)]]
        return sent[0], got, moved, [swapped(value) for value in rest[len(moving) :]]

    down_parts = [down_part(starts[0], [])]
    moving = [add_round(mixed_parts, mixed_given, 1)] if by_ring else []
    token, got, moving, _ = send_round(down_parts[0], moving, [])
    down_got = [got]
    back_half, back_low = run_back(
        (down_index, live), y_chunks, slope, down_weight, low_out, [token], width, size
    )
    if len(starts) > 1:
        down_parts.append(down_part(starts[1], [back_half]))
    if by_ring:
        moving = [add_round(mixed_parts, mixed_given, 2, moving[0])]
        back_low = fence([back_low], down_got[0] + moving + [down_parts[-1][0][0]])[0]
        half = tok_total // 2
        chip_sum = back_low[:half] + swapped(back_low[half:])
        _, back_low = sum_rows([chip_sum[n * rows : (n + 1) * rows] for n in range(chips)])
    else:
        back_low = sum_whole(back_low)
    if len(starts) > 1:
        give = mixed_parts[chips : chips + 1] if by_ring else []
        token, got, moving, given = send_round(
            down_parts[1], moving, down_got[0] + [back_low], give
        )
        down_got.append(got)

    up_parts, waits = [], [token]
    for start in starts:
        up_parts.append(up_part(start, waits))
        waits = [up_parts[-1][0][0]]
    if by_ring:
        mixed_given[0] = given[0]
        moving = [add_round(mixed_parts, mixed_given, 3, moving[0])]
        waits = waits + given
    token, got, moving, _ = send_round(up_parts[0], moving, down_got[-1] + waits)
    up_got = [got]
    input_parts = list(
        run_spread(
            (up_index, rank.reshape(1)),
            back_half, up_weight, back_low, low_in, [token], out_shapes, width, size,
        )
    )
    low_in_part = run_side(columns, back_low, size)
    down_onward = pass_on(down_parts, down_got)
    waits, give = up_got[0] + down_onward + [low_in_part], []
    if by_ring:
        mixed = add_round(mixed_parts, mixed_given, chips, moving[0])
        waits, give = waits + [mixed], input_parts[chips + 1 : chips + 3]
    else:
        mixed, input_grad = scatter_whole(mixed_parts), scatter_whole(input_parts)
    if len(starts) > 1:
        token, got, _, given = send_round(up_parts[1], [], waits, give)
        up_got.append(got)
    if by_ring:
        input_given = [None] + given
        moving = [shifted(add_round(input_parts, input_given, 1), 1)]
        moving = [add_round(input_parts, input_given, 2, moving[0])]

    def last_round(onward, moving, waits, give=()):
        sent = fence(onward + moving + list(give), waits)
        last = [over_dp(value, 3 - way) for value, (_, way) in zip(sent, groups)]
        rest = sent[len(groups) :]
        moved = [shifted(value, 1) for value in rest[: len(moving)]]
        return last, moved, [swapped(value) for value in rest[len(moving) :]]

    def total(parts, gots, last):
        sums = []
        for half, (part, got) in enumerate(zip(parts, gots)):
            for n, (length, _) in enumerate(groups):
                second = last[n][half * length : (half + 1) * length]
                sums.append(part[n][0] + got[n][0].astype(F32) + second.astype(F32))
        return jnp.concatenate(sums, 0)

    give = [input_parts[chips + 3]] if by_ring else []
    down_last, moving, given = last_round(down_onward, moving, up_got[-1], give)
    if by_ring:
        input_given.append(given[0])
        moving = [add_round(input_parts, input_given, 3, moving[0])]
        give = [input_parts[chips]]
    up_last, moving, given = last_round(pass_on(up_parts, up_got), moving, down_last, give)
    if by_ring:
        input_given[0] = given[0]
        input_grad = add_round(input_parts, input_given, chips, moving[0])

    low_in_grad = lax.psum_scatter(
        low_in_part, "dp", scatter_dimension=1, tiled=True
    ).astype(F32)
    down_grad = total(down_parts, down_got, down_last)
    up_sum = total(up_parts, up_got, up_last)
    up_grad = up_sum[:, :up_slots]
    low_out_grad = jnp.transpose(up_sum[:, up_slots], (1, 0, 2)).reshape(-1, count * size)
    return (mixed, input_grad, up_grad, down_grad, low_out_grad, low_in_grad)


def solution(mesh):
    return jax.shard_map(
        functools.partial(local, mesh.shape["mp"], mesh.shape["dp"]),
        mesh=mesh,
        in_specs=(
            P(("dp", "mp"), None),
            P(),
            P(),
            P(),
            P("mp", None, None, None),
            P("mp", None),
            P(None, "mp"),
            P("mp", None, None, None),
            P(("dp", "mp"), None),
        ),
        out_specs=(
            P(("dp", "mp"), None),
            P(("dp", "mp"), None),
            P("mp", None, "dp", None),
            P("mp", None, "dp", None),
            P("dp", "mp"),
            P("mp", "dp"),
        ),
        check_vma=False,
    )
```

time: 1240 us -> 498 us (0.40)
  waiting for transfers between devices: 585 us -> 208 us
  local copies, waits for them, and re-layouts: 342 us -> 49.3 us
  Pallas kernels: 0 us -> 168 us
  matrix products: 131 us -> 2.13 us
  other arithmetic: 78.9 us -> 13.3 us
  blocking collectives: 62.6 us -> 0 us
  starting transfers between devices: 14.8 us -> 40 us
    all_to_all x3 -> x0, waiting for transfers between devices: 426 us -> none  [the longest x1 216 us: local(): lax.all_to_all(pieces.reshape(tok_total, 1, down_width), 'mp', split_axis...]
    ppermute x0 -> x56, waiting for transfers between devices: none -> 208 us  [the longest x24 200 us: shifted(): lax.ppermute(piece, 'mp', [(i, (i + 2 * by) % mp_size) for i in range(mp_...]
    pallas_call x0 -> x32, Pallas kernels: none -> 168 us  [the longest x4 49.2 us: run_gradients(): pl.pallas_call(functools.partial(kernel, len(chunks), len(waits), first,...]
    all_gather x2 -> x0, waiting for transfers between devices: 157 us -> none  [the longest x1 91.6 us: local(): dy_whole = lax.all_gather(cotangent, 'mp', axis=0, tiled=True)]
    dot_general x14 -> x4, matrix products: 131 us -> 2.13 us  [local(): jnp.dot(jnp.concatenate(both, 1), both_low, preferred_element_type=F32)]
    unnamed x30 -> x112, local copies, waits for them, and re-layouts: 165 us -> 38 us
    reshape x7 -> x3, local copies, waits for them, and re-layouts: 67.3 us -> 2.54 us  [the longest x1 1.28 us: local(): jnp.transpose(up_sum[:, up_slots], (1, 0, 2)).reshape(-1, count * size)]
    psum x2 -> x0, blocking collectives: 62.6 us -> none  [the longest x1 31.3 us: local(): back_low = lax.psum(low_back_part, 'mp').astype(jnp.bfloat16)]
  transfers between devices with their start and end apart: 9 -> 57, of which waited for: 4 -> 28; matrix products, arithmetic and copies ran while one was open for 33% -> 8% of each run, Pallas kernels for 0% -> 31%
where the time goes in v2:
time: 498 us; the launch traced here: 496 us
  waiting for transfers between devices  208 us (42%)
  Pallas kernels  168 us (34%)
  local copies, waits for them, and re-layouts  49.3 us (10%)
  starting transfers between devices  40 us (8%)
  between operations  14.6 us (3%)
  other arithmetic  13.3 us (3%)
    ppermute x24, waiting for transfers between devices, shifted(): lax.ppermute(piece, 'mp', [(i, (i + 2 * by) % mp_size) for i in range(mp_...  200 us
    pallas_call x4, Pallas kernels, run_gradients(): pl.pallas_call(functools.partial(kernel, len(chunks), len(waits), first,...  49.2 us
    unnamed x112, local copies, waits for them, and re-layouts  38 us
    pallas_call x8, Pallas kernels, run_add(): pl.pallas_call(add_kernel, out_shape=shape((rows, width), BF16), grid=(st...  31.5 us
    ppermute x24, starting transfers between devices, shifted(): lax.ppermute(piece, 'mp', [(i, (i + 2 * by) % mp_size) for i in range(mp_...  24.8 us
    pallas_call x1, Pallas kernels, run_hidden(): pl.pallas_call(functools.partial(hidden_kernel, len(chunks), len(waits),...  20 us
    pallas_call x1, Pallas kernels, run_spread(): pl.pallas_call(functools.partial(spread_kernel, len(out_shapes), len(wait...  17.8 us
    pallas_call x1, Pallas kernels, run_back(): pl.pallas_call(functools.partial(back_kernel, len(chunks), len(waits), pe...  17.4 us
  transfers between devices with their start and end apart: 57, of which 28 were waited for; matrix products, arithmetic and copies ran while one was open for 8% of the time, Pallas kernels for 31%

profile of v2, /device:TPU:0, one launch (start us, length us, event | category | flops | bytes accessed | tf_op | source)
XLA Modules:
  0.0 495.7 jit_solution(4237130782527516509)
XLA Ops:
  7.2 3.1 collective-permute-start.1
  10.3 28.3 %collective-permute-done.1.refs_1_ = bf16[48,12288]{1,0:T(8,128)(2,1)} collective-permute-done((bf16[48,12288]{1,0:T(8,128)(2,1)}, bf16[48,12288]{1,0:T(8,128)(2,1)}, u32[]{:S(2)}, u32[]{:S(2)}) %collective-permute-start.1) | collective-permute-done | bytes 1179680 | tf_op jit(solution)/shard_map/ppermute | solution.py:563
  41.3 26.5 %collective-permute-done.3.refs_2_ = bf16[48,12288]{1,0:T(8,128)(2,1)} collective-permute-done((bf16[48,12288]{1,0:T(8,128)(2,1)}, bf16[48,12288]{1,0:T(8,128)(2,1)}, u32[]{:S(2)}, u32[]{:S(2)}) %collective-permute-start.3) | collective-permute-done | bytes 1179680 | tf_op jit(solution)/shard_map/ppermute | solution.py:563
  69.3 3.9 collective-permute-start.2
  74.7 22.6 %collective-permute-done.5.refs_3_ = bf16[48,12288]{1,0:T(8,128)(2,1)} collective-permute-done((bf16[48,12288]{1,0:T(8,128)(2,1)}, bf16[48,12288]{1,0:T(8,128)(2,1)}, u32[]{:S(2)}, u32[]{:S(2)}) %collective-permute-start.5) | collective-permute-done | bytes 1179680 | tf_op jit(solution)/shard_map/ppermute | solution.py:563
  98.8 5.9 %collective-permute-done.6 = f32[48,256]{1,0:T(8,128)S(1)} collective-permute-done((f32[48,256]{1,0:T(8,128)S(1)}, f32[48,256]{1,0:T(8,128)S(1)}, u32[]{:S(2)}, u32[]{:S(2)}) %collective-permute-start.6) | collective-permute-done | bytes 49184 | tf_op jit(solution)/shard_map/ppermute | solution.py:563
  105.9 3.6 collective-permute-start.9
  109.5 1.8 collective-permute-done.7
  115.4 2.0 collective-permute-start.10
  119.4 1.3 constant_dynamic-update-slice_fusion.5
  120.8 1.4 constant_dynamic-update-slice_fusion.4
  122.1 1.3 constant_dynamic-update-slice_fusion.3
  123.5 1.5 constant_dynamic-update-slice_fusion.2.refs_8_
  125.0 20.0 %hidden.1 = (bf16[24,384,256]{2,1,0:T(8,128)(2,1)}, f32[24,384,256]{2,1,0:T(8,128)}) custom-call(s32[72]{0:T(128)} %reshape.41.up_ref, bf16[48,12288]{1,0:T(8,128)(2,1)} %refs_0_.12, bf16[48,12288]{1,0:T(8,128)(2,1)} %collective-permute-done.1.refs_1_, bf16[48,12288]{1,0:T(8,128)(2,1)} %collective-permute-done.3.refs_2_, ...), custom_call_target="tpu_custom_call" | custom-call | flops 1 | bytes 1 | tf_op jit(solution)/shard_map/hidden/pallas_call | solution.py:303
  148.2 1.6 dynamic-slice_dynamic-update-slice_fusion.3
  149.8 1.6 dynamic-slice_dynamic-update-slice_fusion.2
  151.4 1.6 dynamic-slice_dynamic-update-slice_fusion.1
  153.0 1.6 dynamic-slice_dynamic-update-slice_fusion.refs_7_.columns
  154.6 16.6 %pieces.1 = (bf16[48,12288]{1,0:T(8,128)(2,1)}, bf16[48,12288]{1,0:T(8,128)(2,1)}, bf16[48,12288]{1,0:T(8,128)(2,1)}, bf16[48,12288]{1,0:T(8,128)(2,1)}, bf16[48...) custom-call(s32[72]{0:T(128)} %reshape.40.down_ref, ...), custom_call_target="tpu_custom_call" | custom-call | flops 1 | bytes 1 | tf_op jit(solution)/shard_map/pieces/pallas_call | solution.py:331
  171.1 5.4 %collective-permute-done.17.refs_0_ = bf16[48,12288]{1,0:T(8,128)(2,1)S(1)} collective-permute-done((bf16[48,12288]{1,0:T(8,128)(2,1)}, bf16[48,12288]{1,0:T(8,128)(2,1)S(1)}, u32[]{:S(2)}, u32[]{:S(2)}) %collective-permute-start.17) | collective-permute-done | bytes 1179680 | tf_op jit(solution)/shard_map/ppermute | solution.py:563
  179.0 2.0 collective-permute-done.20.refs_1_
  181.0 27.3 %collective-permute-done.19.refs_0_ = bf16[48,12288]{1,0:T(8,128)(2,1)S(1)} collective-permute-done((bf16[48,12288]{1,0:T(8,128)(2,1)}, bf16[48,12288]{1,0:T(8,128)(2,1)S(1)}, u32[]{:S(2)}, u32[]{:S(2)}) %collective-permute-start.19) | collective-permute-done | bytes 1179680 | tf_op jit(solution)/shard_map/ppermute | solution.py:563
  211.4 3.7 add_rows.8.refs_2_
  216.1 11.8 %down_kernel.2 = (f32[6,3,64,256]{3,2,1,0:T(8,128)}, bf16[2,6,3,64,256]{4,3,2,1,0:T(8,128)(2,1)}, bf16[6,3,64,256]{3,2,1,0:T(8,128)(2,1)}, f32[6,3,64,256]{3,2,1...) custom-call(s32[72]{0:T(128)} %reshape.40.down_ref, s32[24]{0:T(128)} %dynamic_slice.50.live_ref, ...), custom_call_target="tpu_custom_call" | custom-call | flops 1 | bytes 1 | tf_op jit(solution)/shard_map/down_kernel/pallas_call | solution.py:403
  229.1 1.5 collective-permute-start.27
  230.6 17.4 %back.1 = (bf16[24,384,256]{2,1,0:T(8,128)(2,1)}, f32[384,256]{1,0:T(8,128)}) custom-call(s32[72]{0:T(128)} %reshape.40.down_ref, s32[24]{0:T(128)} %dynamic_slice.50.live_ref, bf16[48,12288]{1,0:T(8,128)(2,1)} %refs_0_.10, bf16[48,12288]{1,0:T(8,128)(2,1)} %get-tuple-element.83.refs_1_, bf16[48,12288]{1,0:T(8,128)(2,1)} %get-tuple-element.88.refs_2_, ...), custom_call_target="tpu_custom_call" | custom-call | flops 1 | bytes 1 | tf_op jit(solution)/shard_map/back/pallas_call | solution.py:356
  248.0 11.7 %down_kernel.3 = (f32[6,3,64,256]{3,2,1,0:T(8,128)}, bf16[2,6,3,64,256]{4,3,2,1,0:T(8,128)(2,1)}, bf16[6,3,64,256]{3,2,1,0:T(8,128)(2,1)}, f32[6,3,64,256]{3,2,1...) custom-call(s32[72]{0:T(128)} %reshape.40.down_ref, s32[24]{0:T(128)} %dynamic_slice.50.live_ref, ...), custom_call_target="tpu_custom_call" | custom-call | flops 1 | bytes 1 | tf_op jit(solution)/shard_map/down_kernel/pallas_call | solution.py:403
  260.7 4.0 add_rows.9.refs_3_.refs_2_
  267.2 1.4 collective-permute-done.28
  269.6 3.8 collective-permute-start.29
  274.0 1.5 collective-permute-done.29
  275.5 3.2 collective-permute-done.30
  279.4 2.3 collective-permute-start.33
  281.6 2.1 collective-permute-start.34
  283.7 1.3 collective-permute-done.32
  287.6 2.0 collective-permute-start.37
  291.1 12.9 %up_kernel.2 = (f32[6,4,64,256]{3,2,1,0:T(8,128)}, bf16[2,6,4,64,256]{4,3,2,1,0:T(8,128)(2,1)}, bf16[6,4,64,256]{3,2,1,0:T(8,128)(2,1)}, f32[6,4,64,256]{3,2,1,0...) custom-call(s32[72]{0:T(128)} %reshape.41.up_ref, s32[4]{0:T(128)} %iota_xor_fusion.quarter_ref, ...), custom_call_target="tpu_custom_call" | custom-call | flops 1 | bytes 1 | tf_op jit(solution)/shard_map/up_kernel/pallas_call | solution.py:403
  304.0 12.8 %up_kernel.3 = (f32[6,4,64,256]{3,2,1,0:T(8,128)}, bf16[2,6,4,64,256]{4,3,2,1,0:T(8,128)(2,1)}, bf16[6,4,64,256]{3,2,1,0:T(8,128)(2,1)}, f32[6,4,64,256]{3,2,1,0...) custom-call(s32[72]{0:T(128)} %reshape.41.up_ref, s32[4]{0:T(128)} %iota_xor_fusion.quarter_ref, ...), custom_call_target="tpu_custom_call" | custom-call | flops 1 | bytes 1 | tf_op jit(solution)/shard_map/up_kernel/pallas_call | solution.py:403
  318.0 4.0 add_rows.10.refs_2_
  325.3 2.8 low_in_part.1.refs_8_
  328.2 17.8 %spread.1 = (bf16[48,12288]{1,0:T(8,128)(2,1)}, bf16[48,12288]{1,0:T(8,128)(2,1)}, bf16[48,12288]{1,0:T(8,128)(2,1)}, bf16[48,12288]{1,0:T(8,128)(2,1)}, bf16[48...) custom-call(s32[72]{0:T(128)} %reshape.41.up_ref, ...), custom_call_target="tpu_custom_call" | custom-call | flops 1 | bytes 1 | tf_op jit(solution)/shard_map/spread/pallas_call | solution.py:430
  345.9 2.9 pass_on.5.refs_7_.refs_1_
  348.8 2.9 pass_on.4.refs_6_.refs_0_
  351.7 3.5 collective-permute-done.40.refs_2_
  355.2 4.0 add_rows.11.refs_9_
  364.9 3.7 add_rows.12
  368.6 30.1 %collective-permute-done.47.refs_2_ = bf16[48,12288]{1,0:T(8,128)(2,1)} collective-permute-done((bf16[48,12288]{1,0:T(8,128)(2,1)}, bf16[48,12288]{1,0:T(8,128)(2,1)}, u32[]{:S(2)}, u32[]{:S(2)}) %collective-permute-start.47) | collective-permute-done | bytes 1179680 | tf_op jit(solution)/shard_map/ppermute | solution.py:563
  398.7 4.0 add_rows.13.refs_2_
  404.5 1.6 collective-permute-start.50
  408.0 3.4 pass_on.7.refs_1_
  411.4 3.3 pass_on.6.refs_0_
  414.7 20.2 %collective-permute-done.49.refs_2_ = bf16[48,12288]{1,0:T(8,128)(2,1)} collective-permute-done((bf16[48,12288]{1,0:T(8,128)(2,1)}, bf16[48,12288]{1,0:T(8,128)(2,1)}, u32[]{:S(2)}, u32[]{:S(2)}) %collective-permute-start.49) | collective-permute-done | bytes 1179680 | tf_op jit(solution)/shard_map/ppermute | solution.py:563
  435.0 4.0 add_rows.14.refs_2_
  441.7 1.3 collective-permute-start.54
  444.6 1.9 copy.59
  446.4 1.9 copy.57
  448.4 2.3 fusion.7
  452.4 2.5 pad_maximum_fusion.1
  454.9 18.6 %collective-permute-done.53.refs_2_ = bf16[48,12288]{1,0:T(8,128)(2,1)} collective-permute-done((bf16[48,12288]{1,0:T(8,128)(2,1)}, bf16[48,12288]{1,0:T(8,128)(2,1)}, u32[]{:S(2)}, u32[]{:S(2)}) %collective-permute-start.53) | collective-permute-done | bytes 1179680 | tf_op jit(solution)/shard_map/ppermute | solution.py:563
  473.5 4.1 add_rows.15
  477.7 3.2 fusion.3
  481.9 2.3 fusion.2
  485.0 1.3 copy.60
  486.3 2.5 slice.110
  (225 shorter events, 56.8 us)
Async XLA Ops:
  7.2 437.4 %reduce-scatter.4.cloned.1.call-start = ((), (), s32[]{:S(2)}) async-start(), calls=%async_computation.1 | async-start | bytes 983040
  7.2 31.4 %collective-permute-start.1 = (bf16[48,12288]{1,0:T(8,128)(2,1)}, bf16[48,12288]{1,0:T(8,128)(2,1)}, u32[]{:S(2)}, u32[]{:S(2)}) collective-permute-start(bf16[48,12288]{1,0:T(8,128)(2,1)} %refs_0_.12), channel_id=1, source_target_pairs={{0,2},{1,3},{2,4},{3,5},{4,6},{5,7},{6,0},{7,1},{8,10},{9,11},{10,... | collective-permute-start | bytes 3538952 | tf_op jit(solution)/shard_map/ppermute | solution.py:563
  38.6 29.3 %collective-permute-start.3 = (bf16[48,12288]{1,0:T(8,128)(2,1)}, bf16[48,12288]{1,0:T(8,128)(2,1)}, u32[]{:S(2)}, u32[]{:S(2)}) collective-permute-start(bf16[48,12288]{1,0:T(8,128)(2,1)} %collective-permute-done.1.refs_1_), channel_id=1, source_target_pairs={{0,2},{1,3},{2,4},{3,5},{4,6},{5,7},{6,0},{7,1},{8,10},{9,11},{10,... | collective-permute-start | bytes 3538952 | tf_op jit(solution)/shard_map/ppermute | solution.py:563
  38.6 29.3 %collective-permute-start = (bf16[1536,256]{1,0:T(8,128)(2,1)}, bf16[1536,256]{1,0:T(8,128)(2,1)S(1)}, u32[]{:S(2)}, u32[]{:S(2)}) collective-permute-start(bf16[1536,256]{1,0:T(8,128)(2,1)} %refs_3_.1), channel_id=1, source_target_pairs={{0,1},{1,0},{2,3},{3,2},{4,5},{5,4},{6,7},{7,6},{8,9},{9,8},{10,11... | collective-permute-start | bytes 2359304 | tf_op jit(solution)/shard_map/ppermute | solution.py:560
  38.6 76.1 %collective-permute-start.11 = (bf16[48,12288]{1,0:T(8,128)(2,1)}, bf16[48,12288]{1,0:T(8,128)(2,1)}, u32[]{:S(2)}, u32[]{:S(2)}) collective-permute-start(bf16[48,12288]{1,0:T(8,128)(2,1)} %refs_0_.12), channel_id=1, source_target_pairs={{0,1},{1,0},{2,3},{3,2},{4,5},{5,4},{6,7},{7,6},{8,9},{9,8},{10,11... | collective-permute-start | bytes 3538952 | tf_op jit(solution)/shard_map/ppermute | solution.py:560
  67.9 29.4 %collective-permute-start.5 = (bf16[48,12288]{1,0:T(8,128)(2,1)}, bf16[48,12288]{1,0:T(8,128)(2,1)}, u32[]{:S(2)}, u32[]{:S(2)}) collective-permute-start(bf16[48,12288]{1,0:T(8,128)(2,1)} %collective-permute-done.3.refs_2_), channel_id=1, source_target_pairs={{0,2},{1,3},{2,4},{3,5},{4,6},{5,7},{6,0},{7,1},{8,10},{9,11},{10,... | collective-permute-start | bytes 3538952 | tf_op jit(solution)/shard_map/ppermute | solution.py:563
  69.3 29.5 %collective-permute-start.2 = (f32[48,256]{1,0:T(8,128)S(1)}, f32[48,256]{1,0:T(8,128)S(1)}, u32[]{:S(2)}, u32[]{:S(2)}) collective-permute-start(f32[48,256]{1,0:T(8,128)S(1)} %fusion.14), channel_id=1, source_target_pairs={{0,6},{1,7},{2,0},{3,1},{4,2},{5,3},{6,4},{7,5},{8,14},{9,15},{10,... | collective-permute-start | bytes 147464 | tf_op jit(solution)/shard_map/ppermute | solution.py:563
  74.6 24.2 %collective-permute-start.4 = (f32[48,256]{1,0:T(8,128)S(1)}, f32[48,256]{1,0:T(8,128)S(1)}, u32[]{:S(2)}, u32[]{:S(2)}) collective-permute-start(f32[48,256]{1,0:T(8,128)S(1)} %fusion.18), channel_id=1, source_target_pairs={{0,4},{1,5},{2,6},{3,7},{4,0},{5,1},{6,2},{7,3},{8,12},{9,13},{10,... | collective-permute-start | bytes 147464 | tf_op jit(solution)/shard_map/ppermute | solution.py:563
  98.3 7.4 %copy-start.25 = (bf16[384,1536]{1,0:T(8,128)(2,1)}, bf16[384,1536]{1,0:T(8,128)(2,1)S(1)}, u32[]{:S(2)}) copy-start(bf16[384,1536]{1,0:T(8,128)(2,1)S(1)} %get-tuple-element.172) | copy-start | bytes 3538948
  98.7 13.9 %copy-start.6 = (bf16[48,12288]{1,0:T(8,128)(2,1)S(1)}, bf16[48,12288]{1,0:T(8,128)(2,1)}, u32[]{:S(2)}) copy-start(bf16[48,12288]{1,0:T(8,128)(2,1)} %refs_0_.10) | copy-start | bytes 3538948
  98.7 6.0 %collective-permute-start.6 = (f32[48,256]{1,0:T(8,128)S(1)}, f32[48,256]{1,0:T(8,128)S(1)}, u32[]{:S(2)}, u32[]{:S(2)}) collective-permute-start(f32[48,256]{1,0:T(8,128)S(1)} %fusion.22), channel_id=1, source_target_pairs={{0,2},{1,3},{2,4},{3,5},{4,6},{5,7},{6,0},{7,1},{8,10},{9,11},{10,... | collective-permute-start | bytes 147464 | tf_op jit(solution)/shard_map/ppermute | solution.py:563
  105.7 5.6 %collective-permute-start.7 = (bf16[48,256]{1,0:T(8,128)(2,1)S(1)}, bf16[48,256]{1,0:T(8,128)(2,1)S(1)}, u32[]{:S(2)}, u32[]{:S(2)}) collective-permute-start(bf16[48,256]{1,0:T(8,128)(2,1)S(1)} %get-tuple-element.196), channel_id=1, source_target_pairs={{0,2},{1,3},{2,4},{3,5},{4,6},{5,7},{6,0},{7,1},{8,10},{9,11},{10,... | collective-permute-start | bytes 73736 | tf_op jit(solution)/shard_map/ppermute | solution.py:563
  105.7 5.6 %collective-permute-start.8 = (bf16[48,256]{1,0:T(8,128)(2,1)S(1)}, bf16[48,256]{1,0:T(8,128)(2,1)S(1)}, u32[]{:S(2)}, u32[]{:S(2)}) collective-permute-start(bf16[48,256]{1,0:T(8,128)(2,1)S(1)} %get-tuple-element.196), channel_id=1, source_target_pairs={{0,4},{1,5},{2,6},{3,7},{4,0},{5,1},{6,2},{7,3},{8,12},{9,13},{10,... | collective-permute-start | bytes 73736 | tf_op jit(solution)/shard_map/ppermute | solution.py:563
  105.9 6.0 %collective-permute-start.9 = (bf16[48,256]{1,0:T(8,128)(2,1)S(1)}, bf16[48,256]{1,0:T(8,128)(2,1)S(1)}, u32[]{:S(2)}, u32[]{:S(2)}) collective-permute-start(bf16[48,256]{1,0:T(8,128)(2,1)S(1)} %get-tuple-element.196), channel_id=1, source_target_pairs={{0,6},{1,7},{2,0},{3,1},{4,2},{5,3},{6,4},{7,5},{8,14},{9,15},{10,... | collective-permute-start | bytes 73736 | tf_op jit(solution)/shard_map/ppermute | solution.py:563
  112.6 2.2 collective-permute-start.15
  113.7 11.3 %collective-permute-start.12 = (bf16[48,12288]{1,0:T(8,128)(2,1)}, bf16[48,12288]{1,0:T(8,128)(2,1)}, u32[]{:S(2)}, u32[]{:S(2)}) collective-permute-start(bf16[48,12288]{1,0:T(8,128)(2,1)} %collective-permute-done.1.refs_1_), channel_id=1, source_target_pairs={{0,1},{1,0},{2,3},{3,2},{4,5},{5,4},{6,7},{7,6},{8,9},{9,8},{10,11... | collective-permute-start | bytes 3538952 | tf_op jit(solution)/shard_map/ppermute | solution.py:560
  114.2 10.8 %collective-permute-start.13 = (bf16[48,12288]{1,0:T(8,128)(2,1)}, bf16[48,12288]{1,0:T(8,128)(2,1)}, u32[]{:S(2)}, u32[]{:S(2)}) collective-permute-start(bf16[48,12288]{1,0:T(8,128)(2,1)} %collective-permute-done.3.refs_2_), channel_id=1, source_target_pairs={{0,1},{1,0},{2,3},{3,2},{4,5},{5,4},{6,7},{7,6},{8,9},{9,8},{10,11... | collective-permute-start | bytes 3538952 | tf_op jit(solution)/shard_map/ppermute | solution.py:560
  114.2 10.8 %collective-permute-start.14 = (bf16[48,12288]{1,0:T(8,128)(2,1)}, bf16[48,12288]{1,0:T(8,128)(2,1)}, u32[]{:S(2)}, u32[]{:S(2)}) collective-permute-start(bf16[48,12288]{1,0:T(8,128)(2,1)} %collective-permute-done.5.refs_3_), channel_id=1, source_target_pairs={{0,1},{1,0},{2,3},{3,2},{4,5},{5,4},{6,7},{7,6},{8,9},{9,8},{10,11... | collective-permute-start | bytes 3538952 | tf_op jit(solution)/shard_map/ppermute | solution.py:560
  114.7 30.4 %collective-permute-start.16 = (bf16[48,12288]{1,0:T(8,128)(2,1)S(1)}, bf16[48,12288]{1,0:T(8,128)(2,1)S(1)}, u32[]{:S(2)}, u32[]{:S(2)}) collective-permute-start(bf16[48,12288]{1,0:T(8,128)(2,1)S(1)} %copy-done.6), channel_id=1, source_target_pairs={{0,1},{1,0},{2,3},{3,2},{4,5},{5,4},{6,7},{7,6},{8,9},{9,8},{10,11... | collective-permute-start | bytes 3538952 | tf_op jit(solution)/shard_map/ppermute | solution.py:560
  115.4 30.3 %collective-permute-start.10 = (bf16[48,12288]{1,0:T(8,128)(2,1)}, bf16[48,12288]{1,0:T(8,128)(2,1)S(1)}, u32[]{:S(2)}, u32[]{:S(2)}) collective-permute-start(bf16[48,12288]{1,0:T(8,128)(2,1)} %fence.11), channel_id=1, source_target_pairs={{0,2},{1,3},{2,4},{3,5},{4,6},{5,7},{6,0},{7,1},{8,10},{9,11},{10,... | collective-permute-start | bytes 3538952 | tf_op jit(solution)/shard_map/ppermute | solution.py:563
  146.7 29.8 %collective-permute-start.17 = (bf16[48,12288]{1,0:T(8,128)(2,1)}, bf16[48,12288]{1,0:T(8,128)(2,1)S(1)}, u32[]{:S(2)}, u32[]{:S(2)}) collective-permute-start(bf16[48,12288]{1,0:T(8,128)(2,1)} %get-tuple-element.83.refs_1_), channel_id=1, source_target_pairs={{0,2},{1,3},{2,4},{3,5},{4,6},{5,7},{6,0},{7,1},{8,10},{9,11},{10,... | collective-permute-start | bytes 3538952 | tf_op jit(solution)/shard_map/ppermute | solution.py:563
  146.9 29.6 %collective-permute-start.18 = (bf16[48,12288]{1,0:T(8,128)(2,1)}, bf16[48,12288]{1,0:T(8,128)(2,1)S(1)}, u32[]{:S(2)}, u32[]{:S(2)}) collective-permute-start(bf16[48,12288]{1,0:T(8,128)(2,1)} %get-tuple-element.83.refs_1_), channel_id=1, source_target_pairs={{0,1},{1,0},{2,3},{3,2},{4,5},{5,4},{6,7},{7,6},{8,9},{9,8},{10,11... | collective-permute-start | bytes 3538952 | tf_op jit(solution)/shard_map/ppermute | solution.py:560
  178.0 3.1 collective-permute-start.20
  178.0 30.4 %collective-permute-start.19 = (bf16[48,12288]{1,0:T(8,128)(2,1)}, bf16[48,12288]{1,0:T(8,128)(2,1)S(1)}, u32[]{:S(2)}, u32[]{:S(2)}) collective-permute-start(bf16[48,12288]{1,0:T(8,128)(2,1)} %get-tuple-element.88.refs_2_), channel_id=1, source_target_pairs={{0,2},{1,3},{2,4},{3,5},{4,6},{5,7},{6,0},{7,1},{8,10},{9,11},{10,... | collective-permute-start | bytes 3538952 | tf_op jit(solution)/shard_map/ppermute | solution.py:563
  178.0 30.4 %collective-permute-start.21 = (bf16[48,12288]{1,0:T(8,128)(2,1)}, bf16[48,12288]{1,0:T(8,128)(2,1)S(1)}, u32[]{:S(2)}, u32[]{:S(2)}) collective-permute-start(bf16[48,12288]{1,0:T(8,128)(2,1)} %get-tuple-element.90), channel_id=1, source_target_pairs={{0,1},{1,0},{2,3},{3,2},{4,5},{5,4},{6,7},{7,6},{8,9},{9,8},{10,11... | collective-permute-start | bytes 3538952 | tf_op jit(solution)/shard_map/ppermute | solution.py:560
  178.5 30.9 %collective-permute-start.22 = (bf16[48,12288]{1,0:T(8,128)(2,1)}, bf16[48,12288]{1,0:T(8,128)(2,1)}, u32[]{:S(2)}, u32[]{:S(2)}) collective-permute-start(bf16[48,12288]{1,0:T(8,128)(2,1)} %get-tuple-element.91), channel_id=1, source_target_pairs={{0,1},{1,0},{2,3},{3,2},{4,5},{5,4},{6,7},{7,6},{8,9},{9,8},{10,11... | collective-permute-start | bytes 3538952 | tf_op jit(solution)/shard_map/ppermute | solution.py:560
  178.5 30.9 %collective-permute-start.23 = (bf16[48,12288]{1,0:T(8,128)(2,1)}, bf16[48,12288]{1,0:T(8,128)(2,1)S(1)}, u32[]{:S(2)}, u32[]{:S(2)}) collective-permute-start(bf16[48,12288]{1,0:T(8,128)(2,1)} %get-tuple-element.88.refs_2_), channel_id=1, source_target_pairs={{0,1},{1,0},{2,3},{3,2},{4,5},{5,4},{6,7},{7,6},{8,9},{9,8},{10,11... | collective-permute-start | bytes 3538952 | tf_op jit(solution)/shard_map/ppermute | solution.py:560
  181.0 28.4 %copy-start.26 = (bf16[48,12288]{1,0:T(8,128)(2,1)}, bf16[48,12288]{1,0:T(8,128)(2,1)S(1)}, u32[]{:S(2)}) copy-start(bf16[48,12288]{1,0:T(8,128)(2,1)S(1)} %collective-permute-done.20.refs_1_) | copy-start | bytes 3538948
  210.8 4.2 collective-permute-start.24
  227.9 31.9 %collective-permute-start.25 = (bf16[48,12288]{1,0:T(8,128)(2,1)}, bf16[48,12288]{1,0:T(8,128)(2,1)S(1)}, u32[]{:S(2)}, u32[]{:S(2)}) collective-permute-start(bf16[48,12288]{1,0:T(8,128)(2,1)} %get-tuple-element.100), channel_id=1, source_target_pairs={{0,2},{1,3},{2,4},{3,5},{4,6},{5,7},{6,0},{7,1},{8,10},{9,11},{10,... | collective-permute-start | bytes 3538952 | tf_op jit(solution)/shard_map/ppermute | solution.py:563
  227.9 36.8 %collective-permute-start.26 = (bf16[2,6,3,64,256]{4,3,2,1,0:T(8,128)(2,1)}, bf16[2,6,3,64,256]{4,3,2,1,0:T(8,128)(2,1)S(1)}, u32[]{:S(2)}, u32[]{:S(2)}) collective-permute-start(bf16[2,6,3,64,256]{4,3,2,1,0:T(8,128)(2,1)} %get-tuple-element.95.refs_11_), channel_id=1, source_target_pairs={{0,16},{8,24},{16,0},{24,8},{1,17},{9,25},{17,1},{25,9},{2,18},{10... | collective-permute-start | bytes 3538952 | tf_op jit(solution)/shard_map/ppermute | solution.py:573
  229.1 35.7 %collective-permute-start.27 = (bf16[2,6,3,64,256]{4,3,2,1,0:T(8,128)(2,1)}, bf16[2,6,3,64,256]{4,3,2,1,0:T(8,128)(2,1)S(1)}, u32[]{:S(2)}, u32[]{:S(2)}) collective-permute-start(bf16[2,6,3,64,256]{4,3,2,1,0:T(8,128)(2,1)} %get-tuple-element.102), channel_id=1, source_target_pairs={{0,8},{8,0},{16,24},{24,16},{1,9},{9,1},{17,25},{25,17},{2,10},{10... | collective-permute-start | bytes 3538952 | tf_op jit(solution)/shard_map/ppermute | solution.py:573
  267.1 1.5 collective-permute-start.28
  269.6 5.9 %collective-permute-start.29 = (f32[48,256]{1,0:T(8,128)S(1)}, f32[48,256]{1,0:T(8,128)S(1)}, u32[]{:S(2)}, u32[]{:S(2)}) collective-permute-start(f32[48,256]{1,0:T(8,128)S(1)} %get-tuple-element.192), channel_id=1, source_target_pairs={{0,6},{1,7},{2,0},{3,1},{4,2},{5,3},{6,4},{7,5},{8,14},{9,15},{10,... | collective-permute-start | bytes 147464 | tf_op jit(solution)/shard_map/ppermute | solution.py:563
  273.4 5.3 %collective-permute-start.30 = (f32[48,256]{1,0:T(8,128)S(1)}, f32[48,256]{1,0:T(8,128)S(1)}, u32[]{:S(2)}, u32[]{:S(2)}) collective-permute-start(f32[48,256]{1,0:T(8,128)S(1)} %get-tuple-element.194), channel_id=1, source_target_pairs={{0,4},{1,5},{2,6},{3,7},{4,0},{5,1},{6,2},{7,3},{8,12},{9,13},{10,... | collective-permute-start | bytes 147464 | tf_op jit(solution)/shard_map/ppermute | solution.py:563
  273.4 5.9 %collective-permute-start.31 = (f32[48,256]{1,0:T(8,128)S(1)}, f32[48,256]{1,0:T(8,128)S(1)}, u32[]{:S(2)}, u32[]{:S(2)}) collective-permute-start(f32[48,256]{1,0:T(8,128)S(1)} %get-tuple-element.193), channel_id=1, source_target_pairs={{0,2},{1,3},{2,4},{3,5},{4,6},{5,7},{6,0},{7,1},{8,10},{9,11},{10,... | collective-permute-start | bytes 147464 | tf_op jit(solution)/shard_map/ppermute | solution.py:563
  279.3 5.7 %collective-permute-start.32 = (bf16[48,256]{1,0:T(8,128)(2,1)S(1)}, bf16[48,256]{1,0:T(8,128)(2,1)S(1)}, u32[]{:S(2)}, u32[]{:S(2)}) collective-permute-start(bf16[48,256]{1,0:T(8,128)(2,1)S(1)} %get-tuple-element.171), channel_id=1, source_target_pairs={{0,2},{1,3},{2,4},{3,5},{4,6},{5,7},{6,0},{7,1},{8,10},{9,11},{10,... | collective-permute-start | bytes 73736 | tf_op jit(solution)/shard_map/ppermute | solution.py:563
  279.4 5.6 %collective-permute-start.33 = (bf16[48,256]{1,0:T(8,128)(2,1)S(1)}, bf16[48,256]{1,0:T(8,128)(2,1)S(1)}, u32[]{:S(2)}, u32[]{:S(2)}) collective-permute-start(bf16[48,256]{1,0:T(8,128)(2,1)S(1)} %get-tuple-element.171), channel_id=1, source_target_pairs={{0,4},{1,5},{2,6},{3,7},{4,0},{5,1},{6,2},{7,3},{8,12},{9,13},{10,... | collective-permute-start | bytes 73736 | tf_op jit(solution)/shard_map/ppermute | solution.py:563
  281.6 3.9 collective-permute-start.34
  285.6 1.4 collective-permute-start.35
  287.6 30.4 %collective-permute-start.37 = (bf16[48,12288]{1,0:T(8,128)(2,1)}, bf16[48,12288]{1,0:T(8,128)(2,1)}, u32[]{:S(2)}, u32[]{:S(2)}) collective-permute-start(bf16[48,12288]{1,0:T(8,128)(2,1)} %get-tuple-element.110), channel_id=1, source_target_pairs={{0,2},{1,3},{2,4},{3,5},{4,6},{5,7},{6,0},{7,1},{8,10},{9,11},{10,... | collective-permute-start | bytes 3538952 | tf_op jit(solution)/shard_map/ppermute | solution.py:563
  289.6 32.3 %collective-permute-start.39 = (bf16[2,6,3,64,256]{4,3,2,1,0:T(8,128)(2,1)}, bf16[2,6,3,64,256]{4,3,2,1,0:T(8,128)(2,1)S(1)}, u32[]{:S(2)}, u32[]{:S(2)}) collective-permute-start(bf16[2,6,3,64,256]{4,3,2,1,0:T(8,128)(2,1)} %get-tuple-element.111), channel_id=1, source_target_pairs={{0,8},{8,0},{16,24},{24,16},{1,9},{9,1},{17,25},{25,17},{2,10},{10... | collective-permute-start | bytes 3538952 | tf_op jit(solution)/shard_map/ppermute | solution.py:573
  290.2 31.8 %collective-permute-start.38 = (bf16[2,6,3,64,256]{4,3,2,1,0:T(8,128)(2,1)}, bf16[2,6,3,64,256]{4,3,2,1,0:T(8,128)(2,1)S(1)}, u32[]{:S(2)}, u32[]{:S(2)}) collective-permute-start(bf16[2,6,3,64,256]{4,3,2,1,0:T(8,128)(2,1)} %get-tuple-element.106.refs_10_), channel_id=1, source_target_pairs={{0,16},{8,24},{16,0},{24,8},{1,17},{9,25},{17,1},{25,9},{2,18},{10... | collective-permute-start | bytes 3538952 | tf_op jit(solution)/shard_map/ppermute | solution.py:573
  291.1 30.9 %collective-permute-start.36 = (bf16[48,12288]{1,0:T(8,128)(2,1)}, bf16[48,12288]{1,0:T(8,128)(2,1)S(1)}, u32[]{:S(2)}, u32[]{:S(2)}) collective-permute-start(bf16[48,12288]{1,0:T(8,128)(2,1)} %get-tuple-element.105), channel_id=1, source_target_pairs={{0,1},{1,0},{2,3},{3,2},{4,5},{5,4},{6,7},{7,6},{8,9},{9,8},{10,11... | collective-permute-start | bytes 3538952 | tf_op jit(solution)/shard_map/ppermute | solution.py:560
  323.8 36.1 %collective-permute-start.41 = (bf16[2,6,4,64,256]{4,3,2,1,0:T(8,128)(2,1)}, bf16[2,6,4,64,256]{4,3,2,1,0:T(8,128)(2,1)S(1)}, u32[]{:S(2)}, u32[]{:S(2)}) collective-permute-start(bf16[2,6,4,64,256]{4,3,2,1,0:T(8,128)(2,1)} %get-tuple-element.115.refs_4_), channel_id=1, source_target_pairs={{0,16},{8,24},{16,0},{24,8},{1,17},{9,25},{17,1},{25,9},{2,18},{10... | collective-permute-start | bytes 4718600 | tf_op jit(solution)/shard_map/ppermute | solution.py:573
  324.3 36.2 %collective-permute-start.42 = (bf16[2,6,4,64,256]{4,3,2,1,0:T(8,128)(2,1)}, bf16[2,6,4,64,256]{4,3,2,1,0:T(8,128)(2,1)S(1)}, u32[]{:S(2)}, u32[]{:S(2)}) collective-permute-start(bf16[2,6,4,64,256]{4,3,2,1,0:T(8,128)(2,1)} %get-tuple-element.123), channel_id=1, source_target_pairs={{0,8},{8,0},{16,24},{24,16},{1,9},{9,1},{17,25},{25,17},{2,10},{10... | collective-permute-start | bytes 4718600 | tf_op jit(solution)/shard_map/ppermute | solution.py:573
  325.3 29.9 %collective-permute-start.40 = (bf16[48,12288]{1,0:T(8,128)(2,1)}, bf16[48,12288]{1,0:T(8,128)(2,1)}, u32[]{:S(2)}, u32[]{:S(2)}) collective-permute-start(bf16[48,12288]{1,0:T(8,128)(2,1)} %get-tuple-element.114), channel_id=1, source_target_pairs={{0,2},{1,3},{2,4},{3,5},{4,6},{5,7},{6,0},{7,1},{8,10},{9,11},{10,... | collective-permute-start | bytes 3538952 | tf_op jit(solution)/shard_map/ppermute | solution.py:563
  361.7 3.2 collective-permute-start.46
  361.7 41.0 %collective-permute-start.43 = (bf16[2,6,4,64,256]{4,3,2,1,0:T(8,128)(2,1)}, bf16[2,6,4,64,256]{4,3,2,1,0:T(8,128)(2,1)S(1)}, u32[]{:S(2)}, u32[]{:S(2)}) collective-permute-start(bf16[2,6,4,64,256]{4,3,2,1,0:T(8,128)(2,1)} %get-tuple-element.128), channel_id=1, source_target_pairs={{0,16},{8,24},{16,0},{24,8},{1,17},{9,25},{17,1},{25,9},{2,18},{10... | collective-permute-start | bytes 4718600 | tf_op jit(solution)/shard_map/ppermute | solution.py:573
  362.8 39.9 %collective-permute-start.44 = (bf16[2,6,4,64,256]{4,3,2,1,0:T(8,128)(2,1)}, bf16[2,6,4,64,256]{4,3,2,1,0:T(8,128)(2,1)S(1)}, u32[]{:S(2)}, u32[]{:S(2)}) collective-permute-start(bf16[2,6,4,64,256]{4,3,2,1,0:T(8,128)(2,1)} %get-tuple-element.131), channel_id=1, source_target_pairs={{0,8},{8,0},{16,24},{24,16},{1,9},{9,1},{17,25},{25,17},{2,10},{10... | collective-permute-start | bytes 4718600 | tf_op jit(solution)/shard_map/ppermute | solution.py:573
  364.0 4.6 collective-permute-start.45
  368.6 30.1 %collective-permute-start.47 = (bf16[48,12288]{1,0:T(8,128)(2,1)}, bf16[48,12288]{1,0:T(8,128)(2,1)}, u32[]{:S(2)}, u32[]{:S(2)}) collective-permute-start(bf16[48,12288]{1,0:T(8,128)(2,1)} %add_rows.12), channel_id=1, source_target_pairs={{0,2},{1,3},{2,4},{3,5},{4,6},{5,7},{6,0},{7,1},{8,10},{9,11},{10,... | collective-permute-start | bytes 3538952 | tf_op jit(solution)/shard_map/ppermute | solution.py:563
  404.5 10.3 %collective-permute-start.48 = (bf16[48,12288]{1,0:T(8,128)(2,1)}, bf16[48,12288]{1,0:T(8,128)(2,1)}, u32[]{:S(2)}, u32[]{:S(2)}) collective-permute-start(bf16[48,12288]{1,0:T(8,128)(2,1)} %get-tuple-element.138), channel_id=1, source_target_pairs={{0,1},{1,0},{2,3},{3,2},{4,5},{5,4},{6,7},{7,6},{8,9},{9,8},{10,11... | collective-permute-start | bytes 3538952 | tf_op jit(solution)/shard_map/ppermute | solution.py:560
  404.5 30.5 %collective-permute-start.49 = (bf16[48,12288]{1,0:T(8,128)(2,1)}, bf16[48,12288]{1,0:T(8,128)(2,1)}, u32[]{:S(2)}, u32[]{:S(2)}) collective-permute-start(bf16[48,12288]{1,0:T(8,128)(2,1)} %get-tuple-element.139), channel_id=1, source_target_pairs={{0,2},{1,3},{2,4},{3,5},{4,6},{5,7},{6,0},{7,1},{8,10},{9,11},{10,... | collective-permute-start | bytes 3538952 | tf_op jit(solution)/shard_map/ppermute | solution.py:563
  404.5 34.9 %collective-permute-start.50 = (bf16[12,3,64,256]{3,2,1,0:T(8,128)(2,1)}, bf16[12,3,64,256]{3,2,1,0:T(8,128)(2,1)S(1)}, u32[]{:S(2)}, u32[]{:S(2)}) collective-permute-start(bf16[12,3,64,256]{3,2,1,0:T(8,128)(2,1)} %get-tuple-element.141), channel_id=1, source_target_pairs={{0,8},{8,0},{16,24},{24,16},{1,9},{9,1},{17,25},{25,17},{2,10},{10... | collective-permute-start | bytes 3538952 | tf_op jit(solution)/shard_map/ppermute | solution.py:573
  406.0 34.6 %collective-permute-start.51 = (bf16[12,3,64,256]{3,2,1,0:T(8,128)(2,1)}, bf16[12,3,64,256]{3,2,1,0:T(8,128)(2,1)S(1)}, u32[]{:S(2)}, u32[]{:S(2)}) collective-permute-start(bf16[12,3,64,256]{3,2,1,0:T(8,128)(2,1)} %get-tuple-element.142), channel_id=1, source_target_pairs={{0,16},{8,24},{16,0},{24,8},{1,17},{9,25},{17,1},{25,9},{2,18},{10... | collective-permute-start | bytes 3538952 | tf_op jit(solution)/shard_map/ppermute | solution.py:573
  441.7 6.7 %copy-start.23 = (bf16[2,6,3,64,256]{4,3,2,1,0:T(8,128)(2,1)S(1)}, bf16[2,6,3,64,256]{4,3,2,1,0:T(8,128)(2,1)}, u32[]{:S(2)}) copy-start(bf16[2,6,3,64,256]{4,3,2,1,0:T(8,128)(2,1)} %copy-done.22) | copy-start | bytes 3538948
  441.7 6.7 %copy-start.29 = (f32[6,3,64,256]{3,2,1,0:T(8,128)S(1)}, f32[6,3,64,256]{3,2,1,0:T(8,128)}, u32[]{:S(2)}) copy-start(f32[6,3,64,256]{3,2,1,0:T(8,128)} %get-tuple-element.104.refs_4_) | copy-start | bytes 3538948
  441.7 6.7 %copy-start.10 = (bf16[2,6,3,64,256]{4,3,2,1,0:T(8,128)(2,1)S(1)}, bf16[2,6,3,64,256]{4,3,2,1,0:T(8,128)(2,1)}, u32[]{:S(2)}) copy-start(bf16[2,6,3,64,256]{4,3,2,1,0:T(8,128)(2,1)} %copy-done.9) | copy-start | bytes 3538948
  441.7 36.1 %collective-permute-start.54 = (bf16[12,4,64,256]{3,2,1,0:T(8,128)(2,1)}, bf16[12,4,64,256]{3,2,1,0:T(8,128)(2,1)}, u32[]{:S(2)}, u32[]{:S(2)}) collective-permute-start(bf16[12,4,64,256]{3,2,1,0:T(8,128)(2,1)} %get-tuple-element.145), channel_id=1, source_target_pairs={{0,8},{8,0},{16,24},{24,16},{1,9},{9,1},{17,25},{25,17},{2,10},{10... | collective-permute-start | bytes 4718600 | tf_op jit(solution)/shard_map/ppermute | solution.py:573
  443.0 11.9 %collective-permute-start.52 = (bf16[48,12288]{1,0:T(8,128)(2,1)}, bf16[48,12288]{1,0:T(8,128)(2,1)}, u32[]{:S(2)}, u32[]{:S(2)}) collective-permute-start(bf16[48,12288]{1,0:T(8,128)(2,1)} %get-tuple-element.143), channel_id=1, source_target_pairs={{0,1},{1,0},{2,3},{3,2},{4,5},{5,4},{6,7},{7,6},{8,9},{9,8},{10,11... | collective-permute-start | bytes 3538952 | tf_op jit(solution)/shard_map/ppermute | solution.py:560
  443.0 30.5 %collective-permute-start.53 = (bf16[48,12288]{1,0:T(8,128)(2,1)}, bf16[48,12288]{1,0:T(8,128)(2,1)}, u32[]{:S(2)}, u32[]{:S(2)}) collective-permute-start(bf16[48,12288]{1,0:T(8,128)(2,1)} %get-tuple-element.144), channel_id=1, source_target_pairs={{0,2},{1,3},{2,4},{3,5},{4,6},{5,7},{6,0},{7,1},{8,10},{9,11},{10,... | collective-permute-start | bytes 3538952 | tf_op jit(solution)/shard_map/ppermute | solution.py:563
  443.8 37.2 %collective-permute-start.55 = (bf16[12,4,64,256]{3,2,1,0:T(8,128)(2,1)}, bf16[12,4,64,256]{3,2,1,0:T(8,128)(2,1)}, u32[]{:S(2)}, u32[]{:S(2)}) collective-permute-start(bf16[12,4,64,256]{3,2,1,0:T(8,128)(2,1)} %get-tuple-element.147), channel_id=1, source_target_pairs={{0,16},{8,24},{16,0},{24,8},{1,17},{9,25},{17,1},{25,9},{2,18},{10... | collective-permute-start | bytes 4718600 | tf_op jit(solution)/shard_map/ppermute | solution.py:573
  473.5 4.3 copy-start.19
  (40 other events, 72.0 us)
Sparse Core Ops, SparseCore 0:
  408.1 31.1 reduce-scatter.3

commit v3 on v2

--- a/solution.py
+++ b/solution.py
@@ -492,7 +492,7 @@
 
 def run_add(arrays):
     rows, width = arrays[0].shape
-    steps = 4 if width % 512 == 0 else 1
+    steps = 2 if width % 256 == 0 else 1
     spec = pl.BlockSpec((rows, width // steps), lambda i: (0, i))
     return pl.pallas_call(
         add_kernel,
@@ -506,21 +506,133 @@
     )(*arrays)
 
 
-def side_kernel(columns, back_low, out):
-    out[...] = dot_tn(columns[...], back_low[...]).astype(BF16)
-
-
-def run_side(columns, back_low, size):
+def low_kernel(chunk_count, place_ref, *refs):
+    chunks, out = refs[: 2 * chunk_count], refs[-1]
+    weight, other_weight = refs[2 * chunk_count : 2 * chunk_count + 2]
+    own = jnp.concatenate([chunk[...] for chunk in chunks[:chunk_count]], axis=0)
+    other = jnp.concatenate([chunk[...] for chunk in chunks[chunk_count:]], axis=0)
+    out[...] = dot_nn(own, weight[...]) + dot_nn(other, other_weight[...])
+
+
+def run_low(places, chunks, weight, other_weight, waits):
+    rows, columns = chunks[0].shape[0], weight.shape[0]
+    out = shape((len(chunks) * rows, weight.shape[1]), F32)
+    return pl.pallas_call(
+        functools.partial(low_kernel, len(chunks)),
+        out_shape=out,
+        grid_spec=pltpu.PrefetchScalarGridSpec(
+            num_scalar_prefetch=1,
+            grid=(1,),
+            in_specs=[pl.BlockSpec((rows, columns), lambda i, at: (0, at[0]))] * len(chunks)
+            + [pl.BlockSpec((rows, columns), lambda i, at: (0, at[1]))] * len(chunks)
+            + [whole_spec(weight), whole_spec(other_weight)]
+            + [any_spec()] * len(waits),
+            out_specs=whole_spec(out),
+        ),
+        compiler_params=params(),
+        cost_estimate=COST,
+        name="low_part",
+    )(places, *chunks, *chunks, weight, other_weight, *waits)
+
+
+def side_kernel(place_ref, *refs):
+    back_low, out = refs[-2:]
+    columns = jnp.concatenate([chunk[...] for chunk in refs[:-2]], axis=0)
+    out[...] = dot_tn(columns, back_low[...]).astype(BF16)
+
+
+def run_side(places, chunks, back_low, col_width):
+    rows = chunks[0].shape[0]
+    out = shape((col_width, back_low.shape[1]), BF16)
     return pl.pallas_call(
         side_kernel,
-        out_shape=shape((columns.shape[1], back_low.shape[1]), BF16),
+        out_shape=out,
+        grid_spec=pltpu.PrefetchScalarGridSpec(
+            num_scalar_prefetch=1,
+            grid=(1,),
+            in_specs=[pl.BlockSpec((rows, col_width), lambda i, at: (0, at[0]))] * len(chunks)
+            + [whole_spec(back_low)],
+            out_specs=whole_spec(out),
+        ),
+        compiler_params=params(),
+        cost_estimate=COST,
+        name="low_in_part",
+    )(places, *chunks, back_low)
+
+
+def sum_kernel(places, own_count, *refs):
+    out, first = refs[-1], 0
+    for number, (last, start) in enumerate(places):
+        own, got = refs[2 * number : 2 * number + 2]
+        length = own.shape[0]
+        total = own[...] + got[0].astype(F32)
+        if last is not None:
+            total = total + refs[2 * own_count + last][start : start + length].astype(F32)
+        out[first : first + length] = total
+        first += length
+
+
+def run_sum(parts, gots, lasts=()):
+    pairs = [
+        (own[0], got, number, half * own[0].shape[0])
+        for half, (part, gots_here) in enumerate(zip(parts, gots))
+        for number, (own, got) in enumerate(zip(part, gots_here))
+    ]
+    places = [(number, start) if lasts else (None, 0) for _, _, number, start in pairs]
+    specs, arrays = [], []
+    for own, got, _, _ in pairs:
+        specs += [
+            whole_spec(own),
+            pl.BlockSpec((1,) + got.shape[1:], lambda i: (0, 0, 0, 0, 0)),
+        ]
+        arrays += [own, got]
+    specs += [whole_spec(last) for last in lasts]
+    length = sum(own.shape[0] for own, _, _, _ in pairs)
+    out = shape((length,) + pairs[0][0].shape[1:], F32)
+    return pl.pallas_call(
+        functools.partial(sum_kernel, places, len(pairs)),
+        out_shape=out,
         grid=(1,),
-        in_specs=[whole_spec(columns), whole_spec(back_low)],
-        out_specs=pl.BlockSpec((columns.shape[1], back_low.shape[1]), lambda i: (0, 0)),
-        compiler_params=params(),
-        cost_estimate=COST,
-        name="low_in_part",
-    )(columns, back_low)
+        in_specs=specs,
+        out_specs=whole_spec(out),
+        compiler_params=params(),
+        cost_estimate=COST,
+        name="sums",
+    )(*arrays, *lasts)
+
+
+def finish_kernel(group_count, *refs):
+    before = refs[0]
+    lasts = refs[1 : 1 + group_count]
+    blocks, side = refs[1 + group_count :]
+    size = blocks.shape[3]
+    for number, last in enumerate(lasts):
+
+        @pl.when(pl.program_id(0) % group_count == number)
+        def _(last=last):
+            for block in range(blocks.shape[0]):
+                total = before[block] + last[block].astype(F32)
+                blocks[block] = total[:-1]
+                side[:, block * size : (block + 1) * size] = total[-1]
+
+
+def run_finish(before, lasts, group):
+    count, slots, rows, size = before.shape
+    part = (group, slots, rows, size)
+    return pl.pallas_call(
+        functools.partial(finish_kernel, len(lasts)),
+        out_shape=[shape((count, slots - 1, rows, size), F32), shape((rows, count * size), F32)],
+        grid=(count // group,),
+        in_specs=[pl.BlockSpec(part, lambda i: (i, 0, 0, 0))]
+        + [pl.BlockSpec(part, lambda i: (i // len(lasts), 0, 0, 0))] * len(lasts),
+        out_specs=[
+            pl.BlockSpec((group, slots - 1, rows, size), lambda i: (i, 0, 0, 0)),
+            pl.BlockSpec((rows, group * size), lambda i: (0, i)),
+        ],
+        compiler_params=params(),
+        cost_estimate=COST,
+        name="finish",
+    )(before, *lasts)
 
 
 def fence(values, waits):
@@ -578,12 +690,13 @@
             for n in range(len(groups))
         ]
 
-    def sum_rows(chip_sums):
-        low = chip_sums[0]
-        for back in range(1, chips):
-            low = low + shifted(chip_sums[back], -back)
-        low = low.astype(BF16)
-        same = jnp.concatenate([low] + [shifted(low, back) for back in range(1, chips)], 0)
+    def sum_rows(chip_sum):
+        sent = chip_sum.astype(BF16)
+        total = chip_sum
+        for by in range(1, chips):
+            got = shifted(sent, by)
+            total = total + jnp.roll(got, by * rows, axis=0).astype(F32)
+        same = total.astype(BF16)
         return same, jnp.concatenate([same, swapped(same)], 0)
 
     def sum_whole(partial):
@@ -594,25 +707,31 @@
         return lax.dynamic_slice_in_dim(piece, place * col_width, col_width, 1)
 
     if by_ring:
-        both_low = jnp.concatenate([low_in, swapped(low_in)], 0)
-        x_same, chip_sums = [tokens], []
+        places = jnp.stack([rank, rank ^ 1]).astype(jnp.int32)
+        other_low = swapped(low_in)
+        x_same, x_other = [tokens], []
+        y_same, y_other = [cotangent], [swapped(cotangent)]
         for step in range(chips):
-            both = [take_columns(x_same[step], rank), take_columns(x_same[step], rank ^ 1)]
-            chip_sums.append(
-                jnp.dot(jnp.concatenate(both, 1), both_low, preferred_element_type=F32)
-            )
             if step < chips - 1:
+                if step == 2:
+                    x_same[2] = fence(x_same[2:], x_other + y_other + [other_low])[0]
                 x_same.append(shifted(x_same[step], 1))
-        x_chunks = x_same + [swapped(piece) for piece in x_same]
-        low_same, low_half = sum_rows(chip_sums)
-        y_same, y_other = [cotangent], [swapped(cotangent)]
-        arriving = shifted(fence([cotangent], [low_same])[0], 1)
+                x_other.append(swapped(x_same[step]))
+        x_other.append(swapped(x_same[-1]))
+        x_chunks = x_same + x_other
+        low_same, low_half = sum_rows(
+            run_low(places, x_same, low_in, other_low, x_other[2:3])
+        )
+        arriving = shifted(cotangent, 1)
+        arrived = fence([arriving], [low_same])[0]
+        y_same.append(arrived)
+        y_other.append(swapped(arrived))
+        arriving = shifted(arrived, 1)
     else:
         x_chunks = [lax.all_gather(tokens, "mp", axis=0, tiled=True)]
         y_chunks = [lax.all_gather(cotangent, "mp", axis=0, tiled=True)]
         low = jnp.dot(take_columns(x_chunks[0], rank), low_in, preferred_element_type=F32)
         low_half = sum_whole(low)
-    columns = jnp.concatenate([take_columns(piece, rank) for piece in x_chunks], 0)
     hidden, slope = run_hidden((up_index,), x_chunks, low_half, up_weight, low_out, [], size)
     if by_ring:
         arrived, hidden = fence([arriving, hidden], y_other + [slope])
@@ -623,17 +742,11 @@
         run_pieces((down_index, live), hidden, down_weight, [], out_shapes, width, size)
     )
     if by_ring:
-        arrived, *mixed_parts[chips:] = fence(
-            [arriving] + mixed_parts[chips:], y_other + [columns]
-        )
-        y_same.append(arrived)
-        y_other.append(swapped(arrived))
-        arriving = shifted(arrived, 1)
-        mixed_given = [None] + [swapped(piece) for piece in mixed_parts[chips + 1 :]]
-        arrived = fence([arriving], mixed_given[1:] + y_other)[0]
+        arrived, *mixed_parts = fence([arriving] + mixed_parts, y_other)
         y_same.append(arrived)
         y_other.append(swapped(arrived))
         y_chunks = y_same + y_other
+        mixed_given = [None, swapped(mixed_parts[chips + 1])]
 
     down_slots = down_weight.shape[1]
     if count % 4 == 0:
@@ -663,8 +776,12 @@
         return sent[0], got, moved, [swapped(value) for value in rest[len(moving) :]]
 
     down_parts = [down_part(starts[0], [])]
-    moving = [add_round(mixed_parts, mixed_given, 1)] if by_ring else []
-    token, got, moving, _ = send_round(down_parts[0], moving, [])
+    give, moving = mixed_parts[chips + 2 :] if by_ring else [], []
+    token, got, _, given = send_round(
+        down_parts[0], [], [y_other[-1], mixed_given[1]] if by_ring else [], give
+    )
+    if by_ring:
+        moving = [shifted(add_round(mixed_parts, mixed_given, 1), 1)]
     down_got = [got]
     back_half, back_low = run_back(
         (down_index, live), y_chunks, slope, down_weight, low_out, [token], width, size
@@ -672,11 +789,12 @@
     if len(starts) > 1:
         down_parts.append(down_part(starts[1], [back_half]))
     if by_ring:
+        mixed_given += given
         moving = [add_round(mixed_parts, mixed_given, 2, moving[0])]
-        back_low = fence([back_low], down_got[0] + moving + [down_parts[-1][0][0]])[0]
+        waits = down_got[0] + moving + given + [down_parts[-1][0][0]]
+        back_low = fence([back_low], waits)[0]
         half = tok_total // 2
-        chip_sum = back_low[:half] + swapped(back_low[half:])
-        _, back_low = sum_rows([chip_sum[n * rows : (n + 1) * rows] for n in range(chips)])
+        _, back_low = sum_rows(back_low[:half] + swapped(back_low[half:]))
     else:
         back_low = sum_whole(back_low)
     if len(starts) > 1:
@@ -702,7 +820,13 @@
             back_half, up_weight, back_low, low_in, [token], out_shapes, width, size,
         )
     )
-    low_in_part = run_side(columns, back_low, size)
+    if by_ring:
+        low_in_part = run_side(places, x_chunks, back_low, col_width)
+    else:
+        low_in_part = lax.dot_general(
+            take_columns(x_chunks[0], rank), back_low, (((0,), (0,)), ((), ())),
+            preferred_element_type=F32,
+        ).astype(BF16)
     down_onward = pass_on(down_parts, down_got)
     waits, give = up_got[0] + down_onward + [low_in_part], []
     if by_ring:
@@ -725,14 +849,6 @@
         moved = [shifted(value, 1) for value in rest[: len(moving)]]
         return last, moved, [swapped(value) for value in rest[len(moving) :]]
 
-    def total(parts, gots, last):
-        sums = []
-        for half, (part, got) in enumerate(zip(parts, gots)):
-            for n, (length, _) in enumerate(groups):
-                second = last[n][half * length : (half + 1) * length]
-                sums.append(part[n][0] + got[n][0].astype(F32) + second.astype(F32))
-        return jnp.concatenate(sums, 0)
-
     give = [input_parts[chips + 3]] if by_ring else []
     down_last, moving, given = last_round(down_onward, moving, up_got[-1], give)
     if by_ring:
@@ -747,10 +863,10 @@
     low_in_grad = lax.psum_scatter(
         low_in_part, "dp", scatter_dimension=1, tiled=True
     ).astype(F32)
-    down_grad = total(down_parts, down_got, down_last)
-    up_sum = total(up_parts, up_got, up_last)
-    up_grad = up_sum[:, :up_slots]
-    low_out_grad = jnp.transpose(up_sum[:, up_slots], (1, 0, 2)).reshape(-1, count * size)
+    down_grad = run_sum(down_parts, down_got, down_last)
+    up_grad, low_out_grad = run_finish(
+        run_sum(up_parts, up_got), up_last, count // (len(starts) * len(groups))
+    )
     return (mixed, input_grad, up_grad, down_grad, low_out_grad, low_in_grad)
 
 

time: 498 us -> 477 us (0.958)
  local copies, waits for them, and re-layouts: 49.3 us -> 27.1 us
  starting transfers between devices: 40 us -> 22.6 us
  Pallas kernels: 168 us -> 184 us
  waiting for transfers between devices: 208 us -> 220 us
  other arithmetic: 13.3 us -> 7.15 us
    pallas_call x1 -> x5, Pallas kernels: 2.84 us -> 27.5 us  [the longest x2 13.4 us: run_sum(): pl.pallas_call(functools.partial(sum_kernel, places, len(pairs)), out_sha...]
    unnamed x112 -> x71, local copies, waits for them, and re-layouts: 38 us -> 22.7 us
    ppermute x24 -> x18, starting transfers between devices: 24.8 us -> 9.73 us  [shifted(): lax.ppermute(piece, 'mp', [(i, (i + 2 * by) % mp_size) for i in range(mp_...]
    add x5 -> x0, other arithmetic: 9.34 us -> none  [the longest x4 8.39 us: total(): sums.append(part[n][0] + got[n][0].astype(F32) + second.astype(F32))]
    pallas_call x8, Pallas kernels: 31.5 us -> 23 us  [run_add(): pl.pallas_call(add_kernel, out_shape=shape((rows, width), BF16), grid=(st...]
    ppermute x20, waiting for transfers between devices: 5.65 us -> 12.6 us  [swapped(): return lax.ppermute(piece, 'mp', swap)]
    ppermute x24 -> x18, waiting for transfers between devices: 200 us -> 200 us  [shifted(): lax.ppermute(piece, 'mp', [(i, (i + 2 * by) % mp_size) for i in range(mp_...]
  transfers between devices with their start and end apart: 57 -> 51, of which waited for: 28 -> 29; matrix products, arithmetic and copies ran while one was open for 8% -> 3% of each run, Pallas kernels for 31% -> 37%
where the time goes in v3:
time: 477 us; the launch traced here: 476 us
  waiting for transfers between devices  220 us (46%)
  Pallas kernels  184 us (39%)
  local copies, waits for them, and re-layouts  27.1 us (6%)
  starting transfers between devices  22.6 us (5%)
  between operations  14.4 us (3%)
  other arithmetic  7.15 us (1%)
    ppermute x18, waiting for transfers between devices, shifted(): lax.ppermute(piece, 'mp', [(i, (i + 2 * by) % mp_size) for i in range(mp_...  200 us
    pallas_call x4, Pallas kernels, run_gradients(): pl.pallas_call(functools.partial(kernel, len(chunks), len(waits), first,...  49.3 us
    pallas_call x8, Pallas kernels, run_add(): pl.pallas_call(add_kernel, out_shape=shape((rows, width), BF16), grid=(st...  23 us
    unnamed x71, local copies, waits for them, and re-layouts  22.7 us
    pallas_call x1, Pallas kernels, run_hidden(): pl.pallas_call(functools.partial(hidden_kernel, len(chunks), len(waits),...  20 us
    pallas_call x1, Pallas kernels, run_spread(): pl.pallas_call(functools.partial(spread_kernel, len(out_shapes), len(wait...  17.8 us
    pallas_call x1, Pallas kernels, run_back(): pl.pallas_call(functools.partial(back_kernel, len(chunks), len(waits), pe...  17.4 us
    pallas_call x1, Pallas kernels, run_pieces(): pl.pallas_call(functools.partial(pieces_kernel, len(out_shapes), len(wait...  16.6 us
  transfers between devices with their start and end apart: 51, of which 29 were waited for; matrix products, arithmetic and copies ran while one was open for 3% of the time, Pallas kernels for 37%

profile of v3, /device:TPU:0, one launch (start us, length us, event | category | flops | bytes accessed | tf_op | source)
XLA Modules:
  0.0 476.0 jit_solution(8098521341402444147)
XLA Ops:
  7.2 3.1 collective-permute-start.1
  10.8 27.7 %collective-permute-done.1.refs_1_.refs_5_ = bf16[48,12288]{1,0:T(8,128)(2,1)S(1)} collective-permute-done((bf16[48,12288]{1,0:T(8,128)(2,1)}, bf16[48,12288]{1,0:T(8,128)(2,1)S(1)}, u32[]{:S(2)}, u32[]{:S(2)}) %collective-permute-start.1) | collective-permute-done | bytes 1179680 | tf_op jit(solution)/shard_map/ppermute | solution.py:675
  39.0 3.7 collective-permute-done.6.refs_4_.refs_9_
  42.7 1.2 copy-done.27
  45.0 23.7 %collective-permute-done.2.refs_0_ = bf16[48,12288]{1,0:T(8,128)(2,1)S(1)} collective-permute-done((bf16[48,12288]{1,0:T(8,128)(2,1)S(1)}, bf16[48,12288]{1,0:T(8,128)(2,1)S(1)}, u32[]{:S(2)}, u32[]{:S(2)}) %collective-permute-start.2) | collective-permute-done | bytes 1179680 | tf_op jit(solution)/shard_map/ppermute | solution.py:675
  70.4 2.4 collective-permute-done.8.refs_10_.refs_6_
  72.8 27.7 %collective-permute-done.7.refs_3_.refs_7_ = bf16[48,12288]{1,0:T(8,128)(2,1)S(1)} collective-permute-done((bf16[48,12288]{1,0:T(8,128)(2,1)}, bf16[48,12288]{1,0:T(8,128)(2,1)S(1)}, u32[]{:S(2)}, u32[]{:S(2)}) %collective-permute-start.7) | collective-permute-done | bytes 1179680 | tf_op jit(solution)/shard_map/ppermute | solution.py:675
  100.5 1.1 copy-done.3
  101.6 3.7 low_part.1
  106.2 2.0 collective-permute-start.9
  108.3 21.3 %collective-permute-done.11 = bf16[192,256]{1,0:T(8,128)(2,1)S(1)} collective-permute-done((bf16[192,256]{1,0:T(8,128)(2,1)S(1)}, bf16[192,256]{1,0:T(8,128)(2,1)S(1)}, u32[]{:S(2)}, u32[]{:S(2)}) %collective-permute-start.11) | collective-permute-done | bytes 98336 | tf_op jit(solution)/shard_map/ppermute | solution.py:675
  130.2 3.6 collective-permute-done.10
  133.8 1.6 add_convert_fusion.1.refs_1_
  138.7 1.6 pad_maximum_fusion.refs_8_
  141.4 20.0 %hidden.1 = (bf16[24,384,256]{2,1,0:T(8,128)(2,1)}, f32[24,384,256]{2,1,0:T(8,128)}) custom-call(s32[72]{0:T(128)} %reshape.19.up_ref, bf16[48,12288]{1,0:T(8,128)(2,1)} %refs_0_.15, bf16[48,12288]{1,0:T(8,128)(2,1)} %copy-done.2, bf16[48,12288]{1,0:T(8,128)(2,1)} %fence.11.refs_2_.refs_6_, bf16[48,12288]{1,0:T(8,128)(2,1)} %copy-done.3, ...), custom_call_target="tpu_custom_call" | custom-call | flops 1 | bytes 1 | tf_op jit(solution)/shard_map/hidden/pallas_call | solution.py:303
  161.4 4.5 collective-permute-done.12.refs_0_
  168.9 16.6 %pieces.1 = (bf16[48,12288]{1,0:T(8,128)(2,1)}, bf16[48,12288]{1,0:T(8,128)(2,1)}, bf16[48,12288]{1,0:T(8,128)(2,1)}, bf16[48,12288]{1,0:T(8,128)(2,1)}, bf16[48...) custom-call(s32[72]{0:T(128)} %reshape.20.down_ref, ...), custom_call_target="tpu_custom_call" | custom-call | flops 1 | bytes 1 | tf_op jit(solution)/shard_map/pieces/pallas_call | solution.py:331
  185.5 11.8 %collective-permute-done.16.refs_0_ = bf16[48,12288]{1,0:T(8,128)(2,1)S(1)} collective-permute-done((bf16[48,12288]{1,0:T(8,128)(2,1)}, bf16[48,12288]{1,0:T(8,128)(2,1)S(1)}, u32[]{:S(2)}, u32[]{:S(2)}) %collective-permute-start.16) | collective-permute-done | bytes 1179680 | tf_op jit(solution)/shard_map/ppermute | solution.py:675
  199.4 2.0 collective-permute-done.19.refs_5_.refs_1_
  202.4 2.6 add_rows.8
  206.0 11.7 %down_kernel.2 = (f32[6,3,64,256]{3,2,1,0:T(8,128)}, bf16[2,6,3,64,256]{4,3,2,1,0:T(8,128)(2,1)}, bf16[6,3,64,256]{3,2,1,0:T(8,128)(2,1)}, f32[6,3,64,256]{3,2,1...) custom-call(s32[72]{0:T(128)} %reshape.20.down_ref, s32[24]{0:T(128)} %dynamic_slice.11.live_ref, ...), custom_call_target="tpu_custom_call" | custom-call | flops 1 | bytes 1 | tf_op jit(solution)/shard_map/down_kernel/pallas_call | solution.py:403
  217.9 1.5 collective-permute-start.23
  219.5 1.5 collective-permute-start.22
  221.0 17.4 %back.1 = (bf16[24,384,256]{2,1,0:T(8,128)(2,1)}, f32[384,256]{1,0:T(8,128)}) custom-call(s32[72]{0:T(128)} %reshape.20.down_ref, s32[24]{0:T(128)} %dynamic_slice.11.live_ref, bf16[48,12288]{1,0:T(8,128)(2,1)} %refs_0_.12, bf16[48,12288]{1,0:T(8,128)(2,1)} %fence.12.refs_1_, bf16[48,12288]{1,0:T(8,128)(2,1)} %get-tuple-element.88.refs_2_, ...), custom_call_target="tpu_custom_call" | custom-call | flops 1 | bytes 1 | tf_op jit(solution)/shard_map/back/pallas_call | solution.py:356
  238.5 11.8 %down_kernel.3 = (f32[6,3,64,256]{3,2,1,0:T(8,128)}, bf16[2,6,3,64,256]{4,3,2,1,0:T(8,128)(2,1)}, bf16[6,3,64,256]{3,2,1,0:T(8,128)(2,1)}, f32[6,3,64,256]{3,2,1...) custom-call(s32[72]{0:T(128)} %reshape.20.down_ref, s32[24]{0:T(128)} %dynamic_slice.11.live_ref, ...), custom_call_target="tpu_custom_call" | custom-call | flops 1 | bytes 1 | tf_op jit(solution)/shard_map/down_kernel/pallas_call | solution.py:403
  250.3 3.0 add_rows.9.refs_3_.refs_2_
  256.4 1.3 collective-permute-done.25
  258.7 3.9 collective-permute-start.28
  263.2 2.5 collective-permute-done.28
  265.7 4.3 collective-permute-done.26
  270.1 2.1 collective-permute-done.27
  272.4 1.3 collective-permute-done.29
  275.6 12.9 %up_kernel.2 = (f32[6,4,64,256]{3,2,1,0:T(8,128)}, bf16[2,6,4,64,256]{4,3,2,1,0:T(8,128)(2,1)}, bf16[6,4,64,256]{3,2,1,0:T(8,128)(2,1)}, f32[6,4,64,256]{3,2,1,0...) custom-call(s32[72]{0:T(128)} %reshape.19.up_ref, s32[4]{0:T(128)} %iota_xor_fusion.quarter_ref, ...), custom_call_target="tpu_custom_call" | custom-call | flops 1 | bytes 1 | tf_op jit(solution)/shard_map/up_kernel/pallas_call | solution.py:403
  288.5 12.9 %up_kernel.3 = (f32[6,4,64,256]{3,2,1,0:T(8,128)}, bf16[2,6,4,64,256]{4,3,2,1,0:T(8,128)(2,1)}, bf16[6,4,64,256]{3,2,1,0:T(8,128)(2,1)}, f32[6,4,64,256]{3,2,1,0...) custom-call(s32[72]{0:T(128)} %reshape.19.up_ref, s32[4]{0:T(128)} %iota_xor_fusion.quarter_ref, ...), custom_call_target="tpu_custom_call" | custom-call | flops 1 | bytes 1 | tf_op jit(solution)/shard_map/up_kernel/pallas_call | solution.py:403
  301.4 3.1 collective-permute-done.31.refs_2_
  304.5 3.0 add_rows.10.refs_2_
  310.4 3.6 low_in_part.1.refs_8_
  313.9 17.8 %spread.1 = (bf16[48,12288]{1,0:T(8,128)(2,1)}, bf16[48,12288]{1,0:T(8,128)(2,1)}, bf16[48,12288]{1,0:T(8,128)(2,1)}, bf16[48,12288]{1,0:T(8,128)(2,1)}, bf16[48...) custom-call(s32[72]{0:T(128)} %reshape.19.up_ref, ...), custom_call_target="tpu_custom_call" | custom-call | flops 1 | bytes 1 | tf_op jit(solution)/shard_map/spread/pallas_call | solution.py:430
  331.8 2.9 pass_on.5.refs_7_.refs_1_
  334.7 2.9 pass_on.4.refs_6_.refs_0_
  337.6 1.5 collective-permute-done.34.refs_2_
  339.1 3.0 add_rows.11.refs_9_
  342.1 3.0 collective-permute-done.36.refs_5_.refs_1_.refs_3_
  347.3 1.2 collective-permute-start.38
  348.6 1.4 collective-permute-done.40.refs_1_
  350.0 2.5 add_rows.12
  352.5 30.1 %collective-permute-done.41.refs_2_ = bf16[48,12288]{1,0:T(8,128)(2,1)} collective-permute-done((bf16[48,12288]{1,0:T(8,128)(2,1)}, bf16[48,12288]{1,0:T(8,128)(2,1)}, u32[]{:S(2)}, u32[]{:S(2)}) %collective-permute-start.41) | collective-permute-done | bytes 1179680 | tf_op jit(solution)/shard_map/ppermute | solution.py:675
  382.7 3.0 add_rows.13.refs_2_
  385.7 1.1 copy-done.17
  387.3 1.3 collective-permute-start.44
  389.1 1.2 copy.61
  390.3 3.4 pass_on.6.refs_0_
  393.7 3.4 pass_on.7.refs_1_
  397.1 20.7 %collective-permute-done.43.refs_2_ = bf16[48,12288]{1,0:T(8,128)(2,1)} collective-permute-done((bf16[48,12288]{1,0:T(8,128)(2,1)}, bf16[48,12288]{1,0:T(8,128)(2,1)}, u32[]{:S(2)}, u32[]{:S(2)}) %collective-permute-start.43) | collective-permute-done | bytes 1179680 | tf_op jit(solution)/shard_map/ppermute | solution.py:675
  417.8 3.0 add_rows.14.refs_2_
  420.8 1.4 collective-permute-done.44.refs_4_.refs_8_
  425.5 1.1 copy.62
  427.6 6.8 %sums.2.refs_0_ = f32[24,4,64,256]{3,2,1,0:T(8,128)} custom-call(f32[6,4,64,256]{3,2,1,0:T(8,128)} %get-tuple-element.124.refs_10_.refs_0_, bf16[2,6,4,64,256]{4,3,2,1,0:T(8,128)(2,1)} %copy-done.16, f32[6,4,64,256]{3,2,1,0:T(8,128)} %get-tuple-element.157.refs_2_, bf16[2,6,4,64,256]{4,3,2,1,0:T(8,128)(2,1)} %copy-done.15, ...), custom_call_target="tpu_custom_call" | custom-call | flops 1 | bytes 1 | tf_op jit(solution)/shard_map/sums/pallas_call | solution.py:592
  434.4 6.5 %sums.3 = f32[24,3,64,256]{3,2,1,0:T(8,128)} custom-call(f32[6,3,64,256]{3,2,1,0:T(8,128)} %get-tuple-element.162.refs_0_, bf16[2,6,3,64,256]{4,3,2,1,0:T(8,128)(2,1)} %copy-done.13, f32[6,3,64,256]{3,2,1,0:T(8,128)} %get-tuple-element.163.refs_2_, bf16[2,6,3,64,256]{4,3,2,1,0:T(8,128)(2,1)} %copy-done.12, ...), custom_call_target="tpu_custom_call" | custom-call | flops 1 | bytes 1 | tf_op jit(solution)/shard_map/sums/pallas_call | solution.py:592
  440.9 15.1 %collective-permute-done.47.refs_2_ = bf16[48,12288]{1,0:T(8,128)(2,1)} collective-permute-done((bf16[48,12288]{1,0:T(8,128)(2,1)}, bf16[48,12288]{1,0:T(8,128)(2,1)}, u32[]{:S(2)}, u32[]{:S(2)}) %collective-permute-start.47) | collective-permute-done | bytes 1179680 | tf_op jit(solution)/shard_map/ppermute | solution.py:675
  456.0 3.0 add_rows.15
  459.0 1.0 collective-permute-done.48.refs_1_
  461.2 1.1 copy-done.30
  462.3 6.8 %finish.1 = (f32[24,3,64,256]{3,2,1,0:T(8,128)}, f32[64,6144]{1,0:T(8,128)}) custom-call(f32[24,4,64,256]{3,2,1,0:T(8,128)} %sums.2.refs_0_, bf16[12,4,64,256]{3,2,1,0:T(8,128)(2,1)} %copy-done.29, bf16[12,4,64,256]{3,2,1,0:T(8,128)(2,1)} %copy-done.30), custom_call_target="tpu_custom_call" | custom-call | flops 1 | bytes 1 | tf_op jit(solution)/shard_map/finish/pallas_call | solution.py:622
  (171 shorter events, 35.3 us)
Async XLA Ops:
  7.2 418.3 %reduce-scatter.4.cloned.1.call-start = ((), (), s32[]{:S(2)}) async-start(), calls=%async_computation.1 | async-start | bytes 983040
  7.2 31.3 %collective-permute-start.1 = (bf16[48,12288]{1,0:T(8,128)(2,1)}, bf16[48,12288]{1,0:T(8,128)(2,1)S(1)}, u32[]{:S(2)}, u32[]{:S(2)}) collective-permute-start(bf16[48,12288]{1,0:T(8,128)(2,1)} %refs_0_.15), channel_id=1, source_target_pairs={{0,2},{1,3},{2,4},{3,5},{4,6},{5,7},{6,0},{7,1},{8,10},{9,11},{10,... | collective-permute-start | bytes 3538952 | tf_op jit(solution)/shard_map/ppermute | solution.py:675
  10.3 32.4 %collective-permute-start.3 = (bf16[48,12288]{1,0:T(8,128)(2,1)}, bf16[48,12288]{1,0:T(8,128)(2,1)S(1)}, u32[]{:S(2)}, u32[]{:S(2)}) collective-permute-start(bf16[48,12288]{1,0:T(8,128)(2,1)} %refs_0_.15), channel_id=1, source_target_pairs={{0,1},{1,0},{2,3},{3,2},{4,5},{5,4},{6,7},{7,6},{8,9},{9,8},{10,11... | collective-permute-start | bytes 3538952 | tf_op jit(solution)/shard_map/ppermute | solution.py:672
  10.3 32.4 %collective-permute-start.5 = (bf16[48,12288]{1,0:T(8,128)(2,1)}, bf16[48,12288]{1,0:T(8,128)(2,1)S(1)}, u32[]{:S(2)}, u32[]{:S(2)}) collective-permute-start(bf16[48,12288]{1,0:T(8,128)(2,1)} %refs_0_.12), channel_id=1, source_target_pairs={{0,1},{1,0},{2,3},{3,2},{4,5},{5,4},{6,7},{7,6},{8,9},{9,8},{10,11... | collective-permute-start | bytes 3538952 | tf_op jit(solution)/shard_map/ppermute | solution.py:672
  38.5 62.0 %copy-start.2 = (bf16[48,12288]{1,0:T(8,128)(2,1)}, bf16[48,12288]{1,0:T(8,128)(2,1)S(1)}, u32[]{:S(2)}) copy-start(bf16[48,12288]{1,0:T(8,128)(2,1)S(1)} %collective-permute-done.1.refs_1_.refs_5_) | copy-start | bytes 3538948
  38.5 4.2 collective-permute-start.4
  38.5 30.2 %collective-permute-start.2 = (bf16[48,12288]{1,0:T(8,128)(2,1)S(1)}, bf16[48,12288]{1,0:T(8,128)(2,1)S(1)}, u32[]{:S(2)}, u32[]{:S(2)}) collective-permute-start(bf16[48,12288]{1,0:T(8,128)(2,1)S(1)} %collective-permute-done.1.refs_1_.refs_5_), channel_id=1, source_target_pairs={{0,2},{1,3},{2,4},{3,5},{4,6},{5,7},{6,0},{7,1},{8,10},{9,11},{10,... | collective-permute-start | bytes 3538952 | tf_op jit(solution)/shard_map/ppermute | solution.py:675
  38.5 4.2 collective-permute-start.6
  42.7 26.0 %copy-start.1 = (bf16[48,12288]{1,0:T(8,128)(2,1)}, bf16[48,12288]{1,0:T(8,128)(2,1)S(1)}, u32[]{:S(2)}) copy-start(bf16[48,12288]{1,0:T(8,128)(2,1)S(1)} %collective-permute-done.5.refs_3_.refs_2_.refs_9_.refs_4_) | copy-start | bytes 3538948
  69.7 3.1 collective-permute-start.8
  69.7 30.8 %collective-permute-start.7 = (bf16[48,12288]{1,0:T(8,128)(2,1)}, bf16[48,12288]{1,0:T(8,128)(2,1)S(1)}, u32[]{:S(2)}, u32[]{:S(2)}) collective-permute-start(bf16[48,12288]{1,0:T(8,128)(2,1)} %fence.11.refs_2_.refs_6_), channel_id=1, source_target_pairs={{0,2},{1,3},{2,4},{3,5},{4,6},{5,7},{6,0},{7,1},{8,10},{9,11},{10,... | collective-permute-start | bytes 3538952 | tf_op jit(solution)/shard_map/ppermute | solution.py:675
  69.7 65.7 %collective-permute-start = (bf16[48,12288]{1,0:T(8,128)(2,1)}, bf16[48,12288]{1,0:T(8,128)(2,1)}, u32[]{:S(2)}, u32[]{:S(2)}) collective-permute-start(bf16[48,12288]{1,0:T(8,128)(2,1)} %refs_0_.12), channel_id=1, source_target_pairs={{0,2},{1,3},{2,4},{3,5},{4,6},{5,7},{6,0},{7,1},{8,10},{9,11},{10,... | collective-permute-start | bytes 3538952 | tf_op jit(solution)/shard_map/ppermute | solution.py:675
  72.8 27.7 %copy-start.5 = (bf16[48,12288]{1,0:T(8,128)(2,1)}, bf16[48,12288]{1,0:T(8,128)(2,1)S(1)}, u32[]{:S(2)}) copy-start(bf16[48,12288]{1,0:T(8,128)(2,1)S(1)} %collective-permute-done.8.refs_10_.refs_6_) | copy-start | bytes 3538948
  106.2 23.4 %collective-permute-start.11 = (bf16[192,256]{1,0:T(8,128)(2,1)S(1)}, bf16[192,256]{1,0:T(8,128)(2,1)S(1)}, u32[]{:S(2)}, u32[]{:S(2)}) collective-permute-start(bf16[192,256]{1,0:T(8,128)(2,1)S(1)} %convert_element_type.33), channel_id=1, source_target_pairs={{0,6},{1,7},{2,0},{3,1},{4,2},{5,3},{6,4},{7,5},{8,14},{9,15},{10,... | collective-permute-start | bytes 294920 | tf_op jit(solution)/shard_map/ppermute | solution.py:675
  106.2 23.9 %collective-permute-start.9 = (bf16[192,256]{1,0:T(8,128)(2,1)S(1)}, bf16[192,256]{1,0:T(8,128)(2,1)S(1)}, u32[]{:S(2)}, u32[]{:S(2)}) collective-permute-start(bf16[192,256]{1,0:T(8,128)(2,1)S(1)} %convert_element_type.33), channel_id=1, source_target_pairs={{0,2},{1,3},{2,4},{3,5},{4,6},{5,7},{6,0},{7,1},{8,10},{9,11},{10,... | collective-permute-start | bytes 294920 | tf_op jit(solution)/shard_map/ppermute | solution.py:675
  108.3 25.5 %collective-permute-start.10 = (bf16[192,256]{1,0:T(8,128)(2,1)S(1)}, bf16[192,256]{1,0:T(8,128)(2,1)S(1)}, u32[]{:S(2)}, u32[]{:S(2)}) collective-permute-start(bf16[192,256]{1,0:T(8,128)(2,1)S(1)} %convert_element_type.33), channel_id=1, source_target_pairs={{0,4},{1,5},{2,6},{3,7},{4,0},{5,1},{6,2},{7,3},{8,12},{9,13},{10,... | collective-permute-start | bytes 294920 | tf_op jit(solution)/shard_map/ppermute | solution.py:675
  108.3 32.1 %collective-permute-start.13 = (bf16[48,12288]{1,0:T(8,128)(2,1)}, bf16[48,12288]{1,0:T(8,128)(2,1)S(1)}, u32[]{:S(2)}, u32[]{:S(2)}) collective-permute-start(bf16[48,12288]{1,0:T(8,128)(2,1)} %copy-done.3), channel_id=1, source_target_pairs={{0,1},{1,0},{2,3},{3,2},{4,5},{5,4},{6,7},{7,6},{8,9},{9,8},{10,11... | collective-permute-start | bytes 3538952 | tf_op jit(solution)/shard_map/ppermute | solution.py:672
  135.4 26.0 %collective-permute-start.15 = (bf16[48,12288]{1,0:T(8,128)(2,1)}, bf16[48,12288]{1,0:T(8,128)(2,1)S(1)}, u32[]{:S(2)}, u32[]{:S(2)}) collective-permute-start(bf16[48,12288]{1,0:T(8,128)(2,1)} %fence.12.refs_1_), channel_id=1, source_target_pairs={{0,1},{1,0},{2,3},{3,2},{4,5},{5,4},{6,7},{7,6},{8,9},{9,8},{10,11... | collective-permute-start | bytes 3538952 | tf_op jit(solution)/shard_map/ppermute | solution.py:672
  135.5 30.4 %collective-permute-start.12 = (bf16[48,12288]{1,0:T(8,128)(2,1)}, bf16[48,12288]{1,0:T(8,128)(2,1)S(1)}, u32[]{:S(2)}, u32[]{:S(2)}) collective-permute-start(bf16[48,12288]{1,0:T(8,128)(2,1)} %fence.12.refs_1_), channel_id=1, source_target_pairs={{0,2},{1,3},{2,4},{3,5},{4,6},{5,7},{6,0},{7,1},{8,10},{9,11},{10,... | collective-permute-start | bytes 3538952 | tf_op jit(solution)/shard_map/ppermute | solution.py:675
  135.6 3.2 collective-permute-start.14
  161.4 4.5 copy-start.4
  166.9 18.6 %collective-permute-start.17 = (bf16[48,12288]{1,0:T(8,128)(2,1)}, bf16[48,12288]{1,0:T(8,128)(2,1)S(1)}, u32[]{:S(2)}, u32[]{:S(2)}) collective-permute-start(bf16[48,12288]{1,0:T(8,128)(2,1)} %get-tuple-element.88.refs_2_), channel_id=1, source_target_pairs={{0,1},{1,0},{2,3},{3,2},{4,5},{5,4},{6,7},{7,6},{8,9},{9,8},{10,11... | collective-permute-start | bytes 3538952 | tf_op jit(solution)/shard_map/ppermute | solution.py:672
  166.9 30.4 %collective-permute-start.16 = (bf16[48,12288]{1,0:T(8,128)(2,1)}, bf16[48,12288]{1,0:T(8,128)(2,1)S(1)}, u32[]{:S(2)}, u32[]{:S(2)}) collective-permute-start(bf16[48,12288]{1,0:T(8,128)(2,1)} %get-tuple-element.88.refs_2_), channel_id=1, source_target_pairs={{0,2},{1,3},{2,4},{3,5},{4,6},{5,7},{6,0},{7,1},{8,10},{9,11},{10,... | collective-permute-start | bytes 3538952 | tf_op jit(solution)/shard_map/ppermute | solution.py:675
  185.5 11.8 %copy-start.8 = (bf16[48,12288]{1,0:T(8,128)(2,1)}, bf16[48,12288]{1,0:T(8,128)(2,1)S(1)}, u32[]{:S(2)}) copy-start(bf16[48,12288]{1,0:T(8,128)(2,1)S(1)} %collective-permute-done.17.refs_11_.refs_6_) | copy-start | bytes 3538948
  198.3 3.1 collective-permute-start.19
  198.3 6.6 %collective-permute-start.18 = (bf16[48,12288]{1,0:T(8,128)(2,1)}, bf16[48,12288]{1,0:T(8,128)(2,1)S(1)}, u32[]{:S(2)}, u32[]{:S(2)}) collective-permute-start(bf16[48,12288]{1,0:T(8,128)(2,1)} %get-tuple-element.99.refs_3_), channel_id=1, source_target_pairs={{0,1},{1,0},{2,3},{3,2},{4,5},{5,4},{6,7},{7,6},{8,9},{9,8},{10,11... | collective-permute-start | bytes 3538952 | tf_op jit(solution)/shard_map/ppermute | solution.py:672
  205.0 45.3 %collective-permute-start.21 = (bf16[48,12288]{1,0:T(8,128)(2,1)}, bf16[48,12288]{1,0:T(8,128)(2,1)}, u32[]{:S(2)}, u32[]{:S(2)}) collective-permute-start(bf16[48,12288]{1,0:T(8,128)(2,1)} %add_rows.8), channel_id=1, source_target_pairs={{0,2},{1,3},{2,4},{3,5},{4,6},{5,7},{6,0},{7,1},{8,10},{9,11},{10,... | collective-permute-start | bytes 3538952 | tf_op jit(solution)/shard_map/ppermute | solution.py:675
  217.7 32.6 %collective-permute-start.20 = (bf16[48,12288]{1,0:T(8,128)(2,1)}, bf16[48,12288]{1,0:T(8,128)(2,1)}, u32[]{:S(2)}, u32[]{:S(2)}) collective-permute-start(bf16[48,12288]{1,0:T(8,128)(2,1)} %get-tuple-element.110), channel_id=1, source_target_pairs={{0,1},{1,0},{2,3},{3,2},{4,5},{5,4},{6,7},{7,6},{8,9},{9,8},{10,11... | collective-permute-start | bytes 3538952 | tf_op jit(solution)/shard_map/ppermute | solution.py:672
  217.9 35.4 %collective-permute-start.23 = (bf16[2,6,3,64,256]{4,3,2,1,0:T(8,128)(2,1)}, bf16[2,6,3,64,256]{4,3,2,1,0:T(8,128)(2,1)S(1)}, u32[]{:S(2)}, u32[]{:S(2)}) collective-permute-start(bf16[2,6,3,64,256]{4,3,2,1,0:T(8,128)(2,1)} %get-tuple-element.113), channel_id=1, source_target_pairs={{0,8},{8,0},{16,24},{24,16},{1,9},{9,1},{17,25},{25,17},{2,10},{10... | collective-permute-start | bytes 3538952 | tf_op jit(solution)/shard_map/ppermute | solution.py:685
  219.4 33.9 %collective-permute-start.24 = (bf16[48,12288]{1,0:T(8,128)(2,1)}, bf16[48,12288]{1,0:T(8,128)(2,1)S(1)}, u32[]{:S(2)}, u32[]{:S(2)}) collective-permute-start(bf16[48,12288]{1,0:T(8,128)(2,1)} %get-tuple-element.115), channel_id=1, source_target_pairs={{0,1},{1,0},{2,3},{3,2},{4,5},{5,4},{6,7},{7,6},{8,9},{9,8},{10,11... | collective-permute-start | bytes 3538952 | tf_op jit(solution)/shard_map/ppermute | solution.py:672
  219.5 33.8 %collective-permute-start.22 = (bf16[2,6,3,64,256]{4,3,2,1,0:T(8,128)(2,1)}, bf16[2,6,3,64,256]{4,3,2,1,0:T(8,128)(2,1)S(1)}, u32[]{:S(2)}, u32[]{:S(2)}) collective-permute-start(bf16[2,6,3,64,256]{4,3,2,1,0:T(8,128)(2,1)} %get-tuple-element.105.refs_11_), channel_id=1, source_target_pairs={{0,16},{8,24},{16,0},{24,8},{1,17},{9,25},{17,1},{25,9},{2,18},{10... | collective-permute-start | bytes 3538952 | tf_op jit(solution)/shard_map/ppermute | solution.py:685
  253.3 1.4 copy-start.26
  253.4 1.8 copy-start.13
  255.2 17.0 %copy-start.28 = (f32[384,256]{1,0:T(8,128)S(1)}, f32[384,256]{1,0:T(8,128)}, u32[]{:S(2)}) copy-start(f32[384,256]{1,0:T(8,128)} %fence.16) | copy-start | bytes 1179652
  256.2 1.5 collective-permute-start.25
  258.7 7.0 %collective-permute-start.28 = (bf16[192,256]{1,0:T(8,128)(2,1)S(1)}, bf16[192,256]{1,0:T(8,128)(2,1)S(1)}, u32[]{:S(2)}, u32[]{:S(2)}) collective-permute-start(bf16[192,256]{1,0:T(8,128)(2,1)S(1)} %fusion), channel_id=1, source_target_pairs={{0,6},{1,7},{2,0},{3,1},{4,2},{5,3},{6,4},{7,5},{8,14},{9,15},{10,... | collective-permute-start | bytes 294920 | tf_op jit(solution)/shard_map/ppermute | solution.py:675
  262.6 7.5 %collective-permute-start.26 = (bf16[192,256]{1,0:T(8,128)(2,1)S(1)}, bf16[192,256]{1,0:T(8,128)(2,1)S(1)}, u32[]{:S(2)}, u32[]{:S(2)}) collective-permute-start(bf16[192,256]{1,0:T(8,128)(2,1)S(1)} %fusion), channel_id=1, source_target_pairs={{0,2},{1,3},{2,4},{3,5},{4,6},{5,7},{6,0},{7,1},{8,10},{9,11},{10,... | collective-permute-start | bytes 294920 | tf_op jit(solution)/shard_map/ppermute | solution.py:675
  262.6 9.7 %collective-permute-start.27 = (bf16[192,256]{1,0:T(8,128)(2,1)S(1)}, bf16[192,256]{1,0:T(8,128)(2,1)S(1)}, u32[]{:S(2)}, u32[]{:S(2)}) collective-permute-start(bf16[192,256]{1,0:T(8,128)(2,1)S(1)} %fusion), channel_id=1, source_target_pairs={{0,4},{1,5},{2,6},{3,7},{4,0},{5,1},{6,2},{7,3},{8,12},{9,13},{10,... | collective-permute-start | bytes 294920 | tf_op jit(solution)/shard_map/ppermute | solution.py:675
  272.3 1.4 collective-permute-start.29
  274.4 30.1 %collective-permute-start.31 = (bf16[48,12288]{1,0:T(8,128)(2,1)}, bf16[48,12288]{1,0:T(8,128)(2,1)}, u32[]{:S(2)}, u32[]{:S(2)}) collective-permute-start(bf16[48,12288]{1,0:T(8,128)(2,1)} %get-tuple-element.122), channel_id=1, source_target_pairs={{0,2},{1,3},{2,4},{3,5},{4,6},{5,7},{6,0},{7,1},{8,10},{9,11},{10,... | collective-permute-start | bytes 3538952 | tf_op jit(solution)/shard_map/ppermute | solution.py:675
  274.4 33.1 %collective-permute-start.30 = (bf16[48,12288]{1,0:T(8,128)(2,1)}, bf16[48,12288]{1,0:T(8,128)(2,1)S(1)}, u32[]{:S(2)}, u32[]{:S(2)}) collective-permute-start(bf16[48,12288]{1,0:T(8,128)(2,1)} %get-tuple-element.117), channel_id=1, source_target_pairs={{0,1},{1,0},{2,3},{3,2},{4,5},{5,4},{6,7},{7,6},{8,9},{9,8},{10,11... | collective-permute-start | bytes 3538952 | tf_op jit(solution)/shard_map/ppermute | solution.py:672
  274.5 33.0 %collective-permute-start.33 = (bf16[2,6,3,64,256]{4,3,2,1,0:T(8,128)(2,1)}, bf16[2,6,3,64,256]{4,3,2,1,0:T(8,128)(2,1)S(1)}, u32[]{:S(2)}, u32[]{:S(2)}) collective-permute-start(bf16[2,6,3,64,256]{4,3,2,1,0:T(8,128)(2,1)} %get-tuple-element.123), channel_id=1, source_target_pairs={{0,8},{8,0},{16,24},{24,16},{1,9},{9,1},{17,25},{25,17},{2,10},{10... | collective-permute-start | bytes 3538952 | tf_op jit(solution)/shard_map/ppermute | solution.py:685
  275.1 32.4 %collective-permute-start.32 = (bf16[2,6,3,64,256]{4,3,2,1,0:T(8,128)(2,1)}, bf16[2,6,3,64,256]{4,3,2,1,0:T(8,128)(2,1)S(1)}, u32[]{:S(2)}, u32[]{:S(2)}) collective-permute-start(bf16[2,6,3,64,256]{4,3,2,1,0:T(8,128)(2,1)} %get-tuple-element.118.refs_10_), channel_id=1, source_target_pairs={{0,16},{8,24},{16,0},{24,8},{1,17},{9,25},{17,1},{25,9},{2,18},{10... | collective-permute-start | bytes 3538952 | tf_op jit(solution)/shard_map/ppermute | solution.py:685
  307.5 1.5 copy-start.19
  307.5 1.8 copy-start.20
  309.3 35.8 %collective-permute-start.36 = (bf16[2,6,4,64,256]{4,3,2,1,0:T(8,128)(2,1)}, bf16[2,6,4,64,256]{4,3,2,1,0:T(8,128)(2,1)S(1)}, u32[]{:S(2)}, u32[]{:S(2)}) collective-permute-start(bf16[2,6,4,64,256]{4,3,2,1,0:T(8,128)(2,1)} %get-tuple-element.135), channel_id=1, source_target_pairs={{0,8},{8,0},{16,24},{24,16},{1,9},{9,1},{17,25},{25,17},{2,10},{10... | collective-permute-start | bytes 4718600 | tf_op jit(solution)/shard_map/ppermute | solution.py:685
  309.8 35.6 %collective-permute-start.35 = (bf16[2,6,4,64,256]{4,3,2,1,0:T(8,128)(2,1)}, bf16[2,6,4,64,256]{4,3,2,1,0:T(8,128)(2,1)S(1)}, u32[]{:S(2)}, u32[]{:S(2)}) collective-permute-start(bf16[2,6,4,64,256]{4,3,2,1,0:T(8,128)(2,1)} %get-tuple-element.127.refs_4_), channel_id=1, source_target_pairs={{0,16},{8,24},{16,0},{24,8},{1,17},{9,25},{17,1},{25,9},{2,18},{10... | collective-permute-start | bytes 4718600 | tf_op jit(solution)/shard_map/ppermute | solution.py:685
  310.4 28.8 %collective-permute-start.34 = (bf16[48,12288]{1,0:T(8,128)(2,1)}, bf16[48,12288]{1,0:T(8,128)(2,1)}, u32[]{:S(2)}, u32[]{:S(2)}) collective-permute-start(bf16[48,12288]{1,0:T(8,128)(2,1)} %get-tuple-element.126), channel_id=1, source_target_pairs={{0,2},{1,3},{2,4},{3,5},{4,6},{5,7},{6,0},{7,1},{8,10},{9,11},{10,... | collective-permute-start | bytes 3538952 | tf_op jit(solution)/shard_map/ppermute | solution.py:675
  345.4 1.4 copy-start.16
  346.8 3.2 collective-permute-start.40
  346.8 38.8 %collective-permute-start.37 = (bf16[2,6,4,64,256]{4,3,2,1,0:T(8,128)(2,1)}, bf16[2,6,4,64,256]{4,3,2,1,0:T(8,128)(2,1)S(1)}, u32[]{:S(2)}, u32[]{:S(2)}) collective-permute-start(bf16[2,6,4,64,256]{4,3,2,1,0:T(8,128)(2,1)} %get-tuple-element.140), channel_id=1, source_target_pairs={{0,16},{8,24},{16,0},{24,8},{1,17},{9,25},{17,1},{25,9},{2,18},{10... | collective-permute-start | bytes 4718600 | tf_op jit(solution)/shard_map/ppermute | solution.py:685
  347.3 38.3 %collective-permute-start.38 = (bf16[2,6,4,64,256]{4,3,2,1,0:T(8,128)(2,1)}, bf16[2,6,4,64,256]{4,3,2,1,0:T(8,128)(2,1)S(1)}, u32[]{:S(2)}, u32[]{:S(2)}) collective-permute-start(bf16[2,6,4,64,256]{4,3,2,1,0:T(8,128)(2,1)} %get-tuple-element.143), channel_id=1, source_target_pairs={{0,8},{8,0},{16,24},{24,16},{1,9},{9,1},{17,25},{25,17},{2,10},{10... | collective-permute-start | bytes 4718600 | tf_op jit(solution)/shard_map/ppermute | solution.py:685
  348.5 4.0 collective-permute-start.39
  352.5 30.1 %collective-permute-start.41 = (bf16[48,12288]{1,0:T(8,128)(2,1)}, bf16[48,12288]{1,0:T(8,128)(2,1)}, u32[]{:S(2)}, u32[]{:S(2)}) collective-permute-start(bf16[48,12288]{1,0:T(8,128)(2,1)} %add_rows.12), channel_id=1, source_target_pairs={{0,2},{1,3},{2,4},{3,5},{4,6},{5,7},{6,0},{7,1},{8,10},{9,11},{10,... | collective-permute-start | bytes 3538952 | tf_op jit(solution)/shard_map/ppermute | solution.py:675
  385.6 1.6 copy-start.18
  387.3 1.8 copy-start.21
  387.3 9.8 %collective-permute-start.42 = (bf16[48,12288]{1,0:T(8,128)(2,1)}, bf16[48,12288]{1,0:T(8,128)(2,1)}, u32[]{:S(2)}, u32[]{:S(2)}) collective-permute-start(bf16[48,12288]{1,0:T(8,128)(2,1)} %get-tuple-element.150), channel_id=1, source_target_pairs={{0,1},{1,0},{2,3},{3,2},{4,5},{5,4},{6,7},{7,6},{8,9},{9,8},{10,11... | collective-permute-start | bytes 3538952 | tf_op jit(solution)/shard_map/ppermute | solution.py:672
  387.3 30.5 %collective-permute-start.43 = (bf16[48,12288]{1,0:T(8,128)(2,1)}, bf16[48,12288]{1,0:T(8,128)(2,1)}, u32[]{:S(2)}, u32[]{:S(2)}) collective-permute-start(bf16[48,12288]{1,0:T(8,128)(2,1)} %get-tuple-element.151), channel_id=1, source_target_pairs={{0,2},{1,3},{2,4},{3,5},{4,6},{5,7},{6,0},{7,1},{8,10},{9,11},{10,... | collective-permute-start | bytes 3538952 | tf_op jit(solution)/shard_map/ppermute | solution.py:675
  387.3 34.9 %collective-permute-start.44 = (bf16[12,3,64,256]{3,2,1,0:T(8,128)(2,1)}, bf16[12,3,64,256]{3,2,1,0:T(8,128)(2,1)S(1)}, u32[]{:S(2)}, u32[]{:S(2)}) collective-permute-start(bf16[12,3,64,256]{3,2,1,0:T(8,128)(2,1)} %get-tuple-element.153), channel_id=1, source_target_pairs={{0,8},{8,0},{16,24},{24,16},{1,9},{9,1},{17,25},{25,17},{2,10},{10... | collective-permute-start | bytes 3538952 | tf_op jit(solution)/shard_map/ppermute | solution.py:685
  388.6 34.6 %collective-permute-start.45 = (bf16[12,3,64,256]{3,2,1,0:T(8,128)(2,1)}, bf16[12,3,64,256]{3,2,1,0:T(8,128)(2,1)S(1)}, u32[]{:S(2)}, u32[]{:S(2)}) collective-permute-start(bf16[12,3,64,256]{3,2,1,0:T(8,128)(2,1)} %get-tuple-element.154), channel_id=1, source_target_pairs={{0,16},{8,24},{16,0},{24,8},{1,17},{9,25},{17,1},{25,9},{2,18},{10... | collective-permute-start | bytes 3538952 | tf_op jit(solution)/shard_map/ppermute | solution.py:685
  424.2 35.8 %collective-permute-start.48 = (bf16[12,4,64,256]{3,2,1,0:T(8,128)(2,1)}, bf16[12,4,64,256]{3,2,1,0:T(8,128)(2,1)S(1)}, u32[]{:S(2)}, u32[]{:S(2)}) collective-permute-start(bf16[12,4,64,256]{3,2,1,0:T(8,128)(2,1)} %get-tuple-element.159), channel_id=1, source_target_pairs={{0,8},{8,0},{16,24},{24,16},{1,9},{9,1},{17,25},{25,17},{2,10},{10... | collective-permute-start | bytes 4718600 | tf_op jit(solution)/shard_map/ppermute | solution.py:685
  425.0 35.8 %collective-permute-start.49 = (bf16[12,4,64,256]{3,2,1,0:T(8,128)(2,1)}, bf16[12,4,64,256]{3,2,1,0:T(8,128)(2,1)S(1)}, u32[]{:S(2)}, u32[]{:S(2)}) collective-permute-start(bf16[12,4,64,256]{3,2,1,0:T(8,128)(2,1)} %get-tuple-element.160), channel_id=1, source_target_pairs={{0,16},{8,24},{16,0},{24,8},{1,17},{9,25},{17,1},{25,9},{2,18},{10... | collective-permute-start | bytes 4718600 | tf_op jit(solution)/shard_map/ppermute | solution.py:685
  425.5 15.4 %collective-permute-start.46 = (bf16[48,12288]{1,0:T(8,128)(2,1)}, bf16[48,12288]{1,0:T(8,128)(2,1)}, u32[]{:S(2)}, u32[]{:S(2)}) collective-permute-start(bf16[48,12288]{1,0:T(8,128)(2,1)} %get-tuple-element.155), channel_id=1, source_target_pairs={{0,1},{1,0},{2,3},{3,2},{4,5},{5,4},{6,7},{7,6},{8,9},{9,8},{10,11... | collective-permute-start | bytes 3538952 | tf_op jit(solution)/shard_map/ppermute | solution.py:672
  425.5 30.5 %collective-permute-start.47 = (bf16[48,12288]{1,0:T(8,128)(2,1)}, bf16[48,12288]{1,0:T(8,128)(2,1)}, u32[]{:S(2)}, u32[]{:S(2)}) collective-permute-start(bf16[48,12288]{1,0:T(8,128)(2,1)} %get-tuple-element.156), channel_id=1, source_target_pairs={{0,2},{1,3},{2,4},{3,5},{4,6},{5,7},{6,0},{7,1},{8,10},{9,11},{10,... | collective-permute-start | bytes 3538952 | tf_op jit(solution)/shard_map/ppermute | solution.py:675
  (21 other events, 21.6 us)
Sparse Core Ops, SparseCore 0:
  390.4 31.6 reduce-scatter.3

commit v4 on v3

--- a/solution.py
+++ b/solution.py
@@ -11,7 +11,7 @@
 BF16 = jnp.bfloat16
 GELU_SCALE = 0.7978845608028654
 GELU_CUBE = 0.044715
-PER_HIDDEN, PER_PIECES, PER_BACK, PER_GRADIENTS, PER_SPREAD = 4, 6, 4, 3, 6
+PER_HIDDEN, PER_PIECES, PER_BACK, PER_GRADIENTS, PER_SPREAD = 4, 6, 4, 4, 6
 COST = pl.CostEstimate(flops=1, bytes_accessed=1, transcendentals=0)
 VMEM_LIMIT = 60 * 1024 * 1024
 
@@ -573,11 +573,11 @@
 
 
 def run_sum(parts, gots, lasts=()):
-    pairs = [
-        (own[0], got, number, half * own[0].shape[0])
-        for half, (part, gots_here) in enumerate(zip(parts, gots))
-        for number, (own, got) in enumerate(zip(part, gots_here))
-    ]
+    pairs, firsts = [], [0] * len(parts[0])
+    for part, gots_here in zip(parts, gots):
+        for number, (own, got) in enumerate(zip(part, gots_here)):
+            pairs.append((own[0], got, number, firsts[number]))
+            firsts[number] += own[0].shape[0]
     places = [(number, start) if lasts else (None, 0) for _, _, number, start in pairs]
     specs, arrays = [], []
     for own, got, _, _ in pairs:
@@ -690,18 +690,40 @@
             for n in range(len(groups))
         ]
 
+    def all_rows(total):
+        same = total.astype(BF16)
+        other, early = swapped(same), (chips - 1) * rows
+        pieces = in_rows([same[:early], same[early:]], [other[:early], other[early:]])
+        return same, jnp.concatenate(pieces, 0)
+
     def sum_rows(chip_sum):
         sent = chip_sum.astype(BF16)
         total = chip_sum
         for by in range(1, chips):
             got = shifted(sent, by)
             total = total + jnp.roll(got, by * rows, axis=0).astype(F32)
-        same = total.astype(BF16)
-        return same, jnp.concatenate([same, swapped(same)], 0)
+        return all_rows(total)
+
+    def sum_rows_in_pairs(chip_sum, waits):
+        near = [(i, i ^ 2) for i in range(mp_size)]
+        far = [(i, i ^ 4) for i in range(mp_size)]
+        got = fence([lax.ppermute(chip_sum.astype(BF16), "mp", near)], waits)[0].astype(F32)
+        even = (rank // 2) % 2 == 0
+        got = jnp.where(even, jnp.roll(got, -rows, axis=0), jnp.roll(got, rows, axis=0))
+        pair_sum = chip_sum + got
+        got = lax.ppermute(pair_sum.astype(BF16), "mp", far).astype(F32)
+        return all_rows(pair_sum + jnp.roll(got, 2 * rows, axis=0))
 
     def sum_whole(partial):
         low = lax.psum_scatter(partial, "mp", scatter_dimension=0, tiled=True).astype(BF16)
         return lax.all_gather(low, "mp", axis=0, tiled=True)
+
+    def in_rows(same, other):
+        return same[:-1] + other[:-1] + same[-1:] + other[-1:]
+
+    def by_core(parts):
+        early = chips - 1
+        return parts[:early] + parts[-2:-1] + parts[early:-2] + parts[-1:]
 
     def take_columns(piece, place):
         return lax.dynamic_slice_in_dim(piece, place * col_width, col_width, 1)
@@ -718,7 +740,7 @@
                 x_same.append(shifted(x_same[step], 1))
                 x_other.append(swapped(x_same[step]))
         x_other.append(swapped(x_same[-1]))
-        x_chunks = x_same + x_other
+        x_chunks = in_rows(x_same, x_other)
         low_same, low_half = sum_rows(
             run_low(places, x_same, low_in, other_low, x_other[2:3])
         )
@@ -742,24 +764,20 @@
         run_pieces((down_index, live), hidden, down_weight, [], out_shapes, width, size)
     )
     if by_ring:
+        mixed_parts = by_core(mixed_parts)
         arrived, *mixed_parts = fence([arriving] + mixed_parts, y_other)
         y_same.append(arrived)
         y_other.append(swapped(arrived))
-        y_chunks = y_same + y_other
-        mixed_given = [None, swapped(mixed_parts[chips + 1])]
+        y_chunks = in_rows(y_same, y_other)
+        mixed_given = [None] + [swapped(piece) for piece in mixed_parts[chips + 1 :]]
 
     down_slots = down_weight.shape[1]
-    if count % 4 == 0:
-        groups = ((count // 4, 2), (count // 4, 1))
-        starts = (0, count // 2)
+    if count % 12 == 0:
+        groups, starts = ((count // 4, 2), (count // 4, 1)), (0, count // 2)
+        down_groups = ((count // 6, 2), (count // 6, 1), (count // 3, 2), (count // 3, 1))
     else:
         groups, starts = ((count, 2),), (0,)
-
-    def down_part(start, waits):
-        return run_gradients(
-            down_kernel, (down_index, live, quarters), y_chunks, [], hidden, waits, start, groups,
-            down_slots, (size, down_slots * size), dp_size, width,
-        )
+        down_groups = groups
 
     def up_part(start, waits):
         return run_gradients(
@@ -775,45 +793,43 @@
         moved = [shifted(value, 1) for value in rest[: len(moving)]]
         return sent[0], got, moved, [swapped(value) for value in rest[len(moving) :]]
 
-    down_parts = [down_part(starts[0], [])]
-    give, moving = mixed_parts[chips + 2 :] if by_ring else [], []
-    token, got, _, given = send_round(
-        down_parts[0], [], [y_other[-1], mixed_given[1]] if by_ring else [], give
+    down_all = run_gradients(
+        down_kernel, (down_index, live, quarters), y_chunks, [], hidden, [], 0, down_groups,
+        down_slots, (size, down_slots * size), dp_size, width,
     )
-    if by_ring:
-        moving = [shifted(add_round(mixed_parts, mixed_given, 1), 1)]
-    down_got = [got]
+    down_parts = [down_all[n : n + len(groups)] for n in range(0, len(down_all), len(groups))]
+    waits = [y_other[-1]] + mixed_given[1:] if by_ring else []
+    token, got, _, _ = send_round(down_parts[0], [], waits)
+    down_got, moving = [got], []
+    if by_ring:
+        moved = shifted(add_round(mixed_parts, mixed_given, 1), 1)
+        moving = [add_round(mixed_parts, mixed_given, 2, moved)]
     back_half, back_low = run_back(
         (down_index, live), y_chunks, slope, down_weight, low_out, [token], width, size
     )
-    if len(starts) > 1:
-        down_parts.append(down_part(starts[1], [back_half]))
-    if by_ring:
-        mixed_given += given
-        moving = [add_round(mixed_parts, mixed_given, 2, moving[0])]
-        waits = down_got[0] + moving + given + [down_parts[-1][0][0]]
-        back_low = fence([back_low], waits)[0]
-        half = tok_total // 2
-        _, back_low = sum_rows(back_low[:half] + swapped(back_low[half:]))
-    else:
-        back_low = sum_whole(back_low)
-    if len(starts) > 1:
-        give = mixed_parts[chips : chips + 1] if by_ring else []
-        token, got, moving, given = send_round(
-            down_parts[1], moving, down_got[0] + [back_low], give
-        )
-        down_got.append(got)
-
+    if len(down_parts) > 1:
+        here = [part[1] for part in down_parts[1]]
+        token, *sent = fence([back_low] + here + moving, down_got[0])
+        back_low, moving = token, sent[len(here) :]
+        down_got.append([over_dp(value, way) for value, (_, way) in zip(sent, groups)])
     up_parts, waits = [], [token]
     for start in starts:
         up_parts.append(up_part(start, waits))
         waits = [up_parts[-1][0][0]]
     if by_ring:
+        low = by_core([back_low[n * rows : (n + 1) * rows] for n in range(mp_size)])
+        chip_sum = jnp.concatenate(low[:chips], 0) + swapped(jnp.concatenate(low[chips:], 0))
+        _, back_low = sum_rows_in_pairs(chip_sum, waits)
+        moving = [add_round(mixed_parts, mixed_given, 3, shifted(moving[0], 1))]
+    else:
+        back_low = sum_whole(back_low)
+    give = [mixed_parts[chips]] if by_ring else []
+    token, got, moving, given = send_round(
+        up_parts[0], moving, down_got[-1] + waits + [back_low], give
+    )
+    up_got = [got]
+    if by_ring:
         mixed_given[0] = given[0]
-        moving = [add_round(mixed_parts, mixed_given, 3, moving[0])]
-        waits = waits + given
-    token, got, moving, _ = send_round(up_parts[0], moving, down_got[-1] + waits)
-    up_got = [got]
     input_parts = list(
         run_spread(
             (up_index, rank.reshape(1)),
@@ -830,6 +846,7 @@
     down_onward = pass_on(down_parts, down_got)
     waits, give = up_got[0] + down_onward + [low_in_part], []
     if by_ring:
+        input_parts = by_core(input_parts)
         mixed = add_round(mixed_parts, mixed_given, chips, moving[0])
         waits, give = waits + [mixed], input_parts[chips + 1 : chips + 3]
     else:

time: 477 us -> 466 us (0.977)
  waiting for transfers between devices: 220 us -> 198 us
  starting transfers between devices: 22.6 us -> 33.4 us
  local copies, waits for them, and re-layouts: 27.1 us -> 36.5 us
  Pallas kernels: 184 us -> 177 us
    ppermute x18 -> x15, waiting for transfers between devices: 200 us -> 181 us  [shifted(): lax.ppermute(piece, 'mp', [(i, (i + 2 * by) % mp_size) for i in range(mp_...]
    pallas_call x4 -> x3, Pallas kernels: 49.3 us -> 42.7 us  [run_gradients(): pl.pallas_call(functools.partial(kernel, len(chunks), len(waits), first,...]
    slice x1 -> x13, local copies, waits for them, and re-layouts: 1.01 us -> 6.87 us  [the longest x2 1.83 us: local(): low = by_core([back_low[n * rows:(n + 1) * rows] for n in range(mp_size)])]
    unnamed x71 -> x75, local copies, waits for them, and re-layouts: 22.7 us -> 26.2 us
    ppermute x18 -> x15, starting transfers between devices: 9.73 us -> 13.2 us  [shifted(): lax.ppermute(piece, 'mp', [(i, (i + 2 * by) % mp_size) for i in range(mp_...]
  transfers between devices with their start and end apart: 51 -> 50, of which waited for: 29 -> 23; matrix products, arithmetic and copies ran while one was open for 3% -> 4% of each run, Pallas kernels for 37% -> 37%
where the time goes in v4:
time: 466 us; the launch traced here: 465 us
  waiting for transfers between devices  198 us (42%)
  Pallas kernels  177 us (38%)
  local copies, waits for them, and re-layouts  36.5 us (8%)
  starting transfers between devices  33.4 us (7%)
  between operations  14.5 us (3%)
  other arithmetic  5.24 us (1%)
    ppermute x15, waiting for transfers between devices, shifted(): lax.ppermute(piece, 'mp', [(i, (i + 2 * by) % mp_size) for i in range(mp_...  181 us
    pallas_call x3, Pallas kernels, run_gradients(): pl.pallas_call(functools.partial(kernel, len(chunks), len(waits), first,...  42.7 us
    unnamed x75, local copies, waits for them, and re-layouts  26.2 us
    pallas_call x8, Pallas kernels, run_add(): pl.pallas_call(add_kernel, out_shape=shape((rows, width), BF16), grid=(st...  23.1 us
    pallas_call x1, Pallas kernels, run_hidden(): pl.pallas_call(functools.partial(hidden_kernel, len(chunks), len(waits),...  20.1 us
    pallas_call x1, Pallas kernels, run_spread(): pl.pallas_call(functools.partial(spread_kernel, len(out_shapes), len(wait...  17.8 us
    pallas_call x1, Pallas kernels, run_back(): pl.pallas_call(functools.partial(back_kernel, len(chunks), len(waits), pe...  17.4 us
    pallas_call x1, Pallas kernels, run_pieces(): pl.pallas_call(functools.partial(pieces_kernel, len(out_shapes), len(wait...  16.5 us
  transfers between devices with their start and end apart: 50, of which 23 were waited for; matrix products, arithmetic and copies ran while one was open for 4% of the time, Pallas kernels for 37%

profile of v4, /device:TPU:0, one launch (start us, length us, event | category | flops | bytes accessed | tf_op | source)
XLA Modules:
  0.0 464.6 jit_solution(12783056838252331237)
XLA Ops:
  7.2 3.1 collective-permute-start.1
  10.8 27.7 %collective-permute-done.1.refs_1_.refs_5_ = bf16[48,12288]{1,0:T(8,128)(2,1)S(1)} collective-permute-done((bf16[48,12288]{1,0:T(8,128)(2,1)}, bf16[48,12288]{1,0:T(8,128)(2,1)S(1)}, u32[]{:S(2)}, u32[]{:S(2)}) %collective-permute-start.1) | collective-permute-done | bytes 1179680 | tf_op jit(solution)/shard_map/ppermute | solution.py:675
  39.0 3.7 collective-permute-done.6.refs_4_.refs_9_
  44.1 1.1 copy-done.6
  45.1 23.6 %collective-permute-done.2.refs_0_ = bf16[48,12288]{1,0:T(8,128)(2,1)S(1)} collective-permute-done((bf16[48,12288]{1,0:T(8,128)(2,1)S(1)}, bf16[48,12288]{1,0:T(8,128)(2,1)S(1)}, u32[]{:S(2)}, u32[]{:S(2)}) %collective-permute-start.2) | collective-permute-done | bytes 1179680 | tf_op jit(solution)/shard_map/ppermute | solution.py:675
  70.3 30.3 %collective-permute-done.7.refs_3_.refs_7_.refs_6_ = bf16[48,12288]{1,0:T(8,128)(2,1)S(1)} collective-permute-done((bf16[48,12288]{1,0:T(8,128)(2,1)}, bf16[48,12288]{1,0:T(8,128)(2,1)S(1)}, u32[]{:S(2)}, u32[]{:S(2)}) %collective-permute-start.7) | collective-permute-done | bytes 1179680 | tf_op jit(solution)/shard_map/ppermute | solution.py:675
  102.6 3.7 low_part.1
  107.3 3.8 collective-permute-start.11
  111.1 17.0 %collective-permute-done.9 = bf16[192,256]{1,0:T(8,128)(2,1)S(1)} collective-permute-done((bf16[192,256]{1,0:T(8,128)(2,1)S(1)}, bf16[192,256]{1,0:T(8,128)(2,1)S(1)}, u32[]{:S(2)}, u32[]{:S(2)}) %collective-permute-start.9) | collective-permute-done | bytes 98336 | tf_op jit(solution)/shard_map/ppermute | solution.py:675
  128.9 4.1 collective-permute-done.10
  133.0 1.6 add_convert_fusion.refs_1_
  142.3 20.1 %hidden.1 = (bf16[24,384,256]{2,1,0:T(8,128)(2,1)}, f32[24,384,256]{2,1,0:T(8,128)}) custom-call(s32[72]{0:T(128)} %reshape.19.up_ref, bf16[48,12288]{1,0:T(8,128)(2,1)} %refs_0_.13, bf16[48,12288]{1,0:T(8,128)(2,1)} %copy-done.1, bf16[48,12288]{1,0:T(8,128)(2,1)} %fence.11.refs_2_.refs_6_, bf16[48,12288]{1,0:T(8,128)(2,1)} %copy-done.5, ...), custom_call_target="tpu_custom_call" | custom-call | flops 1 | bytes 1 | tf_op jit(solution)/shard_map/hidden/pallas_call | solution.py:303
  162.4 2.2 collective-permute-done.12.refs_0_
  167.4 16.5 %pieces.1 = (bf16[48,12288]{1,0:T(8,128)(2,1)}, bf16[48,12288]{1,0:T(8,128)(2,1)}, bf16[48,12288]{1,0:T(8,128)(2,1)}, bf16[48,12288]{1,0:T(8,128)(2,1)}, bf16[48...) custom-call(s32[72]{0:T(128)} %reshape.20.down_ref, ...), custom_call_target="tpu_custom_call" | custom-call | flops 1 | bytes 1 | tf_op jit(solution)/shard_map/pieces/pallas_call | solution.py:331
  183.9 11.1 %collective-permute-done.16.refs_0_ = bf16[48,12288]{1,0:T(8,128)(2,1)S(1)} collective-permute-done((bf16[48,12288]{1,0:T(8,128)(2,1)}, bf16[48,12288]{1,0:T(8,128)(2,1)S(1)}, u32[]{:S(2)}, u32[]{:S(2)}) %collective-permute-start.16) | collective-permute-done | bytes 1179680 | tf_op jit(solution)/shard_map/ppermute | solution.py:675
  197.5 2.0 collective-permute-done.19.refs_3_.refs_1_
  200.6 2.6 add_rows.8
  204.8 16.9 %down_kernel.1 = (f32[4,3,64,256]{3,2,1,0:T(8,128)}, bf16[2,4,3,64,256]{4,3,2,1,0:T(8,128)(2,1)}, bf16[4,3,64,256]{3,2,1,0:T(8,128)(2,1)}, f32[4,3,64,256]{3,2,1...) custom-call(s32[72]{0:T(128)} %reshape.20.down_ref, ...), custom_call_target="tpu_custom_call" | custom-call | flops 1 | bytes 1 | tf_op jit(solution)/shard_map/down_kernel/pallas_call | solution.py:403
  222.7 1.5 collective-permute-start.23
  224.2 1.5 collective-permute-start.24
  225.7 17.4 %back.1 = (bf16[24,384,256]{2,1,0:T(8,128)(2,1)}, f32[384,256]{1,0:T(8,128)}) custom-call(s32[72]{0:T(128)} %reshape.20.down_ref, s32[24]{0:T(128)} %dynamic_slice.11.live_ref, bf16[48,12288]{1,0:T(8,128)(2,1)} %refs_0_.10, bf16[48,12288]{1,0:T(8,128)(2,1)} %fence.12.refs_1_, bf16[48,12288]{1,0:T(8,128)(2,1)} %get-tuple-element.87.refs_2_, ...), custom_call_target="tpu_custom_call" | custom-call | flops 1 | bytes 1 | tf_op jit(solution)/shard_map/back/pallas_call | solution.py:356
  244.2 3.0 add_rows.9.refs_3_
  252.6 2.0 collective-permute-start.25
  254.6 12.9 %up_kernel.2 = (f32[6,4,64,256]{3,2,1,0:T(8,128)}, bf16[2,6,4,64,256]{4,3,2,1,0:T(8,128)(2,1)}, bf16[6,4,64,256]{3,2,1,0:T(8,128)(2,1)}, f32[6,4,64,256]{3,2,1,0...) custom-call(s32[72]{0:T(128)} %reshape.19.up_ref, s32[4]{0:T(128)} %iota_xor_fusion.quarter_ref, ...), custom_call_target="tpu_custom_call" | custom-call | flops 1 | bytes 1 | tf_op jit(solution)/shard_map/up_kernel/pallas_call | solution.py:403
  267.5 12.9 %up_kernel.3 = (f32[6,4,64,256]{3,2,1,0:T(8,128)}, bf16[2,6,4,64,256]{4,3,2,1,0:T(8,128)(2,1)}, bf16[6,4,64,256]{3,2,1,0:T(8,128)(2,1)}, f32[6,4,64,256]{3,2,1,0...) custom-call(s32[72]{0:T(128)} %reshape.19.up_ref, s32[4]{0:T(128)} %iota_xor_fusion.quarter_ref, ...), custom_call_target="tpu_custom_call" | custom-call | flops 1 | bytes 1 | tf_op jit(solution)/shard_map/up_kernel/pallas_call | solution.py:403
  282.9 2.7 collective-permute-start.30
  285.6 2.9 collective-permute-done.30
  288.6 1.3 collective-permute-done.31
  290.6 3.0 add_rows.10.refs_2_
  293.6 1.1 copy-done.13
  295.3 2.2 collective-permute-start.34
  297.5 1.5 collective-permute-start.35
  299.0 1.9 collective-permute-start.33
  300.9 3.6 low_in_part.1.refs_8_
  304.5 17.8 %spread.1 = (bf16[48,12288]{1,0:T(8,128)(2,1)}, bf16[48,12288]{1,0:T(8,128)(2,1)}, bf16[48,12288]{1,0:T(8,128)(2,1)}, bf16[48,12288]{1,0:T(8,128)(2,1)}, bf16[48...) custom-call(s32[72]{0:T(128)} %reshape.19.up_ref, ...), custom_call_target="tpu_custom_call" | custom-call | flops 1 | bytes 1 | tf_op jit(solution)/shard_map/spread/pallas_call | solution.py:430
  322.2 2.9 pass_on.5.refs_7_.refs_1_
  325.1 2.9 pass_on.4.refs_6_.refs_0_
  328.0 1.5 collective-permute-done.33.refs_2_
  329.5 3.0 add_rows.11.refs_9_
  332.5 1.4 collective-permute-done.35.refs_5_.refs_1_.refs_3_
  333.9 1.2 copy-done.10
  335.9 1.5 collective-permute-start.37
  338.3 2.6 add_rows.12
  340.9 1.9 collective-permute-start.40
  342.8 28.2 %collective-permute-done.40.refs_2_ = bf16[48,12288]{1,0:T(8,128)(2,1)} collective-permute-done((bf16[48,12288]{1,0:T(8,128)(2,1)}, bf16[48,12288]{1,0:T(8,128)(2,1)}, u32[]{:S(2)}, u32[]{:S(2)}) %collective-permute-start.40) | collective-permute-done | bytes 1179680 | tf_op jit(solution)/shard_map/ppermute | solution.py:675
  371.0 3.0 add_rows.13.refs_2_
  374.0 1.2 copy-done.11
  375.8 1.5 collective-permute-start.43
  377.3 1.2 collective-permute-start.44
  378.5 1.1 copy.60
  379.6 3.4 pass_on.7.refs_1_
  383.0 3.3 pass_on.6.refs_0_
  386.3 19.8 %collective-permute-done.42.refs_2_ = bf16[48,12288]{1,0:T(8,128)(2,1)} collective-permute-done((bf16[48,12288]{1,0:T(8,128)(2,1)}, bf16[48,12288]{1,0:T(8,128)(2,1)}, u32[]{:S(2)}, u32[]{:S(2)}) %collective-permute-start.42) | collective-permute-done | bytes 1179680 | tf_op jit(solution)/shard_map/ppermute | solution.py:675
  406.1 3.0 add_rows.14.refs_2_
  409.1 1.4 collective-permute-done.43.refs_4_.refs_8_
  410.5 1.2 collective-permute-done.44.refs_5_.refs_9_
  413.5 1.1 collective-permute-start.48
  414.8 1.1 copy.61
  416.9 6.8 %sums.2.refs_0_ = f32[24,4,64,256]{3,2,1,0:T(8,128)} custom-call(f32[6,4,64,256]{3,2,1,0:T(8,128)} %get-tuple-element.120.refs_10_.refs_0_, bf16[2,6,4,64,256]{4,3,2,1,0:T(8,128)(2,1)} %copy-done.9, f32[6,4,64,256]{3,2,1,0:T(8,128)} %get-tuple-element.154.refs_2_, bf16[2,6,4,64,256]{4,3,2,1,0:T(8,128)(2,1)} %copy-done.10, ...), custom_call_target="tpu_custom_call" | custom-call | flops 1 | bytes 1 | tf_op jit(solution)/shard_map/sums/pallas_call | solution.py:592
  423.6 6.5 %sums.3 = f32[24,3,64,256]{3,2,1,0:T(8,128)} custom-call(f32[4,3,64,256]{3,2,1,0:T(8,128)} %get-tuple-element.159.refs_0_, bf16[2,4,3,64,256]{4,3,2,1,0:T(8,128)(2,1)} %copy-done.19, f32[4,3,64,256]{3,2,1,0:T(8,128)} %get-tuple-element.160.refs_2_, bf16[2,4,3,64,256]{4,3,2,1,0:T(8,128)(2,1)} %copy-done.20, f32[8,3,64,256]{3,2,1,0:T(8,128)} %get-tuple-element.161.refs_4_, ...), custom_call_target="tpu_custom_call" | custom-call | flops 1 | bytes 1 | tf_op jit(solution)/shard_map/sums/pallas_call | solution.py:592
  430.2 14.9 %collective-permute-done.46.refs_2_ = bf16[48,12288]{1,0:T(8,128)(2,1)} collective-permute-done((bf16[48,12288]{1,0:T(8,128)(2,1)}, bf16[48,12288]{1,0:T(8,128)(2,1)}, u32[]{:S(2)}, u32[]{:S(2)}) %collective-permute-start.46) | collective-permute-done | bytes 1179680 | tf_op jit(solution)/shard_map/ppermute | solution.py:675
  445.0 3.0 add_rows.15
  449.7 1.1 copy-done.29
  450.9 6.8 %finish.1 = (f32[24,3,64,256]{3,2,1,0:T(8,128)}, f32[64,6144]{1,0:T(8,128)}) custom-call(f32[24,4,64,256]{3,2,1,0:T(8,128)} %sums.2.refs_0_, bf16[12,4,64,256]{3,2,1,0:T(8,128)(2,1)} %copy-done.28, bf16[12,4,64,256]{3,2,1,0:T(8,128)(2,1)} %copy-done.29), custom_call_target="tpu_custom_call" | custom-call | flops 1 | bytes 1 | tf_op jit(solution)/shard_map/finish/pallas_call | solution.py:622
  (181 shorter events, 41.4 us)
Async XLA Ops:
  7.2 407.6 %reduce-scatter.4.cloned.1.call-start = ((), (), s32[]{:S(2)}) async-start(), calls=%async_computation.1 | async-start | bytes 983040
  7.2 31.3 %collective-permute-start.1 = (bf16[48,12288]{1,0:T(8,128)(2,1)}, bf16[48,12288]{1,0:T(8,128)(2,1)S(1)}, u32[]{:S(2)}, u32[]{:S(2)}) collective-permute-start(bf16[48,12288]{1,0:T(8,128)(2,1)} %refs_0_.13), channel_id=1, source_target_pairs={{0,2},{1,3},{2,4},{3,5},{4,6},{5,7},{6,0},{7,1},{8,10},{9,11},{10,... | collective-permute-start | bytes 3538952 | tf_op jit(solution)/shard_map/ppermute | solution.py:675
  10.3 32.4 %collective-permute-start.3 = (bf16[48,12288]{1,0:T(8,128)(2,1)}, bf16[48,12288]{1,0:T(8,128)(2,1)S(1)}, u32[]{:S(2)}, u32[]{:S(2)}) collective-permute-start(bf16[48,12288]{1,0:T(8,128)(2,1)} %refs_0_.13), channel_id=1, source_target_pairs={{0,1},{1,0},{2,3},{3,2},{4,5},{5,4},{6,7},{7,6},{8,9},{9,8},{10,11... | collective-permute-start | bytes 3538952 | tf_op jit(solution)/shard_map/ppermute | solution.py:672
  10.3 32.4 %collective-permute-start.5 = (bf16[48,12288]{1,0:T(8,128)(2,1)}, bf16[48,12288]{1,0:T(8,128)(2,1)S(1)}, u32[]{:S(2)}, u32[]{:S(2)}) collective-permute-start(bf16[48,12288]{1,0:T(8,128)(2,1)} %refs_0_.10), channel_id=1, source_target_pairs={{0,1},{1,0},{2,3},{3,2},{4,5},{5,4},{6,7},{7,6},{8,9},{9,8},{10,11... | collective-permute-start | bytes 3538952 | tf_op jit(solution)/shard_map/ppermute | solution.py:672
  38.5 62.1 %copy-start.1 = (bf16[48,12288]{1,0:T(8,128)(2,1)}, bf16[48,12288]{1,0:T(8,128)(2,1)S(1)}, u32[]{:S(2)}) copy-start(bf16[48,12288]{1,0:T(8,128)(2,1)S(1)} %collective-permute-done.1.refs_1_.refs_5_) | copy-start | bytes 3538948
  38.5 4.2 collective-permute-start.4
  38.5 30.2 %collective-permute-start.2 = (bf16[48,12288]{1,0:T(8,128)(2,1)S(1)}, bf16[48,12288]{1,0:T(8,128)(2,1)S(1)}, u32[]{:S(2)}, u32[]{:S(2)}) collective-permute-start(bf16[48,12288]{1,0:T(8,128)(2,1)S(1)} %collective-permute-done.1.refs_1_.refs_5_), channel_id=1, source_target_pairs={{0,2},{1,3},{2,4},{3,5},{4,6},{5,7},{6,0},{7,1},{8,10},{9,11},{10,... | collective-permute-start | bytes 3538952 | tf_op jit(solution)/shard_map/ppermute | solution.py:675
  38.5 4.2 collective-permute-start.6
  42.7 1.4 copy-start.5
  42.7 26.0 %copy-start.3 = (bf16[48,12288]{1,0:T(8,128)(2,1)}, bf16[48,12288]{1,0:T(8,128)(2,1)S(1)}, u32[]{:S(2)}) copy-start(bf16[48,12288]{1,0:T(8,128)(2,1)S(1)} %collective-permute-done.5.refs_3_.refs_2_.refs_9_) | copy-start | bytes 3538948
  69.7 30.9 %collective-permute-start.7 = (bf16[48,12288]{1,0:T(8,128)(2,1)}, bf16[48,12288]{1,0:T(8,128)(2,1)S(1)}, u32[]{:S(2)}, u32[]{:S(2)}) collective-permute-start(bf16[48,12288]{1,0:T(8,128)(2,1)} %fence.11.refs_2_.refs_6_), channel_id=1, source_target_pairs={{0,2},{1,3},{2,4},{3,5},{4,6},{5,7},{6,0},{7,1},{8,10},{9,11},{10,... | collective-permute-start | bytes 3538952 | tf_op jit(solution)/shard_map/ppermute | solution.py:675
  69.7 30.9 %collective-permute-start.8 = (bf16[48,12288]{1,0:T(8,128)(2,1)}, bf16[48,12288]{1,0:T(8,128)(2,1)S(1)}, u32[]{:S(2)}, u32[]{:S(2)}) collective-permute-start(bf16[48,12288]{1,0:T(8,128)(2,1)} %fence.11.refs_2_.refs_6_), channel_id=1, source_target_pairs={{0,1},{1,0},{2,3},{3,2},{4,5},{5,4},{6,7},{7,6},{8,9},{9,8},{10,11... | collective-permute-start | bytes 3538952 | tf_op jit(solution)/shard_map/ppermute | solution.py:672
  69.7 65.0 %collective-permute-start = (bf16[48,12288]{1,0:T(8,128)(2,1)}, bf16[48,12288]{1,0:T(8,128)(2,1)}, u32[]{:S(2)}, u32[]{:S(2)}) collective-permute-start(bf16[48,12288]{1,0:T(8,128)(2,1)} %refs_0_.10), channel_id=1, source_target_pairs={{0,2},{1,3},{2,4},{3,5},{4,6},{5,7},{6,0},{7,1},{8,10},{9,11},{10,... | collective-permute-start | bytes 3538952 | tf_op jit(solution)/shard_map/ppermute | solution.py:675
  107.2 20.9 %collective-permute-start.9 = (bf16[192,256]{1,0:T(8,128)(2,1)S(1)}, bf16[192,256]{1,0:T(8,128)(2,1)S(1)}, u32[]{:S(2)}, u32[]{:S(2)}) collective-permute-start(bf16[192,256]{1,0:T(8,128)(2,1)S(1)} %convert_element_type.33), channel_id=1, source_target_pairs={{0,2},{1,3},{2,4},{3,5},{4,6},{5,7},{6,0},{7,1},{8,10},{9,11},{10,... | collective-permute-start | bytes 294920 | tf_op jit(solution)/shard_map/ppermute | solution.py:675
  107.3 21.6 %collective-permute-start.11 = (bf16[192,256]{1,0:T(8,128)(2,1)S(1)}, bf16[192,256]{1,0:T(8,128)(2,1)S(1)}, u32[]{:S(2)}, u32[]{:S(2)}) collective-permute-start(bf16[192,256]{1,0:T(8,128)(2,1)S(1)} %convert_element_type.33), channel_id=1, source_target_pairs={{0,6},{1,7},{2,0},{3,1},{4,2},{5,3},{6,4},{7,5},{8,14},{9,15},{10,... | collective-permute-start | bytes 294920 | tf_op jit(solution)/shard_map/ppermute | solution.py:675
  111.1 21.9 %collective-permute-start.10 = (bf16[192,256]{1,0:T(8,128)(2,1)S(1)}, bf16[192,256]{1,0:T(8,128)(2,1)S(1)}, u32[]{:S(2)}, u32[]{:S(2)}) collective-permute-start(bf16[192,256]{1,0:T(8,128)(2,1)S(1)} %convert_element_type.33), channel_id=1, source_target_pairs={{0,4},{1,5},{2,6},{3,7},{4,0},{5,1},{6,2},{7,3},{8,12},{9,13},{10,... | collective-permute-start | bytes 294920 | tf_op jit(solution)/shard_map/ppermute | solution.py:675
  111.1 30.2 %collective-permute-start.13 = (bf16[48,12288]{1,0:T(8,128)(2,1)}, bf16[48,12288]{1,0:T(8,128)(2,1)S(1)}, u32[]{:S(2)}, u32[]{:S(2)}) collective-permute-start(bf16[48,12288]{1,0:T(8,128)(2,1)} %copy-done.2), channel_id=1, source_target_pairs={{0,1},{1,0},{2,3},{3,2},{4,5},{5,4},{6,7},{7,6},{8,9},{9,8},{10,11... | collective-permute-start | bytes 3538952 | tf_op jit(solution)/shard_map/ppermute | solution.py:672
  134.7 29.9 %collective-permute-start.12 = (bf16[48,12288]{1,0:T(8,128)(2,1)}, bf16[48,12288]{1,0:T(8,128)(2,1)S(1)}, u32[]{:S(2)}, u32[]{:S(2)}) collective-permute-start(bf16[48,12288]{1,0:T(8,128)(2,1)} %fence.12.refs_1_), channel_id=1, source_target_pairs={{0,2},{1,3},{2,4},{3,5},{4,6},{5,7},{6,0},{7,1},{8,10},{9,11},{10,... | collective-permute-start | bytes 3538952 | tf_op jit(solution)/shard_map/ppermute | solution.py:675
  134.7 29.9 %collective-permute-start.15 = (bf16[48,12288]{1,0:T(8,128)(2,1)}, bf16[48,12288]{1,0:T(8,128)(2,1)S(1)}, u32[]{:S(2)}, u32[]{:S(2)}) collective-permute-start(bf16[48,12288]{1,0:T(8,128)(2,1)} %fence.12.refs_1_), channel_id=1, source_target_pairs={{0,1},{1,0},{2,3},{3,2},{4,5},{5,4},{6,7},{7,6},{8,9},{9,8},{10,11... | collective-permute-start | bytes 3538952 | tf_op jit(solution)/shard_map/ppermute | solution.py:672
  134.8 4.2 collective-permute-start.14
  164.6 1.4 copy-start.7
  166.0 29.0 %collective-permute-start.16 = (bf16[48,12288]{1,0:T(8,128)(2,1)}, bf16[48,12288]{1,0:T(8,128)(2,1)S(1)}, u32[]{:S(2)}, u32[]{:S(2)}) collective-permute-start(bf16[48,12288]{1,0:T(8,128)(2,1)} %get-tuple-element.87.refs_2_), channel_id=1, source_target_pairs={{0,2},{1,3},{2,4},{3,5},{4,6},{5,7},{6,0},{7,1},{8,10},{9,11},{10,... | collective-permute-start | bytes 3538952 | tf_op jit(solution)/shard_map/ppermute | solution.py:675
  166.0 29.0 %collective-permute-start.17 = (bf16[48,12288]{1,0:T(8,128)(2,1)}, bf16[48,12288]{1,0:T(8,128)(2,1)S(1)}, u32[]{:S(2)}, u32[]{:S(2)}) collective-permute-start(bf16[48,12288]{1,0:T(8,128)(2,1)} %get-tuple-element.87.refs_2_), channel_id=1, source_target_pairs={{0,1},{1,0},{2,3},{3,2},{4,5},{5,4},{6,7},{7,6},{8,9},{9,8},{10,11... | collective-permute-start | bytes 3538952 | tf_op jit(solution)/shard_map/ppermute | solution.py:672
  195.1 1.4 copy-start.15
  196.5 3.1 collective-permute-start.19
  196.5 7.3 %collective-permute-start.18 = (bf16[48,12288]{1,0:T(8,128)(2,1)}, bf16[48,12288]{1,0:T(8,128)(2,1)S(1)}, u32[]{:S(2)}, u32[]{:S(2)}) collective-permute-start(bf16[48,12288]{1,0:T(8,128)(2,1)} %get-tuple-element.98.refs_6_), channel_id=1, source_target_pairs={{0,1},{1,0},{2,3},{3,2},{4,5},{5,4},{6,7},{7,6},{8,9},{9,8},{10,11... | collective-permute-start | bytes 3538952 | tf_op jit(solution)/shard_map/ppermute | solution.py:672
  197.0 24.7 %collective-permute-start.20 = (bf16[48,12288]{1,0:T(8,128)(2,1)}, bf16[48,12288]{1,0:T(8,128)(2,1)}, u32[]{:S(2)}, u32[]{:S(2)}) collective-permute-start(bf16[48,12288]{1,0:T(8,128)(2,1)} %get-tuple-element.102), channel_id=1, source_target_pairs={{0,1},{1,0},{2,3},{3,2},{4,5},{5,4},{6,7},{7,6},{8,9},{9,8},{10,11... | collective-permute-start | bytes 3538952 | tf_op jit(solution)/shard_map/ppermute | solution.py:672
  197.0 24.7 %collective-permute-start.21 = (bf16[48,12288]{1,0:T(8,128)(2,1)}, bf16[48,12288]{1,0:T(8,128)(2,1)S(1)}, u32[]{:S(2)}, u32[]{:S(2)}) collective-permute-start(bf16[48,12288]{1,0:T(8,128)(2,1)} %get-tuple-element.103), channel_id=1, source_target_pairs={{0,1},{1,0},{2,3},{3,2},{4,5},{5,4},{6,7},{7,6},{8,9},{9,8},{10,11... | collective-permute-start | bytes 3538952 | tf_op jit(solution)/shard_map/ppermute | solution.py:672
  203.2 40.0 %collective-permute-start.22 = (bf16[48,12288]{1,0:T(8,128)(2,1)}, bf16[48,12288]{1,0:T(8,128)(2,1)S(1)}, u32[]{:S(2)}, u32[]{:S(2)}) collective-permute-start(bf16[48,12288]{1,0:T(8,128)(2,1)} %add_rows.8), channel_id=1, source_target_pairs={{0,2},{1,3},{2,4},{3,5},{4,6},{5,7},{6,0},{7,1},{8,10},{9,11},{10,... | collective-permute-start | bytes 3538952 | tf_op jit(solution)/shard_map/ppermute | solution.py:675
  222.7 24.5 %collective-permute-start.23 = (bf16[2,4,3,64,256]{4,3,2,1,0:T(8,128)(2,1)}, bf16[2,4,3,64,256]{4,3,2,1,0:T(8,128)(2,1)S(1)}, u32[]{:S(2)}, u32[]{:S(2)}) collective-permute-start(bf16[2,4,3,64,256]{4,3,2,1,0:T(8,128)(2,1)} %get-tuple-element.104.refs_11_), channel_id=1, source_target_pairs={{0,16},{8,24},{16,0},{24,8},{1,17},{9,25},{17,1},{25,9},{2,18},{10... | collective-permute-start | bytes 2359304 | tf_op jit(solution)/shard_map/ppermute | solution.py:685
  224.2 23.0 %collective-permute-start.24 = (bf16[2,4,3,64,256]{4,3,2,1,0:T(8,128)(2,1)}, bf16[2,4,3,64,256]{4,3,2,1,0:T(8,128)(2,1)S(1)}, u32[]{:S(2)}, u32[]{:S(2)}) collective-permute-start(bf16[2,4,3,64,256]{4,3,2,1,0:T(8,128)(2,1)} %get-tuple-element.111), channel_id=1, source_target_pairs={{0,8},{8,0},{16,24},{24,16},{1,9},{9,1},{17,25},{25,17},{2,10},{10... | collective-permute-start | bytes 2359304 | tf_op jit(solution)/shard_map/ppermute | solution.py:685
  250.3 1.5 collective-permute-start.28
  250.3 43.3 %collective-permute-start.27 = (bf16[2,8,3,64,256]{4,3,2,1,0:T(8,128)(2,1)}, bf16[2,8,3,64,256]{4,3,2,1,0:T(8,128)(2,1)S(1)}, u32[]{:S(2)}, u32[]{:S(2)}) collective-permute-start(bf16[2,8,3,64,256]{4,3,2,1,0:T(8,128)(2,1)} %get-tuple-element.119), channel_id=1, source_target_pairs={{0,8},{8,0},{16,24},{24,16},{1,9},{9,1},{17,25},{25,17},{2,10},{10... | collective-permute-start | bytes 4718600 | tf_op jit(solution)/shard_map/ppermute | solution.py:685
  250.9 42.7 %collective-permute-start.26 = (bf16[2,8,3,64,256]{4,3,2,1,0:T(8,128)(2,1)}, bf16[2,8,3,64,256]{4,3,2,1,0:T(8,128)(2,1)S(1)}, u32[]{:S(2)}, u32[]{:S(2)}) collective-permute-start(bf16[2,8,3,64,256]{4,3,2,1,0:T(8,128)(2,1)} %get-tuple-element.118), channel_id=1, source_target_pairs={{0,16},{8,24},{16,0},{24,8},{1,17},{9,25},{17,1},{25,9},{2,18},{10... | collective-permute-start | bytes 4718600 | tf_op jit(solution)/shard_map/ppermute | solution.py:685
  252.5 27.9 %collective-permute-start.29 = (bf16[192,256]{1,0:T(8,128)(2,1)S(1)}, bf16[192,256]{1,0:T(8,128)(2,1)S(1)}, u32[]{:S(2)}, u32[]{:S(2)}) collective-permute-start(bf16[192,256]{1,0:T(8,128)(2,1)S(1)} %fusion.2), channel_id=1, source_target_pairs={{0,2},{1,3},{2,0},{3,1},{4,6},{5,7},{6,4},{7,5},{8,10},{9,11},{10,... | collective-permute-start | bytes 294920 | tf_op jit(solution)/shard_map/ppermute | solution.py:710
  252.6 38.0 %collective-permute-start.25 = (bf16[48,12288]{1,0:T(8,128)(2,1)}, bf16[48,12288]{1,0:T(8,128)(2,1)}, u32[]{:S(2)}, u32[]{:S(2)}) collective-permute-start(bf16[48,12288]{1,0:T(8,128)(2,1)} %get-tuple-element.116), channel_id=1, source_target_pairs={{0,2},{1,3},{2,4},{3,5},{4,6},{5,7},{6,0},{7,1},{8,10},{9,11},{10,... | collective-permute-start | bytes 3538952 | tf_op jit(solution)/shard_map/ppermute | solution.py:675
  281.0 1.8 copy-start.32
  282.9 5.6 %collective-permute-start.30 = (bf16[192,256]{1,0:T(8,128)(2,1)S(1)}, bf16[192,256]{1,0:T(8,128)(2,1)S(1)}, u32[]{:S(2)}, u32[]{:S(2)}) collective-permute-start(bf16[192,256]{1,0:T(8,128)(2,1)S(1)} %get-tuple-element.182), channel_id=1, source_target_pairs={{0,4},{1,5},{2,6},{3,7},{4,0},{5,1},{6,2},{7,3},{8,12},{9,13},{10,... | collective-permute-start | bytes 294920 | tf_op jit(solution)/shard_map/ppermute | solution.py:714
  288.5 1.4 collective-permute-start.31
  293.6 1.7 copy-start.14
  295.3 37.2 %collective-permute-start.34 = (bf16[2,6,4,64,256]{4,3,2,1,0:T(8,128)(2,1)}, bf16[2,6,4,64,256]{4,3,2,1,0:T(8,128)(2,1)S(1)}, u32[]{:S(2)}, u32[]{:S(2)}) collective-permute-start(bf16[2,6,4,64,256]{4,3,2,1,0:T(8,128)(2,1)} %get-tuple-element.124.refs_4_), channel_id=1, source_target_pairs={{0,16},{8,24},{16,0},{24,8},{1,17},{9,25},{17,1},{25,9},{2,18},{10... | collective-permute-start | bytes 4718600 | tf_op jit(solution)/shard_map/ppermute | solution.py:685
  297.5 36.4 %collective-permute-start.35 = (bf16[2,6,4,64,256]{4,3,2,1,0:T(8,128)(2,1)}, bf16[2,6,4,64,256]{4,3,2,1,0:T(8,128)(2,1)S(1)}, u32[]{:S(2)}, u32[]{:S(2)}) collective-permute-start(bf16[2,6,4,64,256]{4,3,2,1,0:T(8,128)(2,1)} %get-tuple-element.132), channel_id=1, source_target_pairs={{0,8},{8,0},{16,24},{24,16},{1,9},{9,1},{17,25},{25,17},{2,10},{10... | collective-permute-start | bytes 4718600 | tf_op jit(solution)/shard_map/ppermute | solution.py:685
  299.0 29.0 %collective-permute-start.32 = (bf16[48,12288]{1,0:T(8,128)(2,1)}, bf16[48,12288]{1,0:T(8,128)(2,1)}, u32[]{:S(2)}, u32[]{:S(2)}) collective-permute-start(bf16[48,12288]{1,0:T(8,128)(2,1)} %get-tuple-element.122), channel_id=1, source_target_pairs={{0,1},{1,0},{2,3},{3,2},{4,5},{5,4},{6,7},{7,6},{8,9},{9,8},{10,11... | collective-permute-start | bytes 3538952 | tf_op jit(solution)/shard_map/ppermute | solution.py:672
  299.0 30.5 %collective-permute-start.33 = (bf16[48,12288]{1,0:T(8,128)(2,1)}, bf16[48,12288]{1,0:T(8,128)(2,1)}, u32[]{:S(2)}, u32[]{:S(2)}) collective-permute-start(bf16[48,12288]{1,0:T(8,128)(2,1)} %get-tuple-element.123), channel_id=1, source_target_pairs={{0,2},{1,3},{2,4},{3,5},{4,6},{5,7},{6,0},{7,1},{8,10},{9,11},{10,... | collective-permute-start | bytes 3538952 | tf_op jit(solution)/shard_map/ppermute | solution.py:675
  332.5 1.4 copy-start.9
  333.9 1.2 copy-start.10
  335.1 3.2 collective-permute-start.39
  335.1 38.8 %collective-permute-start.36 = (bf16[2,6,4,64,256]{4,3,2,1,0:T(8,128)(2,1)}, bf16[2,6,4,64,256]{4,3,2,1,0:T(8,128)(2,1)S(1)}, u32[]{:S(2)}, u32[]{:S(2)}) collective-permute-start(bf16[2,6,4,64,256]{4,3,2,1,0:T(8,128)(2,1)} %get-tuple-element.137), channel_id=1, source_target_pairs={{0,16},{8,24},{16,0},{24,8},{1,17},{9,25},{17,1},{25,9},{2,18},{10... | collective-permute-start | bytes 4718600 | tf_op jit(solution)/shard_map/ppermute | solution.py:685
  335.9 38.1 %collective-permute-start.37 = (bf16[2,6,4,64,256]{4,3,2,1,0:T(8,128)(2,1)}, bf16[2,6,4,64,256]{4,3,2,1,0:T(8,128)(2,1)S(1)}, u32[]{:S(2)}, u32[]{:S(2)}) collective-permute-start(bf16[2,6,4,64,256]{4,3,2,1,0:T(8,128)(2,1)} %get-tuple-element.140), channel_id=1, source_target_pairs={{0,8},{8,0},{16,24},{24,16},{1,9},{9,1},{17,25},{25,17},{2,10},{10... | collective-permute-start | bytes 4718600 | tf_op jit(solution)/shard_map/ppermute | solution.py:685
  337.4 5.3 %collective-permute-start.38 = (bf16[48,12288]{1,0:T(8,128)(2,1)}, bf16[48,12288]{1,0:T(8,128)(2,1)}, u32[]{:S(2)}, u32[]{:S(2)}) collective-permute-start(bf16[48,12288]{1,0:T(8,128)(2,1)} %get-tuple-element.143), channel_id=1, source_target_pairs={{0,1},{1,0},{2,3},{3,2},{4,5},{5,4},{6,7},{7,6},{8,9},{9,8},{10,11... | collective-permute-start | bytes 3538952 | tf_op jit(solution)/shard_map/ppermute | solution.py:672
  340.9 30.1 %collective-permute-start.40 = (bf16[48,12288]{1,0:T(8,128)(2,1)}, bf16[48,12288]{1,0:T(8,128)(2,1)}, u32[]{:S(2)}, u32[]{:S(2)}) collective-permute-start(bf16[48,12288]{1,0:T(8,128)(2,1)} %add_rows.12), channel_id=1, source_target_pairs={{0,2},{1,3},{2,4},{3,5},{4,6},{5,7},{6,0},{7,1},{8,10},{9,11},{10,... | collective-permute-start | bytes 3538952 | tf_op jit(solution)/shard_map/ppermute | solution.py:675
  374.0 1.2 copy-start.11
  374.0 1.6 copy-start.12
  375.6 2.8 copy-start.21
  375.6 10.7 %collective-permute-start.41 = (bf16[48,12288]{1,0:T(8,128)(2,1)}, bf16[48,12288]{1,0:T(8,128)(2,1)}, u32[]{:S(2)}, u32[]{:S(2)}) collective-permute-start(bf16[48,12288]{1,0:T(8,128)(2,1)} %get-tuple-element.147), channel_id=1, source_target_pairs={{0,1},{1,0},{2,3},{3,2},{4,5},{5,4},{6,7},{7,6},{8,9},{9,8},{10,11... | collective-permute-start | bytes 3538952 | tf_op jit(solution)/shard_map/ppermute | solution.py:672
  375.6 30.5 %collective-permute-start.42 = (bf16[48,12288]{1,0:T(8,128)(2,1)}, bf16[48,12288]{1,0:T(8,128)(2,1)}, u32[]{:S(2)}, u32[]{:S(2)}) collective-permute-start(bf16[48,12288]{1,0:T(8,128)(2,1)} %get-tuple-element.148), channel_id=1, source_target_pairs={{0,2},{1,3},{2,4},{3,5},{4,6},{5,7},{6,0},{7,1},{8,10},{9,11},{10,... | collective-permute-start | bytes 3538952 | tf_op jit(solution)/shard_map/ppermute | solution.py:675
  375.8 34.8 %collective-permute-start.43 = (bf16[12,3,64,256]{3,2,1,0:T(8,128)(2,1)}, bf16[12,3,64,256]{3,2,1,0:T(8,128)(2,1)S(1)}, u32[]{:S(2)}, u32[]{:S(2)}) collective-permute-start(bf16[12,3,64,256]{3,2,1,0:T(8,128)(2,1)} %get-tuple-element.150), channel_id=1, source_target_pairs={{0,8},{8,0},{16,24},{24,16},{1,9},{9,1},{17,25},{25,17},{2,10},{10... | collective-permute-start | bytes 3538952 | tf_op jit(solution)/shard_map/ppermute | solution.py:685
  377.3 34.5 %collective-permute-start.44 = (bf16[12,3,64,256]{3,2,1,0:T(8,128)(2,1)}, bf16[12,3,64,256]{3,2,1,0:T(8,128)(2,1)S(1)}, u32[]{:S(2)}, u32[]{:S(2)}) collective-permute-start(bf16[12,3,64,256]{3,2,1,0:T(8,128)(2,1)} %get-tuple-element.151), channel_id=1, source_target_pairs={{0,16},{8,24},{16,0},{24,8},{1,17},{9,25},{17,1},{25,9},{2,18},{10... | collective-permute-start | bytes 3538952 | tf_op jit(solution)/shard_map/ppermute | solution.py:685
  410.5 1.2 copy-start.22
  412.8 35.8 %collective-permute-start.47 = (bf16[12,4,64,256]{3,2,1,0:T(8,128)(2,1)}, bf16[12,4,64,256]{3,2,1,0:T(8,128)(2,1)S(1)}, u32[]{:S(2)}, u32[]{:S(2)}) collective-permute-start(bf16[12,4,64,256]{3,2,1,0:T(8,128)(2,1)} %get-tuple-element.156), channel_id=1, source_target_pairs={{0,8},{8,0},{16,24},{24,16},{1,9},{9,1},{17,25},{25,17},{2,10},{10... | collective-permute-start | bytes 4718600 | tf_op jit(solution)/shard_map/ppermute | solution.py:685
  413.5 35.8 %collective-permute-start.48 = (bf16[12,4,64,256]{3,2,1,0:T(8,128)(2,1)}, bf16[12,4,64,256]{3,2,1,0:T(8,128)(2,1)S(1)}, u32[]{:S(2)}, u32[]{:S(2)}) collective-permute-start(bf16[12,4,64,256]{3,2,1,0:T(8,128)(2,1)} %get-tuple-element.157), channel_id=1, source_target_pairs={{0,16},{8,24},{16,0},{24,8},{1,17},{9,25},{17,1},{25,9},{2,18},{10... | collective-permute-start | bytes 4718600 | tf_op jit(solution)/shard_map/ppermute | solution.py:685
  414.5 15.6 %collective-permute-start.45 = (bf16[48,12288]{1,0:T(8,128)(2,1)}, bf16[48,12288]{1,0:T(8,128)(2,1)}, u32[]{:S(2)}, u32[]{:S(2)}) collective-permute-start(bf16[48,12288]{1,0:T(8,128)(2,1)} %get-tuple-element.152), channel_id=1, source_target_pairs={{0,1},{1,0},{2,3},{3,2},{4,5},{5,4},{6,7},{7,6},{8,9},{9,8},{10,11... | collective-permute-start | bytes 3538952 | tf_op jit(solution)/shard_map/ppermute | solution.py:672
  414.5 30.5 %collective-permute-start.46 = (bf16[48,12288]{1,0:T(8,128)(2,1)}, bf16[48,12288]{1,0:T(8,128)(2,1)}, u32[]{:S(2)}, u32[]{:S(2)}) collective-permute-start(bf16[48,12288]{1,0:T(8,128)(2,1)} %get-tuple-element.153), channel_id=1, source_target_pairs={{0,2},{1,3},{2,4},{3,5},{4,6},{5,7},{6,0},{7,1},{8,10},{9,11},{10,... | collective-permute-start | bytes 3538952 | tf_op jit(solution)/shard_map/ppermute | solution.py:675
  448.5 1.2 copy-start.28
  (22 other events, 21.1 us)
Sparse Core Ops, SparseCore 0:
  379.8 30.6 reduce-scatter.3

commit v5 on v4

--- a/solution.py
+++ b/solution.py
@@ -787,11 +787,10 @@
 
     def send_round(parts, moving, waits, give=()):
         here = [part[1] for part in parts]
-        sent = fence(here + moving + list(give), waits)
+        sent = fence(here + list(give), waits + moving)
         got = [over_dp(value, way) for value, (_, way) in zip(sent, groups)]
-        rest = sent[len(here) :]
-        moved = [shifted(value, 1) for value in rest[: len(moving)]]
-        return sent[0], got, moved, [swapped(value) for value in rest[len(moving) :]]
+        moved = [shifted(value, 1) for value in moving]
+        return sent[0], got, moved, [swapped(value) for value in sent[len(here) :]]
 
     down_all = run_gradients(
         down_kernel, (down_index, live, quarters), y_chunks, [], hidden, [], 0, down_groups,
@@ -809,13 +808,11 @@
     )
     if len(down_parts) > 1:
         here = [part[1] for part in down_parts[1]]
-        token, *sent = fence([back_low] + here + moving, down_got[0])
-        back_low, moving = token, sent[len(here) :]
+        token, *sent = fence([back_low] + here, down_got[0] + moving)
+        back_low = token
         down_got.append([over_dp(value, way) for value, (_, way) in zip(sent, groups)])
-    up_parts, waits = [], [token]
-    for start in starts:
-        up_parts.append(up_part(start, waits))
-        waits = [up_parts[-1][0][0]]
+    up_parts = [up_part(starts[0], [token])]
+    waits = [up_parts[0][0][0]]
     if by_ring:
         low = by_core([back_low[n * rows : (n + 1) * rows] for n in range(mp_size)])
         chip_sum = jnp.concatenate(low[:chips], 0) + swapped(jnp.concatenate(low[chips:], 0))
@@ -828,6 +825,8 @@
         up_parts[0], moving, down_got[-1] + waits + [back_low], give
     )
     up_got = [got]
+    if len(starts) > 1:
+        up_parts.append(up_part(starts[1], [token]))
     if by_ring:
         mixed_given[0] = given[0]
     input_parts = list(
@@ -844,7 +843,7 @@
             preferred_element_type=F32,
         ).astype(BF16)
     down_onward = pass_on(down_parts, down_got)
-    waits, give = up_got[0] + down_onward + [low_in_part], []
+    waits, give = up_got[0], []
     if by_ring:
         input_parts = by_core(input_parts)
         mixed = add_round(mixed_parts, mixed_given, chips, moving[0])
@@ -860,14 +859,15 @@
         moving = [add_round(input_parts, input_given, 2, moving[0])]
 
     def last_round(onward, moving, waits, give=()):
-        sent = fence(onward + moving + list(give), waits)
+        sent = fence(onward + list(give), waits + moving)
         last = [over_dp(value, 3 - way) for value, (_, way) in zip(sent, groups)]
-        rest = sent[len(groups) :]
-        moved = [shifted(value, 1) for value in rest[: len(moving)]]
-        return last, moved, [swapped(value) for value in rest[len(moving) :]]
+        moved = [shifted(value, 1) for value in moving]
+        return last, moved, [swapped(value) for value in sent[len(groups) :]]
 
     give = [input_parts[chips + 3]] if by_ring else []
-    down_last, moving, given = last_round(down_onward, moving, up_got[-1], give)
+    down_last, moving, given = last_round(
+        down_onward, moving, up_got[-1] + [low_in_part], give
+    )
     if by_ring:
         input_given.append(given[0])
         moving = [add_round(input_parts, input_given, 3, moving[0])]

time: 466 us -> 466 us (level)
  waiting for transfers between devices: 198 us -> 206 us
  starting transfers between devices: 33.4 us -> 26.4 us
    ppermute x1, waiting for transfers between devices: 2.88 us -> 16.2 us  [sum_rows_in_pairs(): got = lax.ppermute(pair_sum.astype(BF16), 'mp', far).astype(F32)]
    ppermute x15, waiting for transfers between devices: 181 us -> 172 us  [shifted(): lax.ppermute(piece, 'mp', [(i, (i + 2 * by) % mp_size) for i in range(mp_...]
    ppermute x15, starting transfers between devices: 13.2 us -> 7.21 us  [shifted(): lax.ppermute(piece, 'mp', [(i, (i + 2 * by) % mp_size) for i in range(mp_...]
where the time goes in v5:
time: 466 us; the launch traced here: 464 us
  waiting for transfers between devices  206 us (44%)
  Pallas kernels  178 us (38%)
  local copies, waits for them, and re-layouts  34.3 us (7%)
  starting transfers between devices  26.4 us (6%)
  between operations  14.5 us (3%)
  other arithmetic  5.15 us (1%)
    ppermute x15, waiting for transfers between devices, shifted(): lax.ppermute(piece, 'mp', [(i, (i + 2 * by) % mp_size) for i in range(mp_...  172 us
    pallas_call x3, Pallas kernels, run_gradients(): pl.pallas_call(functools.partial(kernel, len(chunks), len(waits), first,...  42.8 us
    unnamed x75, local copies, waits for them, and re-layouts  23.9 us
    pallas_call x8, Pallas kernels, run_add(): pl.pallas_call(add_kernel, out_shape=shape((rows, width), BF16), grid=(st...  23.1 us
    pallas_call x1, Pallas kernels, run_hidden(): pl.pallas_call(functools.partial(hidden_kernel, len(chunks), len(waits),...  20 us
    pallas_call x1, Pallas kernels, run_spread(): pl.pallas_call(functools.partial(spread_kernel, len(out_shapes), len(wait...  17.7 us
    pallas_call x1, Pallas kernels, run_back(): pl.pallas_call(functools.partial(back_kernel, len(chunks), len(waits), pe...  17.4 us
    pallas_call x1, Pallas kernels, run_pieces(): pl.pallas_call(functools.partial(pieces_kernel, len(out_shapes), len(wait...  16.5 us
  transfers between devices with their start and end apart: 50, of which 23 were waited for; matrix products, arithmetic and copies ran while one was open for 4% of the time, Pallas kernels for 37%

profile of v5, /device:TPU:0, one launch (start us, length us, event | category | flops | bytes accessed | tf_op | source)
XLA Modules:
  0.0 464.2 jit_solution(14972829947857995603)
XLA Ops:
  7.2 3.1 collective-permute-start.1
  10.8 27.7 %collective-permute-done.1.refs_1_.refs_5_ = bf16[48,12288]{1,0:T(8,128)(2,1)S(1)} collective-permute-done((bf16[48,12288]{1,0:T(8,128)(2,1)}, bf16[48,12288]{1,0:T(8,128)(2,1)S(1)}, u32[]{:S(2)}, u32[]{:S(2)}) %collective-permute-start.1) | collective-permute-done | bytes 1179680 | tf_op jit(solution)/shard_map/ppermute | solution.py:675
  39.0 3.7 collective-permute-done.6.refs_4_.refs_9_
  42.7 1.2 copy-done.27
  44.0 1.0 copy-done.6
  45.0 23.7 %collective-permute-done.2.refs_0_ = bf16[48,12288]{1,0:T(8,128)(2,1)S(1)} collective-permute-done((bf16[48,12288]{1,0:T(8,128)(2,1)S(1)}, bf16[48,12288]{1,0:T(8,128)(2,1)S(1)}, u32[]{:S(2)}, u32[]{:S(2)}) %collective-permute-start.2) | collective-permute-done | bytes 1179680 | tf_op jit(solution)/shard_map/ppermute | solution.py:675
  70.3 2.4 collective-permute-done.8.refs_10_.refs_5_
  72.7 27.7 %collective-permute-done.7.refs_3_.refs_7_.refs_6_ = bf16[48,12288]{1,0:T(8,128)(2,1)S(1)} collective-permute-done((bf16[48,12288]{1,0:T(8,128)(2,1)}, bf16[48,12288]{1,0:T(8,128)(2,1)S(1)}, u32[]{:S(2)}, u32[]{:S(2)}) %collective-permute-start.7) | collective-permute-done | bytes 1179680 | tf_op jit(solution)/shard_map/ppermute | solution.py:675
  100.5 1.1 copy-done.2
  101.5 3.7 low_part.1
  106.2 2.0 collective-permute-start.9
  108.2 21.3 %collective-permute-done.11 = bf16[192,256]{1,0:T(8,128)(2,1)S(1)} collective-permute-done((bf16[192,256]{1,0:T(8,128)(2,1)S(1)}, bf16[192,256]{1,0:T(8,128)(2,1)S(1)}, u32[]{:S(2)}, u32[]{:S(2)}) %collective-permute-start.11) | collective-permute-done | bytes 98336 | tf_op jit(solution)/shard_map/ppermute | solution.py:675
  130.1 3.6 collective-permute-done.10
  133.8 1.6 add_convert_fusion.refs_1_
  142.2 1.0 copy-done.8
  143.2 20.0 %hidden.1 = (bf16[24,384,256]{2,1,0:T(8,128)(2,1)}, f32[24,384,256]{2,1,0:T(8,128)}) custom-call(s32[72]{0:T(128)} %reshape.19.up_ref, bf16[48,12288]{1,0:T(8,128)(2,1)} %refs_0_.13, bf16[48,12288]{1,0:T(8,128)(2,1)} %copy-done.1, bf16[48,12288]{1,0:T(8,128)(2,1)} %fence.11.refs_2_.refs_6_, bf16[48,12288]{1,0:T(8,128)(2,1)} %copy-done.5, ...), custom_call_target="tpu_custom_call" | custom-call | flops 1 | bytes 1 | tf_op jit(solution)/shard_map/hidden/pallas_call | solution.py:303
  163.3 2.6 collective-permute-done.12.refs_0_
  165.9 1.0 copy-done.16
  168.9 16.5 %pieces.1 = (bf16[48,12288]{1,0:T(8,128)(2,1)}, bf16[48,12288]{1,0:T(8,128)(2,1)}, bf16[48,12288]{1,0:T(8,128)(2,1)}, bf16[48,12288]{1,0:T(8,128)(2,1)}, bf16[48...) custom-call(s32[72]{0:T(128)} %reshape.20.down_ref, ...), custom_call_target="tpu_custom_call" | custom-call | flops 1 | bytes 1 | tf_op jit(solution)/shard_map/pieces/pallas_call | solution.py:331
  185.5 11.8 %collective-permute-done.16.refs_0_ = bf16[48,12288]{1,0:T(8,128)(2,1)S(1)} collective-permute-done((bf16[48,12288]{1,0:T(8,128)(2,1)}, bf16[48,12288]{1,0:T(8,128)(2,1)S(1)}, u32[]{:S(2)}, u32[]{:S(2)}) %collective-permute-start.16) | collective-permute-done | bytes 1179680 | tf_op jit(solution)/shard_map/ppermute | solution.py:675
  197.3 1.0 copy-done.17
  199.4 2.0 collective-permute-done.19.refs_3_.refs_1_
  201.4 1.0 copy-done.24
  202.4 2.6 add_rows.8
  206.5 16.9 %down_kernel.1 = (f32[4,3,64,256]{3,2,1,0:T(8,128)}, bf16[2,4,3,64,256]{4,3,2,1,0:T(8,128)(2,1)}, bf16[4,3,64,256]{3,2,1,0:T(8,128)(2,1)}, f32[4,3,64,256]{3,2,1...) custom-call(s32[72]{0:T(128)} %reshape.20.down_ref, ...), custom_call_target="tpu_custom_call" | custom-call | flops 1 | bytes 1 | tf_op jit(solution)/shard_map/down_kernel/pallas_call | solution.py:403
  223.4 1.0 copy-done.25
  224.4 1.5 collective-permute-start.23
  225.9 1.5 collective-permute-start.22
  227.5 17.4 %back.1 = (bf16[24,384,256]{2,1,0:T(8,128)(2,1)}, f32[384,256]{1,0:T(8,128)}) custom-call(s32[72]{0:T(128)} %reshape.20.down_ref, s32[24]{0:T(128)} %dynamic_slice.11.live_ref, bf16[48,12288]{1,0:T(8,128)(2,1)} %refs_0_.10, bf16[48,12288]{1,0:T(8,128)(2,1)} %fence.12.refs_1_, bf16[48,12288]{1,0:T(8,128)(2,1)} %get-tuple-element.83.refs_2_, ...), custom_call_target="tpu_custom_call" | custom-call | flops 1 | bytes 1 | tf_op jit(solution)/shard_map/back/pallas_call | solution.py:356
  245.9 3.0 add_rows.9.refs_5_
  254.3 2.0 collective-permute-start.31
  256.2 13.0 %up_kernel.2 = (f32[6,4,64,256]{3,2,1,0:T(8,128)}, bf16[2,6,4,64,256]{4,3,2,1,0:T(8,128)(2,1)}, bf16[6,4,64,256]{3,2,1,0:T(8,128)(2,1)}, f32[6,4,64,256]{3,2,1,0...) custom-call(s32[72]{0:T(128)} %reshape.19.up_ref, s32[4]{0:T(128)} %iota_xor_fusion.quarter_ref, ...), custom_call_target="tpu_custom_call" | custom-call | flops 1 | bytes 1 | tf_op jit(solution)/shard_map/up_kernel/pallas_call | solution.py:403
  271.7 2.7 collective-permute-start.29
  274.5 16.2 %collective-permute-done.29 = bf16[192,256]{1,0:T(8,128)(2,1)S(1)} collective-permute-done((bf16[192,256]{1,0:T(8,128)(2,1)S(1)}, bf16[192,256]{1,0:T(8,128)(2,1)S(1)}, u32[]{:S(2)}, u32[]{:S(2)}) %collective-permute-start.29) | collective-permute-done | bytes 98336 | tf_op jit(solution)/shard_map/ppermute | solution.py:714
  290.8 1.3 collective-permute-done.30
  292.8 3.0 add_rows.10.refs_7_
  295.8 1.1 copy-done.13
  298.4 1.5 collective-permute-start.34
  299.9 17.7 %spread.1 = (bf16[48,12288]{1,0:T(8,128)(2,1)}, bf16[48,12288]{1,0:T(8,128)(2,1)}, bf16[48,12288]{1,0:T(8,128)(2,1)}, bf16[48,12288]{1,0:T(8,128)(2,1)}, bf16[48...) custom-call(s32[72]{0:T(128)} %reshape.19.up_ref, ...), custom_call_target="tpu_custom_call" | custom-call | flops 1 | bytes 1 | tf_op jit(solution)/shard_map/spread/pallas_call | solution.py:430
  317.6 12.9 %up_kernel.3 = (f32[6,4,64,256]{3,2,1,0:T(8,128)}, bf16[2,6,4,64,256]{4,3,2,1,0:T(8,128)(2,1)}, bf16[6,4,64,256]{3,2,1,0:T(8,128)(2,1)}, f32[6,4,64,256]{3,2,1,0...) custom-call(s32[72]{0:T(128)} %reshape.19.up_ref, s32[4]{0:T(128)} %iota_xor_fusion.quarter_ref, ...), custom_call_target="tpu_custom_call" | custom-call | flops 1 | bytes 1 | tf_op jit(solution)/shard_map/up_kernel/pallas_call | solution.py:403
  330.5 3.0 add_rows.11.refs_6_
  335.9 1.5 collective-permute-start.36
  339.1 2.6 add_rows.12
  341.6 3.6 low_in_part.1.refs_5_
  345.2 2.9 pass_on.6.refs_0_
  348.1 2.9 pass_on.7.refs_1_
  351.0 20.8 %collective-permute-done.40.refs_2_ = bf16[48,12288]{1,0:T(8,128)(2,1)} collective-permute-done((bf16[48,12288]{1,0:T(8,128)(2,1)}, bf16[48,12288]{1,0:T(8,128)(2,1)}, u32[]{:S(2)}, u32[]{:S(2)}) %collective-permute-start.40) | collective-permute-done | bytes 1179680 | tf_op jit(solution)/shard_map/ppermute | solution.py:675
  371.8 3.0 add_rows.13.refs_6_
  374.8 1.2 copy-done.11
  376.5 1.1 collective-permute-start.41
  377.6 1.2 collective-permute-start.42
  378.8 1.2 copy.56
  380.0 3.4 pass_on.4.refs_0_
  383.4 3.4 pass_on.5.refs_1_
  386.8 17.3 %collective-permute-done.44.refs_2_ = bf16[48,12288]{1,0:T(8,128)(2,1)} collective-permute-done((bf16[48,12288]{1,0:T(8,128)(2,1)}, bf16[48,12288]{1,0:T(8,128)(2,1)}, u32[]{:S(2)}, u32[]{:S(2)}) %collective-permute-start.44) | collective-permute-done | bytes 1179680 | tf_op jit(solution)/shard_map/ppermute | solution.py:675
  404.1 3.0 add_rows.14.refs_5_
  407.1 4.3 collective-permute-done.41.refs_3_.refs_8_
  414.2 1.5 collective-permute-start.48
  415.8 1.1 copy.57
  417.8 6.8 %sums.2.refs_0_ = f32[24,4,64,256]{3,2,1,0:T(8,128)} custom-call(f32[6,4,64,256]{3,2,1,0:T(8,128)} %get-tuple-element.114.refs_1_.refs_5_.refs_0_, bf16[2,6,4,64,256]{4,3,2,1,0:T(8,128)(2,1)} %copy-done.10, f32[6,4,64,256]{3,2,1,0:T(8,128)} %get-tuple-element.145.refs_2_, bf16[2,6,4,64,256]{4,3,2,1,0:T(8,128)(2,1)} %copy-done.9, ...), custom_call_target="tpu_custom_call" | custom-call | flops 1 | bytes 1 | tf_op jit(solution)/shard_map/sums/pallas_call | solution.py:592
  424.6 6.6 %sums.3 = f32[24,3,64,256]{3,2,1,0:T(8,128)} custom-call(f32[4,3,64,256]{3,2,1,0:T(8,128)} %get-tuple-element.151.refs_0_, bf16[2,4,3,64,256]{4,3,2,1,0:T(8,128)(2,1)} %copy-done.20, f32[4,3,64,256]{3,2,1,0:T(8,128)} %get-tuple-element.152.refs_2_, bf16[2,4,3,64,256]{4,3,2,1,0:T(8,128)(2,1)} %copy-done.19, f32[8,3,64,256]{3,2,1,0:T(8,128)} %get-tuple-element.153.refs_4_, ...), custom_call_target="tpu_custom_call" | custom-call | flops 1 | bytes 1 | tf_op jit(solution)/shard_map/sums/pallas_call | solution.py:592
  431.3 15.0 %collective-permute-done.46.refs_2_ = bf16[48,12288]{1,0:T(8,128)(2,1)} collective-permute-done((bf16[48,12288]{1,0:T(8,128)(2,1)S(1)}, bf16[48,12288]{1,0:T(8,128)(2,1)}, u32[]{:S(2)}, u32[]{:S(2)}) %collective-permute-start.46) | collective-permute-done | bytes 1179680 | tf_op jit(solution)/shard_map/ppermute | solution.py:675
  446.3 3.0 add_rows.15
  450.5 6.8 %finish.1 = (f32[24,3,64,256]{3,2,1,0:T(8,128)}, f32[64,6144]{1,0:T(8,128)}) custom-call(f32[24,4,64,256]{3,2,1,0:T(8,128)} %sums.2.refs_0_, bf16[12,4,64,256]{3,2,1,0:T(8,128)(2,1)} %copy-done.29, bf16[12,4,64,256]{3,2,1,0:T(8,128)(2,1)} %collective-permute-done.48.refs_2_), custom_call_target="tpu_custom_call" | custom-call | flops 1 | bytes 1 | tf_op jit(solution)/shard_map/finish/pallas_call | solution.py:622
  (181 shorter events, 36.1 us)
Async XLA Ops:
  7.2 408.6 %reduce-scatter.4.cloned.1.call-start = ((), (), s32[]{:S(2)}) async-start(), calls=%async_computation.1 | async-start | bytes 983040
  7.2 31.3 %collective-permute-start.1 = (bf16[48,12288]{1,0:T(8,128)(2,1)}, bf16[48,12288]{1,0:T(8,128)(2,1)S(1)}, u32[]{:S(2)}, u32[]{:S(2)}) collective-permute-start(bf16[48,12288]{1,0:T(8,128)(2,1)} %refs_0_.13), channel_id=1, source_target_pairs={{0,2},{1,3},{2,4},{3,5},{4,6},{5,7},{6,0},{7,1},{8,10},{9,11},{10,... | collective-permute-start | bytes 3538952 | tf_op jit(solution)/shard_map/ppermute | solution.py:675
  10.3 32.4 %collective-permute-start.3 = (bf16[48,12288]{1,0:T(8,128)(2,1)}, bf16[48,12288]{1,0:T(8,128)(2,1)S(1)}, u32[]{:S(2)}, u32[]{:S(2)}) collective-permute-start(bf16[48,12288]{1,0:T(8,128)(2,1)} %refs_0_.13), channel_id=1, source_target_pairs={{0,1},{1,0},{2,3},{3,2},{4,5},{5,4},{6,7},{7,6},{8,9},{9,8},{10,11... | collective-permute-start | bytes 3538952 | tf_op jit(solution)/shard_map/ppermute | solution.py:672
  10.3 32.4 %collective-permute-start.5 = (bf16[48,12288]{1,0:T(8,128)(2,1)}, bf16[48,12288]{1,0:T(8,128)(2,1)S(1)}, u32[]{:S(2)}, u32[]{:S(2)}) collective-permute-start(bf16[48,12288]{1,0:T(8,128)(2,1)} %refs_0_.10), channel_id=1, source_target_pairs={{0,1},{1,0},{2,3},{3,2},{4,5},{5,4},{6,7},{7,6},{8,9},{9,8},{10,11... | collective-permute-start | bytes 3538952 | tf_op jit(solution)/shard_map/ppermute | solution.py:672
  38.5 62.0 %copy-start.1 = (bf16[48,12288]{1,0:T(8,128)(2,1)}, bf16[48,12288]{1,0:T(8,128)(2,1)S(1)}, u32[]{:S(2)}) copy-start(bf16[48,12288]{1,0:T(8,128)(2,1)S(1)} %collective-permute-done.1.refs_1_.refs_5_) | copy-start | bytes 3538948
  38.5 4.2 collective-permute-start.4
  38.5 30.2 %collective-permute-start.2 = (bf16[48,12288]{1,0:T(8,128)(2,1)S(1)}, bf16[48,12288]{1,0:T(8,128)(2,1)S(1)}, u32[]{:S(2)}, u32[]{:S(2)}) collective-permute-start(bf16[48,12288]{1,0:T(8,128)(2,1)S(1)} %collective-permute-done.1.refs_1_.refs_5_), channel_id=1, source_target_pairs={{0,2},{1,3},{2,4},{3,5},{4,6},{5,7},{6,0},{7,1},{8,10},{9,11},{10,... | collective-permute-start | bytes 3538952 | tf_op jit(solution)/shard_map/ppermute | solution.py:675
  38.5 4.2 collective-permute-start.6
  42.7 1.3 copy-start.27
  42.7 26.0 %copy-start.3 = (bf16[48,12288]{1,0:T(8,128)(2,1)}, bf16[48,12288]{1,0:T(8,128)(2,1)S(1)}, u32[]{:S(2)}) copy-start(bf16[48,12288]{1,0:T(8,128)(2,1)S(1)} %collective-permute-done.5.refs_3_.refs_2_.refs_9_) | copy-start | bytes 3538948
  42.7 1.3 copy-start.5
  69.7 3.1 collective-permute-start.8
  69.7 30.8 %collective-permute-start.7 = (bf16[48,12288]{1,0:T(8,128)(2,1)}, bf16[48,12288]{1,0:T(8,128)(2,1)S(1)}, u32[]{:S(2)}, u32[]{:S(2)}) collective-permute-start(bf16[48,12288]{1,0:T(8,128)(2,1)} %fence.11.refs_2_.refs_6_), channel_id=1, source_target_pairs={{0,2},{1,3},{2,4},{3,5},{4,6},{5,7},{6,0},{7,1},{8,10},{9,11},{10,... | collective-permute-start | bytes 3538952 | tf_op jit(solution)/shard_map/ppermute | solution.py:675
  69.7 65.7 %collective-permute-start = (bf16[48,12288]{1,0:T(8,128)(2,1)}, bf16[48,12288]{1,0:T(8,128)(2,1)}, u32[]{:S(2)}, u32[]{:S(2)}) collective-permute-start(bf16[48,12288]{1,0:T(8,128)(2,1)} %refs_0_.10), channel_id=1, source_target_pairs={{0,2},{1,3},{2,4},{3,5},{4,6},{5,7},{6,0},{7,1},{8,10},{9,11},{10,... | collective-permute-start | bytes 3538952 | tf_op jit(solution)/shard_map/ppermute | solution.py:675
  72.7 27.7 %copy-start.4 = (bf16[48,12288]{1,0:T(8,128)(2,1)}, bf16[48,12288]{1,0:T(8,128)(2,1)S(1)}, u32[]{:S(2)}) copy-start(bf16[48,12288]{1,0:T(8,128)(2,1)S(1)} %collective-permute-done.8.refs_10_.refs_5_) | copy-start | bytes 3538948
  106.1 23.4 %collective-permute-start.11 = (bf16[192,256]{1,0:T(8,128)(2,1)S(1)}, bf16[192,256]{1,0:T(8,128)(2,1)S(1)}, u32[]{:S(2)}, u32[]{:S(2)}) collective-permute-start(bf16[192,256]{1,0:T(8,128)(2,1)S(1)} %convert_element_type.33), channel_id=1, source_target_pairs={{0,6},{1,7},{2,0},{3,1},{4,2},{5,3},{6,4},{7,5},{8,14},{9,15},{10,... | collective-permute-start | bytes 294920 | tf_op jit(solution)/shard_map/ppermute | solution.py:675
  106.2 23.9 %collective-permute-start.9 = (bf16[192,256]{1,0:T(8,128)(2,1)S(1)}, bf16[192,256]{1,0:T(8,128)(2,1)S(1)}, u32[]{:S(2)}, u32[]{:S(2)}) collective-permute-start(bf16[192,256]{1,0:T(8,128)(2,1)S(1)} %convert_element_type.33), channel_id=1, source_target_pairs={{0,2},{1,3},{2,4},{3,5},{4,6},{5,7},{6,0},{7,1},{8,10},{9,11},{10,... | collective-permute-start | bytes 294920 | tf_op jit(solution)/shard_map/ppermute | solution.py:675
  108.2 25.6 %collective-permute-start.10 = (bf16[192,256]{1,0:T(8,128)(2,1)S(1)}, bf16[192,256]{1,0:T(8,128)(2,1)S(1)}, u32[]{:S(2)}, u32[]{:S(2)}) collective-permute-start(bf16[192,256]{1,0:T(8,128)(2,1)S(1)} %convert_element_type.33), channel_id=1, source_target_pairs={{0,4},{1,5},{2,6},{3,7},{4,0},{5,1},{6,2},{7,3},{8,12},{9,13},{10,... | collective-permute-start | bytes 294920 | tf_op jit(solution)/shard_map/ppermute | solution.py:675
  108.2 34.0 %collective-permute-start.13 = (bf16[48,12288]{1,0:T(8,128)(2,1)}, bf16[48,12288]{1,0:T(8,128)(2,1)S(1)}, u32[]{:S(2)}, u32[]{:S(2)}) collective-permute-start(bf16[48,12288]{1,0:T(8,128)(2,1)} %copy-done.2), channel_id=1, source_target_pairs={{0,1},{1,0},{2,3},{3,2},{4,5},{5,4},{6,7},{7,6},{8,9},{9,8},{10,11... | collective-permute-start | bytes 3538952 | tf_op jit(solution)/shard_map/ppermute | solution.py:672
  135.4 27.8 %collective-permute-start.15 = (bf16[48,12288]{1,0:T(8,128)(2,1)}, bf16[48,12288]{1,0:T(8,128)(2,1)S(1)}, u32[]{:S(2)}, u32[]{:S(2)}) collective-permute-start(bf16[48,12288]{1,0:T(8,128)(2,1)} %fence.12.refs_1_), channel_id=1, source_target_pairs={{0,1},{1,0},{2,3},{3,2},{4,5},{5,4},{6,7},{7,6},{8,9},{9,8},{10,11... | collective-permute-start | bytes 3538952 | tf_op jit(solution)/shard_map/ppermute | solution.py:672
  135.5 30.4 %collective-permute-start.12 = (bf16[48,12288]{1,0:T(8,128)(2,1)}, bf16[48,12288]{1,0:T(8,128)(2,1)S(1)}, u32[]{:S(2)}, u32[]{:S(2)}) collective-permute-start(bf16[48,12288]{1,0:T(8,128)(2,1)} %fence.12.refs_1_), channel_id=1, source_target_pairs={{0,2},{1,3},{2,4},{3,5},{4,6},{5,7},{6,0},{7,1},{8,10},{9,11},{10,... | collective-permute-start | bytes 3538952 | tf_op jit(solution)/shard_map/ppermute | solution.py:675
  135.6 4.3 collective-permute-start.14
  163.3 2.6 copy-start.7
  166.9 18.6 %collective-permute-start.17 = (bf16[48,12288]{1,0:T(8,128)(2,1)}, bf16[48,12288]{1,0:T(8,128)(2,1)S(1)}, u32[]{:S(2)}, u32[]{:S(2)}) collective-permute-start(bf16[48,12288]{1,0:T(8,128)(2,1)} %get-tuple-element.83.refs_2_), channel_id=1, source_target_pairs={{0,1},{1,0},{2,3},{3,2},{4,5},{5,4},{6,7},{7,6},{8,9},{9,8},{10,11... | collective-permute-start | bytes 3538952 | tf_op jit(solution)/shard_map/ppermute | solution.py:672
  166.9 30.4 %collective-permute-start.16 = (bf16[48,12288]{1,0:T(8,128)(2,1)}, bf16[48,12288]{1,0:T(8,128)(2,1)S(1)}, u32[]{:S(2)}, u32[]{:S(2)}) collective-permute-start(bf16[48,12288]{1,0:T(8,128)(2,1)} %get-tuple-element.83.refs_2_), channel_id=1, source_target_pairs={{0,2},{1,3},{2,4},{3,5},{4,6},{5,7},{6,0},{7,1},{8,10},{9,11},{10,... | collective-permute-start | bytes 3538952 | tf_op jit(solution)/shard_map/ppermute | solution.py:675
  185.5 11.8 %copy-start.15 = (bf16[48,12288]{1,0:T(8,128)(2,1)}, bf16[48,12288]{1,0:T(8,128)(2,1)S(1)}, u32[]{:S(2)}) copy-start(bf16[48,12288]{1,0:T(8,128)(2,1)S(1)} %collective-permute-done.17.refs_11_.refs_5_) | copy-start | bytes 3538948
  198.4 3.1 collective-permute-start.19
  198.4 7.2 %collective-permute-start.18 = (bf16[48,12288]{1,0:T(8,128)(2,1)}, bf16[48,12288]{1,0:T(8,128)(2,1)S(1)}, u32[]{:S(2)}, u32[]{:S(2)}) collective-permute-start(bf16[48,12288]{1,0:T(8,128)(2,1)} %get-tuple-element.94.refs_6_), channel_id=1, source_target_pairs={{0,1},{1,0},{2,3},{3,2},{4,5},{5,4},{6,7},{7,6},{8,9},{9,8},{10,11... | collective-permute-start | bytes 3538952 | tf_op jit(solution)/shard_map/ppermute | solution.py:672
  198.9 24.5 %collective-permute-start.20 = (bf16[48,12288]{1,0:T(8,128)(2,1)}, bf16[48,12288]{1,0:T(8,128)(2,1)}, u32[]{:S(2)}, u32[]{:S(2)}) collective-permute-start(bf16[48,12288]{1,0:T(8,128)(2,1)} %get-tuple-element.98), channel_id=1, source_target_pairs={{0,1},{1,0},{2,3},{3,2},{4,5},{5,4},{6,7},{7,6},{8,9},{9,8},{10,11... | collective-permute-start | bytes 3538952 | tf_op jit(solution)/shard_map/ppermute | solution.py:672
  198.9 24.5 %collective-permute-start.21 = (bf16[48,12288]{1,0:T(8,128)(2,1)}, bf16[48,12288]{1,0:T(8,128)(2,1)S(1)}, u32[]{:S(2)}, u32[]{:S(2)}) collective-permute-start(bf16[48,12288]{1,0:T(8,128)(2,1)} %get-tuple-element.99), channel_id=1, source_target_pairs={{0,1},{1,0},{2,3},{3,2},{4,5},{5,4},{6,7},{7,6},{8,9},{9,8},{10,11... | collective-permute-start | bytes 3538952 | tf_op jit(solution)/shard_map/ppermute | solution.py:672
  205.0 39.9 %collective-permute-start.24 = (bf16[48,12288]{1,0:T(8,128)(2,1)}, bf16[48,12288]{1,0:T(8,128)(2,1)S(1)}, u32[]{:S(2)}, u32[]{:S(2)}) collective-permute-start(bf16[48,12288]{1,0:T(8,128)(2,1)} %add_rows.8), channel_id=1, source_target_pairs={{0,2},{1,3},{2,4},{3,5},{4,6},{5,7},{6,0},{7,1},{8,10},{9,11},{10,... | collective-permute-start | bytes 3538952 | tf_op jit(solution)/shard_map/ppermute | solution.py:675
  224.4 24.5 %collective-permute-start.23 = (bf16[2,4,3,64,256]{4,3,2,1,0:T(8,128)(2,1)}, bf16[2,4,3,64,256]{4,3,2,1,0:T(8,128)(2,1)S(1)}, u32[]{:S(2)}, u32[]{:S(2)}) collective-permute-start(bf16[2,4,3,64,256]{4,3,2,1,0:T(8,128)(2,1)} %get-tuple-element.105), channel_id=1, source_target_pairs={{0,8},{8,0},{16,24},{24,16},{1,9},{9,1},{17,25},{25,17},{2,10},{10... | collective-permute-start | bytes 2359304 | tf_op jit(solution)/shard_map/ppermute | solution.py:685
  225.9 23.0 %collective-permute-start.22 = (bf16[2,4,3,64,256]{4,3,2,1,0:T(8,128)(2,1)}, bf16[2,4,3,64,256]{4,3,2,1,0:T(8,128)(2,1)S(1)}, u32[]{:S(2)}, u32[]{:S(2)}) collective-permute-start(bf16[2,4,3,64,256]{4,3,2,1,0:T(8,128)(2,1)} %get-tuple-element.100.refs_11_), channel_id=1, source_target_pairs={{0,16},{8,24},{16,0},{24,8},{1,17},{9,25},{17,1},{25,9},{2,18},{10... | collective-permute-start | bytes 2359304 | tf_op jit(solution)/shard_map/ppermute | solution.py:685
  251.9 1.5 collective-permute-start.27
  252.0 43.7 %collective-permute-start.25 = (bf16[2,8,3,64,256]{4,3,2,1,0:T(8,128)(2,1)}, bf16[2,8,3,64,256]{4,3,2,1,0:T(8,128)(2,1)S(1)}, u32[]{:S(2)}, u32[]{:S(2)}) collective-permute-start(bf16[2,8,3,64,256]{4,3,2,1,0:T(8,128)(2,1)} %get-tuple-element.112), channel_id=1, source_target_pairs={{0,16},{8,24},{16,0},{24,8},{1,17},{9,25},{17,1},{25,9},{2,18},{10... | collective-permute-start | bytes 4718600 | tf_op jit(solution)/shard_map/ppermute | solution.py:685
  252.6 43.2 %collective-permute-start.26 = (bf16[2,8,3,64,256]{4,3,2,1,0:T(8,128)(2,1)}, bf16[2,8,3,64,256]{4,3,2,1,0:T(8,128)(2,1)S(1)}, u32[]{:S(2)}, u32[]{:S(2)}) collective-permute-start(bf16[2,8,3,64,256]{4,3,2,1,0:T(8,128)(2,1)} %get-tuple-element.113), channel_id=1, source_target_pairs={{0,8},{8,0},{16,24},{24,16},{1,9},{9,1},{17,25},{25,17},{2,10},{10... | collective-permute-start | bytes 4718600 | tf_op jit(solution)/shard_map/ppermute | solution.py:685
  254.2 15.1 %collective-permute-start.28 = (bf16[192,256]{1,0:T(8,128)(2,1)S(1)}, bf16[192,256]{1,0:T(8,128)(2,1)S(1)}, u32[]{:S(2)}, u32[]{:S(2)}) collective-permute-start(bf16[192,256]{1,0:T(8,128)(2,1)S(1)} %fusion.2), channel_id=1, source_target_pairs={{0,2},{1,3},{2,0},{3,1},{4,6},{5,7},{6,4},{7,5},{8,10},{9,11},{10,... | collective-permute-start | bytes 294920 | tf_op jit(solution)/shard_map/ppermute | solution.py:710
  254.3 38.5 %collective-permute-start.31 = (bf16[48,12288]{1,0:T(8,128)(2,1)}, bf16[48,12288]{1,0:T(8,128)(2,1)}, u32[]{:S(2)}, u32[]{:S(2)}) collective-permute-start(bf16[48,12288]{1,0:T(8,128)(2,1)} %add_rows.9.refs_5_), channel_id=1, source_target_pairs={{0,2},{1,3},{2,4},{3,5},{4,6},{5,7},{6,0},{7,1},{8,10},{9,11},{10,... | collective-permute-start | bytes 3538952 | tf_op jit(solution)/shard_map/ppermute | solution.py:675
  269.9 1.8 copy-start.32
  271.7 18.9 %collective-permute-start.29 = (bf16[192,256]{1,0:T(8,128)(2,1)S(1)}, bf16[192,256]{1,0:T(8,128)(2,1)S(1)}, u32[]{:S(2)}, u32[]{:S(2)}) collective-permute-start(bf16[192,256]{1,0:T(8,128)(2,1)S(1)} %get-tuple-element.174), channel_id=1, source_target_pairs={{0,4},{1,5},{2,6},{3,7},{4,0},{5,1},{6,2},{7,3},{8,12},{9,13},{10,... | collective-permute-start | bytes 294920 | tf_op jit(solution)/shard_map/ppermute | solution.py:714
  290.7 1.4 collective-permute-start.30
  295.8 1.7 copy-start.14
  297.4 36.7 %collective-permute-start.35 = (bf16[2,6,4,64,256]{4,3,2,1,0:T(8,128)(2,1)}, bf16[2,6,4,64,256]{4,3,2,1,0:T(8,128)(2,1)S(1)}, u32[]{:S(2)}, u32[]{:S(2)}) collective-permute-start(bf16[2,6,4,64,256]{4,3,2,1,0:T(8,128)(2,1)} %get-tuple-element.125), channel_id=1, source_target_pairs={{0,8},{8,0},{16,24},{24,16},{1,9},{9,1},{17,25},{25,17},{2,10},{10... | collective-permute-start | bytes 4718600 | tf_op jit(solution)/shard_map/ppermute | solution.py:685
  298.4 36.4 %collective-permute-start.34 = (bf16[2,6,4,64,256]{4,3,2,1,0:T(8,128)(2,1)}, bf16[2,6,4,64,256]{4,3,2,1,0:T(8,128)(2,1)S(1)}, u32[]{:S(2)}, u32[]{:S(2)}) collective-permute-start(bf16[2,6,4,64,256]{4,3,2,1,0:T(8,128)(2,1)} %get-tuple-element.117.refs_4_.refs_10_), channel_id=1, source_target_pairs={{0,16},{8,24},{16,0},{24,8},{1,17},{9,25},{17,1},{25,9},{2,18},{10... | collective-permute-start | bytes 4718600 | tf_op jit(solution)/shard_map/ppermute | solution.py:685
  299.9 30.6 %collective-permute-start.33 = (bf16[48,12288]{1,0:T(8,128)(2,1)}, bf16[48,12288]{1,0:T(8,128)(2,1)}, u32[]{:S(2)}, u32[]{:S(2)}) collective-permute-start(bf16[48,12288]{1,0:T(8,128)(2,1)} %add_rows.10.refs_7_), channel_id=1, source_target_pairs={{0,2},{1,3},{2,4},{3,5},{4,6},{5,7},{6,0},{7,1},{8,10},{9,11},{10,... | collective-permute-start | bytes 3538952 | tf_op jit(solution)/shard_map/ppermute | solution.py:675
  299.9 30.6 %collective-permute-start.32 = (bf16[48,12288]{1,0:T(8,128)(2,1)}, bf16[48,12288]{1,0:T(8,128)(2,1)}, u32[]{:S(2)}, u32[]{:S(2)}) collective-permute-start(bf16[48,12288]{1,0:T(8,128)(2,1)} %get-tuple-element.116), channel_id=1, source_target_pairs={{0,1},{1,0},{2,3},{3,2},{4,5},{5,4},{6,7},{7,6},{8,9},{9,8},{10,11... | collective-permute-start | bytes 3538952 | tf_op jit(solution)/shard_map/ppermute | solution.py:672
  335.9 3.2 collective-permute-start.39
  335.9 38.9 %collective-permute-start.36 = (bf16[2,6,4,64,256]{4,3,2,1,0:T(8,128)(2,1)}, bf16[2,6,4,64,256]{4,3,2,1,0:T(8,128)(2,1)S(1)}, u32[]{:S(2)}, u32[]{:S(2)}) collective-permute-start(bf16[2,6,4,64,256]{4,3,2,1,0:T(8,128)(2,1)} %get-tuple-element.126), channel_id=1, source_target_pairs={{0,16},{8,24},{16,0},{24,8},{1,17},{9,25},{17,1},{25,9},{2,18},{10... | collective-permute-start | bytes 4718600 | tf_op jit(solution)/shard_map/ppermute | solution.py:685
  337.4 37.4 %collective-permute-start.37 = (bf16[2,6,4,64,256]{4,3,2,1,0:T(8,128)(2,1)}, bf16[2,6,4,64,256]{4,3,2,1,0:T(8,128)(2,1)S(1)}, u32[]{:S(2)}, u32[]{:S(2)}) collective-permute-start(bf16[2,6,4,64,256]{4,3,2,1,0:T(8,128)(2,1)} %get-tuple-element.129), channel_id=1, source_target_pairs={{0,8},{8,0},{16,24},{24,16},{1,9},{9,1},{17,25},{25,17},{2,10},{10... | collective-permute-start | bytes 4718600 | tf_op jit(solution)/shard_map/ppermute | solution.py:685
  338.2 12.8 %collective-permute-start.38 = (bf16[48,12288]{1,0:T(8,128)(2,1)}, bf16[48,12288]{1,0:T(8,128)(2,1)}, u32[]{:S(2)}, u32[]{:S(2)}) collective-permute-start(bf16[48,12288]{1,0:T(8,128)(2,1)} %get-tuple-element.137), channel_id=1, source_target_pairs={{0,1},{1,0},{2,3},{3,2},{4,5},{5,4},{6,7},{7,6},{8,9},{9,8},{10,11... | collective-permute-start | bytes 3538952 | tf_op jit(solution)/shard_map/ppermute | solution.py:672
  341.6 30.1 %collective-permute-start.40 = (bf16[48,12288]{1,0:T(8,128)(2,1)}, bf16[48,12288]{1,0:T(8,128)(2,1)}, u32[]{:S(2)}, u32[]{:S(2)}) collective-permute-start(bf16[48,12288]{1,0:T(8,128)(2,1)} %add_rows.12), channel_id=1, source_target_pairs={{0,2},{1,3},{2,4},{3,5},{4,6},{5,7},{6,0},{7,1},{8,10},{9,11},{10,... | collective-permute-start | bytes 3538952 | tf_op jit(solution)/shard_map/ppermute | solution.py:675
  374.8 29.3 %collective-permute-start.44 = (bf16[48,12288]{1,0:T(8,128)(2,1)}, bf16[48,12288]{1,0:T(8,128)(2,1)}, u32[]{:S(2)}, u32[]{:S(2)}) collective-permute-start(bf16[48,12288]{1,0:T(8,128)(2,1)} %add_rows.13.refs_6_), channel_id=1, source_target_pairs={{0,2},{1,3},{2,4},{3,5},{4,6},{5,7},{6,0},{7,1},{8,10},{9,11},{10,... | collective-permute-start | bytes 3538952 | tf_op jit(solution)/shard_map/ppermute | solution.py:675
  374.8 1.2 copy-start.11
  374.8 1.7 copy-start.12
  376.5 2.3 copy-start.21
  376.5 27.6 %collective-permute-start.43 = (bf16[48,12288]{1,0:T(8,128)(2,1)}, bf16[48,12288]{1,0:T(8,128)(2,1)}, u32[]{:S(2)}, u32[]{:S(2)}) collective-permute-start(bf16[48,12288]{1,0:T(8,128)(2,1)} %get-tuple-element.143), channel_id=1, source_target_pairs={{0,1},{1,0},{2,3},{3,2},{4,5},{5,4},{6,7},{7,6},{8,9},{9,8},{10,11... | collective-permute-start | bytes 3538952 | tf_op jit(solution)/shard_map/ppermute | solution.py:672
  376.5 34.9 %collective-permute-start.41 = (bf16[12,3,64,256]{3,2,1,0:T(8,128)(2,1)}, bf16[12,3,64,256]{3,2,1,0:T(8,128)(2,1)S(1)}, u32[]{:S(2)}, u32[]{:S(2)}) collective-permute-start(bf16[12,3,64,256]{3,2,1,0:T(8,128)(2,1)} %get-tuple-element.140), channel_id=1, source_target_pairs={{0,8},{8,0},{16,24},{24,16},{1,9},{9,1},{17,25},{25,17},{2,10},{10... | collective-permute-start | bytes 3538952 | tf_op jit(solution)/shard_map/ppermute | solution.py:685
  377.6 34.6 %collective-permute-start.42 = (bf16[12,3,64,256]{3,2,1,0:T(8,128)(2,1)}, bf16[12,3,64,256]{3,2,1,0:T(8,128)(2,1)S(1)}, u32[]{:S(2)}, u32[]{:S(2)}) collective-permute-start(bf16[12,3,64,256]{3,2,1,0:T(8,128)(2,1)} %get-tuple-element.141), channel_id=1, source_target_pairs={{0,16},{8,24},{16,0},{24,8},{1,17},{9,25},{17,1},{25,9},{2,18},{10... | collective-permute-start | bytes 3538952 | tf_op jit(solution)/shard_map/ppermute | solution.py:685
  413.3 2.4 copy-start.26
  413.3 36.0 %collective-permute-start.47 = (bf16[12,4,64,256]{3,2,1,0:T(8,128)(2,1)}, bf16[12,4,64,256]{3,2,1,0:T(8,128)(2,1)S(1)}, u32[]{:S(2)}, u32[]{:S(2)}) collective-permute-start(bf16[12,4,64,256]{3,2,1,0:T(8,128)(2,1)} %get-tuple-element.148), channel_id=1, source_target_pairs={{0,8},{8,0},{16,24},{24,16},{1,9},{9,1},{17,25},{25,17},{2,10},{10... | collective-permute-start | bytes 4718600 | tf_op jit(solution)/shard_map/ppermute | solution.py:685
  414.2 35.8 %collective-permute-start.48 = (bf16[12,4,64,256]{3,2,1,0:T(8,128)(2,1)}, bf16[12,4,64,256]{3,2,1,0:T(8,128)(2,1)}, u32[]{:S(2)}, u32[]{:S(2)}) collective-permute-start(bf16[12,4,64,256]{3,2,1,0:T(8,128)(2,1)} %get-tuple-element.149), channel_id=1, source_target_pairs={{0,16},{8,24},{16,0},{24,8},{1,17},{9,25},{17,1},{25,9},{2,18},{10... | collective-permute-start | bytes 4718600 | tf_op jit(solution)/shard_map/ppermute | solution.py:685
  415.7 15.5 %collective-permute-start.45 = (bf16[48,12288]{1,0:T(8,128)(2,1)}, bf16[48,12288]{1,0:T(8,128)(2,1)}, u32[]{:S(2)}, u32[]{:S(2)}) collective-permute-start(bf16[48,12288]{1,0:T(8,128)(2,1)} %get-tuple-element.144), channel_id=1, source_target_pairs={{0,1},{1,0},{2,3},{3,2},{4,5},{5,4},{6,7},{7,6},{8,9},{9,8},{10,11... | collective-permute-start | bytes 3538952 | tf_op jit(solution)/shard_map/ppermute | solution.py:672
  415.7 30.6 %collective-permute-start.46 = (bf16[48,12288]{1,0:T(8,128)(2,1)S(1)}, bf16[48,12288]{1,0:T(8,128)(2,1)}, u32[]{:S(2)}, u32[]{:S(2)}) collective-permute-start(bf16[48,12288]{1,0:T(8,128)(2,1)S(1)} %copy-done.26), channel_id=1, source_target_pairs={{0,2},{1,3},{2,4},{3,5},{4,6},{5,7},{6,0},{7,1},{8,10},{9,11},{10,... | collective-permute-start | bytes 3538952 | tf_op jit(solution)/shard_map/ppermute | solution.py:675
  449.3 1.2 copy-start.29
  (22 other events, 21.3 us)
Sparse Core Ops, SparseCore 0:
  380.1 31.2 reduce-scatter.3

commit v6 on v5

--- a/solution.py
+++ b/solution.py
@@ -847,7 +847,7 @@
     if by_ring:
         input_parts = by_core(input_parts)
         mixed = add_round(mixed_parts, mixed_given, chips, moving[0])
-        waits, give = waits + [mixed], input_parts[chips + 1 : chips + 3]
+        waits, give = waits + moving, input_parts[chips + 1 : chips + 3]
     else:
         mixed, input_grad = scatter_whole(mixed_parts), scatter_whole(input_parts)
     if len(starts) > 1:
@@ -866,7 +866,7 @@
 
     give = [input_parts[chips + 3]] if by_ring else []
     down_last, moving, given = last_round(
-        down_onward, moving, up_got[-1] + [low_in_part], give
+        down_onward, moving, up_got[-1] + [low_in_part, mixed], give
     )
     if by_ring:
         input_given.append(given[0])

time: 466 us -> 466 us (level)
  no operation moved by 1% of the time
where the time goes in v6:
time: 466 us; the launch traced here: 464 us
  waiting for transfers between devices  206 us (44%)
  Pallas kernels  177 us (38%)
  local copies, waits for them, and re-layouts  34.2 us (7%)
  starting transfers between devices  26.9 us (6%)
  between operations  14.5 us (3%)
  other arithmetic  5.23 us (1%)
    ppermute x15, waiting for transfers between devices, shifted(): lax.ppermute(piece, 'mp', [(i, (i + 2 * by) % mp_size) for i in range(mp_...  169 us
    pallas_call x3, Pallas kernels, run_gradients(): pl.pallas_call(functools.partial(kernel, len(chunks), len(waits), first,...  42.7 us
    unnamed x75, local copies, waits for them, and re-layouts  23.9 us
    pallas_call x8, Pallas kernels, run_add(): pl.pallas_call(add_kernel, out_shape=shape((rows, width), BF16), grid=(st...  23.1 us
    pallas_call x1, Pallas kernels, run_hidden(): pl.pallas_call(functools.partial(hidden_kernel, len(chunks), len(waits),...  20 us
    pallas_call x1, Pallas kernels, run_spread(): pl.pallas_call(functools.partial(spread_kernel, len(out_shapes), len(wait...  17.7 us
    pallas_call x1, Pallas kernels, run_back(): pl.pallas_call(functools.partial(back_kernel, len(chunks), len(waits), pe...  17.4 us
    pallas_call x1, Pallas kernels, run_pieces(): pl.pallas_call(functools.partial(pieces_kernel, len(out_shapes), len(wait...  16.5 us
  transfers between devices with their start and end apart: 50, of which 23 were waited for; matrix products, arithmetic and copies ran while one was open for 4% of the time, Pallas kernels for 37%

profile of v6, /device:TPU:0, one launch (start us, length us, event | category | flops | bytes accessed | tf_op | source)
XLA Modules:
  0.0 464.1 jit_solution(14737477558943818871)
XLA Ops:
  7.2 3.1 collective-permute-start.1
  10.8 27.7 %collective-permute-done.1.refs_1_.refs_5_ = bf16[48,12288]{1,0:T(8,128)(2,1)S(1)} collective-permute-done((bf16[48,12288]{1,0:T(8,128)(2,1)}, bf16[48,12288]{1,0:T(8,128)(2,1)S(1)}, u32[]{:S(2)}, u32[]{:S(2)}) %collective-permute-start.1) | collective-permute-done | bytes 1179680 | tf_op jit(solution)/shard_map/ppermute | solution.py:675
  39.0 3.7 collective-permute-done.6.refs_4_.refs_9_
  42.7 1.2 copy-done.27
  44.0 1.1 copy-done.6
  45.0 23.7 %collective-permute-done.2.refs_0_ = bf16[48,12288]{1,0:T(8,128)(2,1)S(1)} collective-permute-done((bf16[48,12288]{1,0:T(8,128)(2,1)S(1)}, bf16[48,12288]{1,0:T(8,128)(2,1)S(1)}, u32[]{:S(2)}, u32[]{:S(2)}) %collective-permute-start.2) | collective-permute-done | bytes 1179680 | tf_op jit(solution)/shard_map/ppermute | solution.py:675
  70.4 2.4 collective-permute-done.8.refs_10_.refs_5_
  72.8 27.7 %collective-permute-done.7.refs_3_.refs_7_.refs_6_ = bf16[48,12288]{1,0:T(8,128)(2,1)S(1)} collective-permute-done((bf16[48,12288]{1,0:T(8,128)(2,1)}, bf16[48,12288]{1,0:T(8,128)(2,1)S(1)}, u32[]{:S(2)}, u32[]{:S(2)}) %collective-permute-start.7) | collective-permute-done | bytes 1179680 | tf_op jit(solution)/shard_map/ppermute | solution.py:675
  100.5 1.0 copy-done.2
  101.5 3.7 low_part.1
  106.2 2.0 collective-permute-start.9
  108.2 21.3 %collective-permute-done.11 = bf16[192,256]{1,0:T(8,128)(2,1)S(1)} collective-permute-done((bf16[192,256]{1,0:T(8,128)(2,1)S(1)}, bf16[192,256]{1,0:T(8,128)(2,1)S(1)}, u32[]{:S(2)}, u32[]{:S(2)}) %collective-permute-start.11) | collective-permute-done | bytes 98336 | tf_op jit(solution)/shard_map/ppermute | solution.py:675
  130.2 3.6 collective-permute-done.10
  133.8 1.6 add_convert_fusion.refs_1_
  142.1 1.0 copy-done.8
  143.2 20.0 %hidden.1 = (bf16[24,384,256]{2,1,0:T(8,128)(2,1)}, f32[24,384,256]{2,1,0:T(8,128)}) custom-call(s32[72]{0:T(128)} %reshape.19.up_ref, bf16[48,12288]{1,0:T(8,128)(2,1)} %refs_0_.13, bf16[48,12288]{1,0:T(8,128)(2,1)} %copy-done.1, bf16[48,12288]{1,0:T(8,128)(2,1)} %fence.11.refs_2_.refs_6_, bf16[48,12288]{1,0:T(8,128)(2,1)} %copy-done.5, ...), custom_call_target="tpu_custom_call" | custom-call | flops 1 | bytes 1 | tf_op jit(solution)/shard_map/hidden/pallas_call | solution.py:303
  163.2 2.7 collective-permute-done.12.refs_0_
  168.9 16.5 %pieces.1 = (bf16[48,12288]{1,0:T(8,128)(2,1)}, bf16[48,12288]{1,0:T(8,128)(2,1)}, bf16[48,12288]{1,0:T(8,128)(2,1)}, bf16[48,12288]{1,0:T(8,128)(2,1)}, bf16[48...) custom-call(s32[72]{0:T(128)} %reshape.20.down_ref, ...), custom_call_target="tpu_custom_call" | custom-call | flops 1 | bytes 1 | tf_op jit(solution)/shard_map/pieces/pallas_call | solution.py:331
  185.5 11.8 %collective-permute-done.16.refs_0_ = bf16[48,12288]{1,0:T(8,128)(2,1)S(1)} collective-permute-done((bf16[48,12288]{1,0:T(8,128)(2,1)}, bf16[48,12288]{1,0:T(8,128)(2,1)S(1)}, u32[]{:S(2)}, u32[]{:S(2)}) %collective-permute-start.16) | collective-permute-done | bytes 1179680 | tf_op jit(solution)/shard_map/ppermute | solution.py:675
  197.3 1.0 copy-done.17
  199.4 2.0 collective-permute-done.19.refs_3_.refs_1_
  202.4 2.6 add_rows.8
  205.5 1.1 copy-done.18
  206.6 16.9 %down_kernel.1 = (f32[4,3,64,256]{3,2,1,0:T(8,128)}, bf16[2,4,3,64,256]{4,3,2,1,0:T(8,128)(2,1)}, bf16[4,3,64,256]{3,2,1,0:T(8,128)(2,1)}, f32[4,3,64,256]{3,2,1...) custom-call(s32[72]{0:T(128)} %reshape.20.down_ref, ...), custom_call_target="tpu_custom_call" | custom-call | flops 1 | bytes 1 | tf_op jit(solution)/shard_map/down_kernel/pallas_call | solution.py:403
  224.5 1.5 collective-permute-start.23
  226.0 1.5 collective-permute-start.22
  227.5 17.4 %back.1 = (bf16[24,384,256]{2,1,0:T(8,128)(2,1)}, f32[384,256]{1,0:T(8,128)}) custom-call(s32[72]{0:T(128)} %reshape.20.down_ref, s32[24]{0:T(128)} %dynamic_slice.11.live_ref, bf16[48,12288]{1,0:T(8,128)(2,1)} %refs_0_.10, bf16[48,12288]{1,0:T(8,128)(2,1)} %fence.12.refs_1_, bf16[48,12288]{1,0:T(8,128)(2,1)} %get-tuple-element.83.refs_2_, ...), custom_call_target="tpu_custom_call" | custom-call | flops 1 | bytes 1 | tf_op jit(solution)/shard_map/back/pallas_call | solution.py:356
  244.9 1.0 copy-done.30
  245.9 3.0 add_rows.9.refs_5_
  254.3 2.0 collective-permute-start.31
  256.3 12.9 %up_kernel.2 = (f32[6,4,64,256]{3,2,1,0:T(8,128)}, bf16[2,6,4,64,256]{4,3,2,1,0:T(8,128)(2,1)}, bf16[6,4,64,256]{3,2,1,0:T(8,128)(2,1)}, f32[6,4,64,256]{3,2,1,0...) custom-call(s32[72]{0:T(128)} %reshape.19.up_ref, s32[4]{0:T(128)} %iota_xor_fusion.quarter_ref, ...), custom_call_target="tpu_custom_call" | custom-call | flops 1 | bytes 1 | tf_op jit(solution)/shard_map/up_kernel/pallas_call | solution.py:403
  271.7 2.7 collective-permute-start.29
  274.4 16.3 %collective-permute-done.29 = bf16[192,256]{1,0:T(8,128)(2,1)S(1)} collective-permute-done((bf16[192,256]{1,0:T(8,128)(2,1)S(1)}, bf16[192,256]{1,0:T(8,128)(2,1)S(1)}, u32[]{:S(2)}, u32[]{:S(2)}) %collective-permute-start.29) | collective-permute-done | bytes 98336 | tf_op jit(solution)/shard_map/ppermute | solution.py:714
  290.8 1.3 collective-permute-done.30
  292.8 3.0 add_rows.10.refs_7_
  295.8 1.1 copy-done.13
  298.4 1.5 collective-permute-start.34
  299.9 17.7 %spread.1 = (bf16[48,12288]{1,0:T(8,128)(2,1)}, bf16[48,12288]{1,0:T(8,128)(2,1)}, bf16[48,12288]{1,0:T(8,128)(2,1)}, bf16[48,12288]{1,0:T(8,128)(2,1)}, bf16[48...) custom-call(s32[72]{0:T(128)} %reshape.19.up_ref, ...), custom_call_target="tpu_custom_call" | custom-call | flops 1 | bytes 1 | tf_op jit(solution)/shard_map/spread/pallas_call | solution.py:430
  317.6 12.9 %up_kernel.3 = (f32[6,4,64,256]{3,2,1,0:T(8,128)}, bf16[2,6,4,64,256]{4,3,2,1,0:T(8,128)(2,1)}, bf16[6,4,64,256]{3,2,1,0:T(8,128)(2,1)}, f32[6,4,64,256]{3,2,1,0...) custom-call(s32[72]{0:T(128)} %reshape.19.up_ref, s32[4]{0:T(128)} %iota_xor_fusion.quarter_ref, ...), custom_call_target="tpu_custom_call" | custom-call | flops 1 | bytes 1 | tf_op jit(solution)/shard_map/up_kernel/pallas_call | solution.py:403
  330.5 3.6 collective-permute-done.35.refs_5_.refs_1_.refs_3_
  335.9 1.5 collective-permute-start.36
  339.1 2.5 add_rows.12
  341.6 3.6 low_in_part.1.refs_5_
  345.2 2.9 pass_on.6.refs_0_
  348.1 2.9 pass_on.7.refs_1_
  351.0 3.0 add_rows.11.refs_6_
  354.0 17.7 %collective-permute-done.40.refs_2_ = bf16[48,12288]{1,0:T(8,128)(2,1)} collective-permute-done((bf16[48,12288]{1,0:T(8,128)(2,1)}, bf16[48,12288]{1,0:T(8,128)(2,1)}, u32[]{:S(2)}, u32[]{:S(2)}) %collective-permute-start.40) | collective-permute-done | bytes 1179680 | tf_op jit(solution)/shard_map/ppermute | solution.py:675
  371.7 3.0 add_rows.13.refs_7_
  374.8 1.1 copy-done.11
  376.5 1.1 collective-permute-start.41
  377.6 1.2 collective-permute-start.42
  378.8 1.2 copy.56
  380.0 3.4 pass_on.4.refs_0_
  383.3 3.4 pass_on.5.refs_1_
  386.7 17.3 %collective-permute-done.44.refs_2_ = bf16[48,12288]{1,0:T(8,128)(2,1)} collective-permute-done((bf16[48,12288]{1,0:T(8,128)(2,1)}, bf16[48,12288]{1,0:T(8,128)(2,1)}, u32[]{:S(2)}, u32[]{:S(2)}) %collective-permute-start.44) | collective-permute-done | bytes 1179680 | tf_op jit(solution)/shard_map/ppermute | solution.py:675
  404.0 3.0 add_rows.14.refs_5_
  407.0 4.3 collective-permute-done.41.refs_3_.refs_8_
  414.2 1.5 collective-permute-start.48
  415.7 1.1 copy.57
  417.8 6.8 %sums.2.refs_0_ = f32[24,4,64,256]{3,2,1,0:T(8,128)} custom-call(f32[6,4,64,256]{3,2,1,0:T(8,128)} %get-tuple-element.114.refs_1_.refs_5_.refs_0_, bf16[2,6,4,64,256]{4,3,2,1,0:T(8,128)(2,1)} %copy-done.10, f32[6,4,64,256]{3,2,1,0:T(8,128)} %get-tuple-element.145.refs_2_, bf16[2,6,4,64,256]{4,3,2,1,0:T(8,128)(2,1)} %copy-done.9, ...), custom_call_target="tpu_custom_call" | custom-call | flops 1 | bytes 1 | tf_op jit(solution)/shard_map/sums/pallas_call | solution.py:592
  424.6 6.5 %sums.3 = f32[24,3,64,256]{3,2,1,0:T(8,128)} custom-call(f32[4,3,64,256]{3,2,1,0:T(8,128)} %get-tuple-element.151.refs_0_, bf16[2,4,3,64,256]{4,3,2,1,0:T(8,128)(2,1)} %copy-done.20, f32[4,3,64,256]{3,2,1,0:T(8,128)} %get-tuple-element.152.refs_2_, bf16[2,4,3,64,256]{4,3,2,1,0:T(8,128)(2,1)} %copy-done.19, f32[8,3,64,256]{3,2,1,0:T(8,128)} %get-tuple-element.153.refs_4_, ...), custom_call_target="tpu_custom_call" | custom-call | flops 1 | bytes 1 | tf_op jit(solution)/shard_map/sums/pallas_call | solution.py:592
  431.1 15.1 %collective-permute-done.46.refs_2_ = bf16[48,12288]{1,0:T(8,128)(2,1)} collective-permute-done((bf16[48,12288]{1,0:T(8,128)(2,1)S(1)}, bf16[48,12288]{1,0:T(8,128)(2,1)}, u32[]{:S(2)}, u32[]{:S(2)}) %collective-permute-start.46) | collective-permute-done | bytes 1179680 | tf_op jit(solution)/shard_map/ppermute | solution.py:675
  446.2 3.0 add_rows.15
  450.4 6.8 %finish.1 = (f32[24,3,64,256]{3,2,1,0:T(8,128)}, f32[64,6144]{1,0:T(8,128)}) custom-call(f32[24,4,64,256]{3,2,1,0:T(8,128)} %sums.2.refs_0_, bf16[12,4,64,256]{3,2,1,0:T(8,128)(2,1)} %copy-done.29, bf16[12,4,64,256]{3,2,1,0:T(8,128)(2,1)} %collective-permute-done.48.refs_2_), custom_call_target="tpu_custom_call" | custom-call | flops 1 | bytes 1 | tf_op jit(solution)/shard_map/finish/pallas_call | solution.py:622
  (181 shorter events, 36.5 us)
Async XLA Ops:
  7.2 408.5 %reduce-scatter.4.cloned.1.call-start = ((), (), s32[]{:S(2)}) async-start(), calls=%async_computation.1 | async-start | bytes 983040
  7.2 31.3 %collective-permute-start.1 = (bf16[48,12288]{1,0:T(8,128)(2,1)}, bf16[48,12288]{1,0:T(8,128)(2,1)S(1)}, u32[]{:S(2)}, u32[]{:S(2)}) collective-permute-start(bf16[48,12288]{1,0:T(8,128)(2,1)} %refs_0_.13), channel_id=1, source_target_pairs={{0,2},{1,3},{2,4},{3,5},{4,6},{5,7},{6,0},{7,1},{8,10},{9,11},{10,... | collective-permute-start | bytes 3538952 | tf_op jit(solution)/shard_map/ppermute | solution.py:675
  10.3 32.4 %collective-permute-start.3 = (bf16[48,12288]{1,0:T(8,128)(2,1)}, bf16[48,12288]{1,0:T(8,128)(2,1)S(1)}, u32[]{:S(2)}, u32[]{:S(2)}) collective-permute-start(bf16[48,12288]{1,0:T(8,128)(2,1)} %refs_0_.13), channel_id=1, source_target_pairs={{0,1},{1,0},{2,3},{3,2},{4,5},{5,4},{6,7},{7,6},{8,9},{9,8},{10,11... | collective-permute-start | bytes 3538952 | tf_op jit(solution)/shard_map/ppermute | solution.py:672
  10.3 32.4 %collective-permute-start.5 = (bf16[48,12288]{1,0:T(8,128)(2,1)}, bf16[48,12288]{1,0:T(8,128)(2,1)S(1)}, u32[]{:S(2)}, u32[]{:S(2)}) collective-permute-start(bf16[48,12288]{1,0:T(8,128)(2,1)} %refs_0_.10), channel_id=1, source_target_pairs={{0,1},{1,0},{2,3},{3,2},{4,5},{5,4},{6,7},{7,6},{8,9},{9,8},{10,11... | collective-permute-start | bytes 3538952 | tf_op jit(solution)/shard_map/ppermute | solution.py:672
  38.5 62.0 %copy-start.1 = (bf16[48,12288]{1,0:T(8,128)(2,1)}, bf16[48,12288]{1,0:T(8,128)(2,1)S(1)}, u32[]{:S(2)}) copy-start(bf16[48,12288]{1,0:T(8,128)(2,1)S(1)} %collective-permute-done.1.refs_1_.refs_5_) | copy-start | bytes 3538948
  38.5 4.2 collective-permute-start.4
  38.5 30.2 %collective-permute-start.2 = (bf16[48,12288]{1,0:T(8,128)(2,1)S(1)}, bf16[48,12288]{1,0:T(8,128)(2,1)S(1)}, u32[]{:S(2)}, u32[]{:S(2)}) collective-permute-start(bf16[48,12288]{1,0:T(8,128)(2,1)S(1)} %collective-permute-done.1.refs_1_.refs_5_), channel_id=1, source_target_pairs={{0,2},{1,3},{2,4},{3,5},{4,6},{5,7},{6,0},{7,1},{8,10},{9,11},{10,... | collective-permute-start | bytes 3538952 | tf_op jit(solution)/shard_map/ppermute | solution.py:675
  38.5 4.2 collective-permute-start.6
  42.7 1.3 copy-start.27
  42.7 26.0 %copy-start.3 = (bf16[48,12288]{1,0:T(8,128)(2,1)}, bf16[48,12288]{1,0:T(8,128)(2,1)S(1)}, u32[]{:S(2)}) copy-start(bf16[48,12288]{1,0:T(8,128)(2,1)S(1)} %collective-permute-done.5.refs_3_.refs_2_.refs_9_) | copy-start | bytes 3538948
  42.7 1.3 copy-start.5
  69.7 3.1 collective-permute-start.8
  69.7 30.8 %collective-permute-start.7 = (bf16[48,12288]{1,0:T(8,128)(2,1)}, bf16[48,12288]{1,0:T(8,128)(2,1)S(1)}, u32[]{:S(2)}, u32[]{:S(2)}) collective-permute-start(bf16[48,12288]{1,0:T(8,128)(2,1)} %fence.11.refs_2_.refs_6_), channel_id=1, source_target_pairs={{0,2},{1,3},{2,4},{3,5},{4,6},{5,7},{6,0},{7,1},{8,10},{9,11},{10,... | collective-permute-start | bytes 3538952 | tf_op jit(solution)/shard_map/ppermute | solution.py:675
  69.7 65.7 %collective-permute-start = (bf16[48,12288]{1,0:T(8,128)(2,1)}, bf16[48,12288]{1,0:T(8,128)(2,1)}, u32[]{:S(2)}, u32[]{:S(2)}) collective-permute-start(bf16[48,12288]{1,0:T(8,128)(2,1)} %refs_0_.10), channel_id=1, source_target_pairs={{0,2},{1,3},{2,4},{3,5},{4,6},{5,7},{6,0},{7,1},{8,10},{9,11},{10,... | collective-permute-start | bytes 3538952 | tf_op jit(solution)/shard_map/ppermute | solution.py:675
  72.8 27.7 %copy-start.4 = (bf16[48,12288]{1,0:T(8,128)(2,1)}, bf16[48,12288]{1,0:T(8,128)(2,1)S(1)}, u32[]{:S(2)}) copy-start(bf16[48,12288]{1,0:T(8,128)(2,1)S(1)} %collective-permute-done.8.refs_10_.refs_5_) | copy-start | bytes 3538948
  106.1 23.4 %collective-permute-start.11 = (bf16[192,256]{1,0:T(8,128)(2,1)S(1)}, bf16[192,256]{1,0:T(8,128)(2,1)S(1)}, u32[]{:S(2)}, u32[]{:S(2)}) collective-permute-start(bf16[192,256]{1,0:T(8,128)(2,1)S(1)} %convert_element_type.33), channel_id=1, source_target_pairs={{0,6},{1,7},{2,0},{3,1},{4,2},{5,3},{6,4},{7,5},{8,14},{9,15},{10,... | collective-permute-start | bytes 294920 | tf_op jit(solution)/shard_map/ppermute | solution.py:675
  106.2 23.9 %collective-permute-start.9 = (bf16[192,256]{1,0:T(8,128)(2,1)S(1)}, bf16[192,256]{1,0:T(8,128)(2,1)S(1)}, u32[]{:S(2)}, u32[]{:S(2)}) collective-permute-start(bf16[192,256]{1,0:T(8,128)(2,1)S(1)} %convert_element_type.33), channel_id=1, source_target_pairs={{0,2},{1,3},{2,4},{3,5},{4,6},{5,7},{6,0},{7,1},{8,10},{9,11},{10,... | collective-permute-start | bytes 294920 | tf_op jit(solution)/shard_map/ppermute | solution.py:675
  108.2 25.6 %collective-permute-start.10 = (bf16[192,256]{1,0:T(8,128)(2,1)S(1)}, bf16[192,256]{1,0:T(8,128)(2,1)S(1)}, u32[]{:S(2)}, u32[]{:S(2)}) collective-permute-start(bf16[192,256]{1,0:T(8,128)(2,1)S(1)} %convert_element_type.33), channel_id=1, source_target_pairs={{0,4},{1,5},{2,6},{3,7},{4,0},{5,1},{6,2},{7,3},{8,12},{9,13},{10,... | collective-permute-start | bytes 294920 | tf_op jit(solution)/shard_map/ppermute | solution.py:675
  108.2 33.9 %collective-permute-start.13 = (bf16[48,12288]{1,0:T(8,128)(2,1)}, bf16[48,12288]{1,0:T(8,128)(2,1)S(1)}, u32[]{:S(2)}, u32[]{:S(2)}) collective-permute-start(bf16[48,12288]{1,0:T(8,128)(2,1)} %copy-done.2), channel_id=1, source_target_pairs={{0,1},{1,0},{2,3},{3,2},{4,5},{5,4},{6,7},{7,6},{8,9},{9,8},{10,11... | collective-permute-start | bytes 3538952 | tf_op jit(solution)/shard_map/ppermute | solution.py:672
  135.4 27.8 %collective-permute-start.15 = (bf16[48,12288]{1,0:T(8,128)(2,1)}, bf16[48,12288]{1,0:T(8,128)(2,1)S(1)}, u32[]{:S(2)}, u32[]{:S(2)}) collective-permute-start(bf16[48,12288]{1,0:T(8,128)(2,1)} %fence.12.refs_1_), channel_id=1, source_target_pairs={{0,1},{1,0},{2,3},{3,2},{4,5},{5,4},{6,7},{7,6},{8,9},{9,8},{10,11... | collective-permute-start | bytes 3538952 | tf_op jit(solution)/shard_map/ppermute | solution.py:672
  135.5 30.4 %collective-permute-start.12 = (bf16[48,12288]{1,0:T(8,128)(2,1)}, bf16[48,12288]{1,0:T(8,128)(2,1)S(1)}, u32[]{:S(2)}, u32[]{:S(2)}) collective-permute-start(bf16[48,12288]{1,0:T(8,128)(2,1)} %fence.12.refs_1_), channel_id=1, source_target_pairs={{0,2},{1,3},{2,4},{3,5},{4,6},{5,7},{6,0},{7,1},{8,10},{9,11},{10,... | collective-permute-start | bytes 3538952 | tf_op jit(solution)/shard_map/ppermute | solution.py:675
  135.6 4.2 collective-permute-start.14
  163.2 2.7 copy-start.7
  166.9 18.6 %collective-permute-start.17 = (bf16[48,12288]{1,0:T(8,128)(2,1)}, bf16[48,12288]{1,0:T(8,128)(2,1)S(1)}, u32[]{:S(2)}, u32[]{:S(2)}) collective-permute-start(bf16[48,12288]{1,0:T(8,128)(2,1)} %get-tuple-element.83.refs_2_), channel_id=1, source_target_pairs={{0,1},{1,0},{2,3},{3,2},{4,5},{5,4},{6,7},{7,6},{8,9},{9,8},{10,11... | collective-permute-start | bytes 3538952 | tf_op jit(solution)/shard_map/ppermute | solution.py:672
  166.9 30.4 %collective-permute-start.16 = (bf16[48,12288]{1,0:T(8,128)(2,1)}, bf16[48,12288]{1,0:T(8,128)(2,1)S(1)}, u32[]{:S(2)}, u32[]{:S(2)}) collective-permute-start(bf16[48,12288]{1,0:T(8,128)(2,1)} %get-tuple-element.83.refs_2_), channel_id=1, source_target_pairs={{0,2},{1,3},{2,4},{3,5},{4,6},{5,7},{6,0},{7,1},{8,10},{9,11},{10,... | collective-permute-start | bytes 3538952 | tf_op jit(solution)/shard_map/ppermute | solution.py:675
  185.5 11.8 %copy-start.15 = (bf16[48,12288]{1,0:T(8,128)(2,1)}, bf16[48,12288]{1,0:T(8,128)(2,1)S(1)}, u32[]{:S(2)}) copy-start(bf16[48,12288]{1,0:T(8,128)(2,1)S(1)} %collective-permute-done.17.refs_11_.refs_5_) | copy-start | bytes 3538948
  198.4 3.1 collective-permute-start.19
  198.4 7.1 %collective-permute-start.18 = (bf16[48,12288]{1,0:T(8,128)(2,1)}, bf16[48,12288]{1,0:T(8,128)(2,1)S(1)}, u32[]{:S(2)}, u32[]{:S(2)}) collective-permute-start(bf16[48,12288]{1,0:T(8,128)(2,1)} %get-tuple-element.94.refs_6_), channel_id=1, source_target_pairs={{0,1},{1,0},{2,3},{3,2},{4,5},{5,4},{6,7},{7,6},{8,9},{9,8},{10,11... | collective-permute-start | bytes 3538952 | tf_op jit(solution)/shard_map/ppermute | solution.py:672
  198.9 24.6 %collective-permute-start.20 = (bf16[48,12288]{1,0:T(8,128)(2,1)}, bf16[48,12288]{1,0:T(8,128)(2,1)}, u32[]{:S(2)}, u32[]{:S(2)}) collective-permute-start(bf16[48,12288]{1,0:T(8,128)(2,1)} %get-tuple-element.98), channel_id=1, source_target_pairs={{0,1},{1,0},{2,3},{3,2},{4,5},{5,4},{6,7},{7,6},{8,9},{9,8},{10,11... | collective-permute-start | bytes 3538952 | tf_op jit(solution)/shard_map/ppermute | solution.py:672
  198.9 24.6 %collective-permute-start.21 = (bf16[48,12288]{1,0:T(8,128)(2,1)}, bf16[48,12288]{1,0:T(8,128)(2,1)S(1)}, u32[]{:S(2)}, u32[]{:S(2)}) collective-permute-start(bf16[48,12288]{1,0:T(8,128)(2,1)} %get-tuple-element.99), channel_id=1, source_target_pairs={{0,1},{1,0},{2,3},{3,2},{4,5},{5,4},{6,7},{7,6},{8,9},{9,8},{10,11... | collective-permute-start | bytes 3538952 | tf_op jit(solution)/shard_map/ppermute | solution.py:672
  205.0 39.9 %collective-permute-start.24 = (bf16[48,12288]{1,0:T(8,128)(2,1)}, bf16[48,12288]{1,0:T(8,128)(2,1)S(1)}, u32[]{:S(2)}, u32[]{:S(2)}) collective-permute-start(bf16[48,12288]{1,0:T(8,128)(2,1)} %add_rows.8), channel_id=1, source_target_pairs={{0,2},{1,3},{2,4},{3,5},{4,6},{5,7},{6,0},{7,1},{8,10},{9,11},{10,... | collective-permute-start | bytes 3538952 | tf_op jit(solution)/shard_map/ppermute | solution.py:675
  224.5 24.5 %collective-permute-start.23 = (bf16[2,4,3,64,256]{4,3,2,1,0:T(8,128)(2,1)}, bf16[2,4,3,64,256]{4,3,2,1,0:T(8,128)(2,1)S(1)}, u32[]{:S(2)}, u32[]{:S(2)}) collective-permute-start(bf16[2,4,3,64,256]{4,3,2,1,0:T(8,128)(2,1)} %get-tuple-element.105), channel_id=1, source_target_pairs={{0,8},{8,0},{16,24},{24,16},{1,9},{9,1},{17,25},{25,17},{2,10},{10... | collective-permute-start | bytes 2359304 | tf_op jit(solution)/shard_map/ppermute | solution.py:685
  226.0 23.0 %collective-permute-start.22 = (bf16[2,4,3,64,256]{4,3,2,1,0:T(8,128)(2,1)}, bf16[2,4,3,64,256]{4,3,2,1,0:T(8,128)(2,1)S(1)}, u32[]{:S(2)}, u32[]{:S(2)}) collective-permute-start(bf16[2,4,3,64,256]{4,3,2,1,0:T(8,128)(2,1)} %get-tuple-element.100.refs_11_), channel_id=1, source_target_pairs={{0,16},{8,24},{16,0},{24,8},{1,17},{9,25},{17,1},{25,9},{2,18},{10... | collective-permute-start | bytes 2359304 | tf_op jit(solution)/shard_map/ppermute | solution.py:685
  252.0 1.5 collective-permute-start.27
  252.0 43.7 %collective-permute-start.25 = (bf16[2,8,3,64,256]{4,3,2,1,0:T(8,128)(2,1)}, bf16[2,8,3,64,256]{4,3,2,1,0:T(8,128)(2,1)S(1)}, u32[]{:S(2)}, u32[]{:S(2)}) collective-permute-start(bf16[2,8,3,64,256]{4,3,2,1,0:T(8,128)(2,1)} %get-tuple-element.112), channel_id=1, source_target_pairs={{0,16},{8,24},{16,0},{24,8},{1,17},{9,25},{17,1},{25,9},{2,18},{10... | collective-permute-start | bytes 4718600 | tf_op jit(solution)/shard_map/ppermute | solution.py:685
  252.6 43.2 %collective-permute-start.26 = (bf16[2,8,3,64,256]{4,3,2,1,0:T(8,128)(2,1)}, bf16[2,8,3,64,256]{4,3,2,1,0:T(8,128)(2,1)S(1)}, u32[]{:S(2)}, u32[]{:S(2)}) collective-permute-start(bf16[2,8,3,64,256]{4,3,2,1,0:T(8,128)(2,1)} %get-tuple-element.113), channel_id=1, source_target_pairs={{0,8},{8,0},{16,24},{24,16},{1,9},{9,1},{17,25},{25,17},{2,10},{10... | collective-permute-start | bytes 4718600 | tf_op jit(solution)/shard_map/ppermute | solution.py:685
  254.2 15.1 %collective-permute-start.28 = (bf16[192,256]{1,0:T(8,128)(2,1)S(1)}, bf16[192,256]{1,0:T(8,128)(2,1)S(1)}, u32[]{:S(2)}, u32[]{:S(2)}) collective-permute-start(bf16[192,256]{1,0:T(8,128)(2,1)S(1)} %fusion.2), channel_id=1, source_target_pairs={{0,2},{1,3},{2,0},{3,1},{4,6},{5,7},{6,4},{7,5},{8,10},{9,11},{10,... | collective-permute-start | bytes 294920 | tf_op jit(solution)/shard_map/ppermute | solution.py:710
  254.3 38.5 %collective-permute-start.31 = (bf16[48,12288]{1,0:T(8,128)(2,1)}, bf16[48,12288]{1,0:T(8,128)(2,1)}, u32[]{:S(2)}, u32[]{:S(2)}) collective-permute-start(bf16[48,12288]{1,0:T(8,128)(2,1)} %add_rows.9.refs_5_), channel_id=1, source_target_pairs={{0,2},{1,3},{2,4},{3,5},{4,6},{5,7},{6,0},{7,1},{8,10},{9,11},{10,... | collective-permute-start | bytes 3538952 | tf_op jit(solution)/shard_map/ppermute | solution.py:675
  269.8 1.8 copy-start.32
  271.7 19.0 %collective-permute-start.29 = (bf16[192,256]{1,0:T(8,128)(2,1)S(1)}, bf16[192,256]{1,0:T(8,128)(2,1)S(1)}, u32[]{:S(2)}, u32[]{:S(2)}) collective-permute-start(bf16[192,256]{1,0:T(8,128)(2,1)S(1)} %get-tuple-element.174), channel_id=1, source_target_pairs={{0,4},{1,5},{2,6},{3,7},{4,0},{5,1},{6,2},{7,3},{8,12},{9,13},{10,... | collective-permute-start | bytes 294920 | tf_op jit(solution)/shard_map/ppermute | solution.py:714
  290.7 1.4 collective-permute-start.30
  295.8 1.7 copy-start.14
  297.4 36.7 %collective-permute-start.35 = (bf16[2,6,4,64,256]{4,3,2,1,0:T(8,128)(2,1)}, bf16[2,6,4,64,256]{4,3,2,1,0:T(8,128)(2,1)S(1)}, u32[]{:S(2)}, u32[]{:S(2)}) collective-permute-start(bf16[2,6,4,64,256]{4,3,2,1,0:T(8,128)(2,1)} %get-tuple-element.125), channel_id=1, source_target_pairs={{0,8},{8,0},{16,24},{24,16},{1,9},{9,1},{17,25},{25,17},{2,10},{10... | collective-permute-start | bytes 4718600 | tf_op jit(solution)/shard_map/ppermute | solution.py:685
  298.4 36.4 %collective-permute-start.34 = (bf16[2,6,4,64,256]{4,3,2,1,0:T(8,128)(2,1)}, bf16[2,6,4,64,256]{4,3,2,1,0:T(8,128)(2,1)S(1)}, u32[]{:S(2)}, u32[]{:S(2)}) collective-permute-start(bf16[2,6,4,64,256]{4,3,2,1,0:T(8,128)(2,1)} %get-tuple-element.117.refs_4_.refs_10_), channel_id=1, source_target_pairs={{0,16},{8,24},{16,0},{24,8},{1,17},{9,25},{17,1},{25,9},{2,18},{10... | collective-permute-start | bytes 4718600 | tf_op jit(solution)/shard_map/ppermute | solution.py:685
  299.9 30.6 %collective-permute-start.33 = (bf16[48,12288]{1,0:T(8,128)(2,1)}, bf16[48,12288]{1,0:T(8,128)(2,1)}, u32[]{:S(2)}, u32[]{:S(2)}) collective-permute-start(bf16[48,12288]{1,0:T(8,128)(2,1)} %add_rows.10.refs_7_), channel_id=1, source_target_pairs={{0,2},{1,3},{2,4},{3,5},{4,6},{5,7},{6,0},{7,1},{8,10},{9,11},{10,... | collective-permute-start | bytes 3538952 | tf_op jit(solution)/shard_map/ppermute | solution.py:675
  334.1 1.2 copy-start.9
  335.9 3.2 collective-permute-start.39
  335.9 38.8 %collective-permute-start.36 = (bf16[2,6,4,64,256]{4,3,2,1,0:T(8,128)(2,1)}, bf16[2,6,4,64,256]{4,3,2,1,0:T(8,128)(2,1)S(1)}, u32[]{:S(2)}, u32[]{:S(2)}) collective-permute-start(bf16[2,6,4,64,256]{4,3,2,1,0:T(8,128)(2,1)} %get-tuple-element.126), channel_id=1, source_target_pairs={{0,16},{8,24},{16,0},{24,8},{1,17},{9,25},{17,1},{25,9},{2,18},{10... | collective-permute-start | bytes 4718600 | tf_op jit(solution)/shard_map/ppermute | solution.py:685
  337.4 37.3 %collective-permute-start.37 = (bf16[2,6,4,64,256]{4,3,2,1,0:T(8,128)(2,1)}, bf16[2,6,4,64,256]{4,3,2,1,0:T(8,128)(2,1)S(1)}, u32[]{:S(2)}, u32[]{:S(2)}) collective-permute-start(bf16[2,6,4,64,256]{4,3,2,1,0:T(8,128)(2,1)} %get-tuple-element.129), channel_id=1, source_target_pairs={{0,8},{8,0},{16,24},{24,16},{1,9},{9,1},{17,25},{25,17},{2,10},{10... | collective-permute-start | bytes 4718600 | tf_op jit(solution)/shard_map/ppermute | solution.py:685
  338.2 12.8 %collective-permute-start.32 = (bf16[48,12288]{1,0:T(8,128)(2,1)}, bf16[48,12288]{1,0:T(8,128)(2,1)}, u32[]{:S(2)}, u32[]{:S(2)}) collective-permute-start(bf16[48,12288]{1,0:T(8,128)(2,1)} %get-tuple-element.116), channel_id=1, source_target_pairs={{0,1},{1,0},{2,3},{3,2},{4,5},{5,4},{6,7},{7,6},{8,9},{9,8},{10,11... | collective-permute-start | bytes 3538952 | tf_op jit(solution)/shard_map/ppermute | solution.py:672
  338.2 15.8 %collective-permute-start.38 = (bf16[48,12288]{1,0:T(8,128)(2,1)}, bf16[48,12288]{1,0:T(8,128)(2,1)}, u32[]{:S(2)}, u32[]{:S(2)}) collective-permute-start(bf16[48,12288]{1,0:T(8,128)(2,1)} %get-tuple-element.137), channel_id=1, source_target_pairs={{0,1},{1,0},{2,3},{3,2},{4,5},{5,4},{6,7},{7,6},{8,9},{9,8},{10,11... | collective-permute-start | bytes 3538952 | tf_op jit(solution)/shard_map/ppermute | solution.py:672
  341.6 30.1 %collective-permute-start.40 = (bf16[48,12288]{1,0:T(8,128)(2,1)}, bf16[48,12288]{1,0:T(8,128)(2,1)}, u32[]{:S(2)}, u32[]{:S(2)}) collective-permute-start(bf16[48,12288]{1,0:T(8,128)(2,1)} %add_rows.12), channel_id=1, source_target_pairs={{0,2},{1,3},{2,4},{3,5},{4,6},{5,7},{6,0},{7,1},{8,10},{9,11},{10,... | collective-permute-start | bytes 3538952 | tf_op jit(solution)/shard_map/ppermute | solution.py:675
  374.7 29.3 %collective-permute-start.44 = (bf16[48,12288]{1,0:T(8,128)(2,1)}, bf16[48,12288]{1,0:T(8,128)(2,1)}, u32[]{:S(2)}, u32[]{:S(2)}) collective-permute-start(bf16[48,12288]{1,0:T(8,128)(2,1)} %add_rows.13.refs_7_), channel_id=1, source_target_pairs={{0,2},{1,3},{2,4},{3,5},{4,6},{5,7},{6,0},{7,1},{8,10},{9,11},{10,... | collective-permute-start | bytes 3538952 | tf_op jit(solution)/shard_map/ppermute | solution.py:675
  374.7 1.1 copy-start.11
  374.8 1.7 copy-start.12
  376.5 2.3 copy-start.21
  376.5 27.6 %collective-permute-start.43 = (bf16[48,12288]{1,0:T(8,128)(2,1)}, bf16[48,12288]{1,0:T(8,128)(2,1)}, u32[]{:S(2)}, u32[]{:S(2)}) collective-permute-start(bf16[48,12288]{1,0:T(8,128)(2,1)} %get-tuple-element.143), channel_id=1, source_target_pairs={{0,1},{1,0},{2,3},{3,2},{4,5},{5,4},{6,7},{7,6},{8,9},{9,8},{10,11... | collective-permute-start | bytes 3538952 | tf_op jit(solution)/shard_map/ppermute | solution.py:672
  376.5 34.9 %collective-permute-start.41 = (bf16[12,3,64,256]{3,2,1,0:T(8,128)(2,1)}, bf16[12,3,64,256]{3,2,1,0:T(8,128)(2,1)S(1)}, u32[]{:S(2)}, u32[]{:S(2)}) collective-permute-start(bf16[12,3,64,256]{3,2,1,0:T(8,128)(2,1)} %get-tuple-element.140), channel_id=1, source_target_pairs={{0,8},{8,0},{16,24},{24,16},{1,9},{9,1},{17,25},{25,17},{2,10},{10... | collective-permute-start | bytes 3538952 | tf_op jit(solution)/shard_map/ppermute | solution.py:685
  377.6 34.6 %collective-permute-start.42 = (bf16[12,3,64,256]{3,2,1,0:T(8,128)(2,1)}, bf16[12,3,64,256]{3,2,1,0:T(8,128)(2,1)S(1)}, u32[]{:S(2)}, u32[]{:S(2)}) collective-permute-start(bf16[12,3,64,256]{3,2,1,0:T(8,128)(2,1)} %get-tuple-element.141), channel_id=1, source_target_pairs={{0,16},{8,24},{16,0},{24,8},{1,17},{9,25},{17,1},{25,9},{2,18},{10... | collective-permute-start | bytes 3538952 | tf_op jit(solution)/shard_map/ppermute | solution.py:685
  413.2 2.4 copy-start.26
  413.2 36.0 %collective-permute-start.47 = (bf16[12,4,64,256]{3,2,1,0:T(8,128)(2,1)}, bf16[12,4,64,256]{3,2,1,0:T(8,128)(2,1)S(1)}, u32[]{:S(2)}, u32[]{:S(2)}) collective-permute-start(bf16[12,4,64,256]{3,2,1,0:T(8,128)(2,1)} %get-tuple-element.148), channel_id=1, source_target_pairs={{0,8},{8,0},{16,24},{24,16},{1,9},{9,1},{17,25},{25,17},{2,10},{10... | collective-permute-start | bytes 4718600 | tf_op jit(solution)/shard_map/ppermute | solution.py:685
  414.2 35.8 %collective-permute-start.48 = (bf16[12,4,64,256]{3,2,1,0:T(8,128)(2,1)}, bf16[12,4,64,256]{3,2,1,0:T(8,128)(2,1)}, u32[]{:S(2)}, u32[]{:S(2)}) collective-permute-start(bf16[12,4,64,256]{3,2,1,0:T(8,128)(2,1)} %get-tuple-element.149), channel_id=1, source_target_pairs={{0,16},{8,24},{16,0},{24,8},{1,17},{9,25},{17,1},{25,9},{2,18},{10... | collective-permute-start | bytes 4718600 | tf_op jit(solution)/shard_map/ppermute | solution.py:685
  415.7 15.4 %collective-permute-start.45 = (bf16[48,12288]{1,0:T(8,128)(2,1)}, bf16[48,12288]{1,0:T(8,128)(2,1)}, u32[]{:S(2)}, u32[]{:S(2)}) collective-permute-start(bf16[48,12288]{1,0:T(8,128)(2,1)} %get-tuple-element.144), channel_id=1, source_target_pairs={{0,1},{1,0},{2,3},{3,2},{4,5},{5,4},{6,7},{7,6},{8,9},{9,8},{10,11... | collective-permute-start | bytes 3538952 | tf_op jit(solution)/shard_map/ppermute | solution.py:672
  415.7 30.6 %collective-permute-start.46 = (bf16[48,12288]{1,0:T(8,128)(2,1)S(1)}, bf16[48,12288]{1,0:T(8,128)(2,1)}, u32[]{:S(2)}, u32[]{:S(2)}) collective-permute-start(bf16[48,12288]{1,0:T(8,128)(2,1)S(1)} %copy-done.26), channel_id=1, source_target_pairs={{0,2},{1,3},{2,4},{3,5},{4,6},{5,7},{6,0},{7,1},{8,10},{9,11},{10,... | collective-permute-start | bytes 3538952 | tf_op jit(solution)/shard_map/ppermute | solution.py:675
  (22 other events, 21.2 us)
Sparse Core Ops, SparseCore 0:
  380.1 31.2 reduce-scatter.3
